TPU v7x, 32 devices: a whole 2x2x4 slice. The times are simulated.
32 devices in a mesh: dp: 4 (over y, x), fsdp: 8 (over z, core).
Axes of the slice: x: 2, y: 2, z: 4, core: 2. Of those that a mesh axis runs over, the one named last changes fastest.
Arguments:
- latents: bfloat16 [64, 864, 768], P(('dp', 'fsdp')), may hold values from -6 to 6
- captions: bfloat16 [64, 256, 1024], P(('dp', 'fsdp')), may hold values from -6 to 6
- caption_lengths: int32 [64], P(('dp', 'fsdp')), may hold values from 5 to 256, as said below
- timesteps: int32 [64], P(('dp', 'fsdp')), may hold values from 0 to 999
- cotangent: bfloat16 [64, 864, 768], P(('dp', 'fsdp')), may hold values from -6 to 6
- master_weights: float32 [15151104], P(('dp', 'fsdp')), may hold values from -2 to 2
- first_moment: float32 [15151104], P(('dp', 'fsdp')), may hold values from -0.08563604577551912 to 0.08563604577551912
- second_moment: float32 [15151104], P(('dp', 'fsdp')), may hold values from 3.3000896e-05 to 0.00052867435
Outputs:
- output: bfloat16 [64, 864, 768], P(('dp', 'fsdp'))
- input_grad: bfloat16 [64, 864, 768], P(('dp', 'fsdp'))
- grad_norm: float32 [], replicated
- new_master: float32 [15151104], P(('dp', 'fsdp'))
- new_first: float32 [15151104], P(('dp', 'fsdp'))
- new_second: float32 [15151104], P(('dp', 'fsdp'))
Inputs may be any that keep to these rules, and one draw needn't show every extreme that they name: `caption_lengths`: some clip has a caption of exactly 256 tokens and another one of exactly 5.
All inputs are finite; a program needn't handle non-finite values.
Results may differ from a plain program's by a relative error of at most 0.023.
Values may be sent and summed in bfloat16 or wider, within the bound.
A program may use at most 320 MiB of HBM per device.

v0:
```python
import functools
import math

import jax
import jax.numpy as jnp
from jax import lax
from jax.sharding import PartitionSpec as P

D = 768
HEADS = 12
HD = 64
FF = 3072
CTX = 1024
STEP = 5


NORM_EPS = 1e-06
BETA_ONE = 0.9
BETA_TWO = 0.999
ADAM_EPS = 1e-08
RATE = 0.03
DECAY = 0.01
CLIP = 500.0


def layout_sizes():
    return [
        (D, 9 * D),
        (9 * D,),
        (D, 3 * D),
        (D, D),
        (D,),
        (D, D),
        (CTX, 2 * D),
        (D, D),
        (D,),
        (D, FF),
        (FF,),
        (FF, D),
        (D,),
    ]


def unpack(flat_vector):
    pieces = []
    offset = 0
    for layout_shape in layout_sizes():
        number = math.prod(layout_shape)
        pieces.append(flat_vector[offset : offset + number].reshape(layout_shape))
        offset += number
    return pieces


def embed(steps_in):
    half_width = D // 2
    frequency = jnp.exp(-math.log(10000.0) * jnp.arange(half_width, dtype=jnp.float32) / half_width)
    angles = steps_in.astype(jnp.float32)[:, None] * frequency[None, :]
    return jnp.concatenate([jnp.cos(angles), jnp.sin(angles)], axis=1)


def normalize(hidden):
    centred = hidden - jnp.mean(hidden, axis=-1, keepdims=True)
    inverse = lax.rsqrt(jnp.mean(centred * centred, axis=-1, keepdims=True) + NORM_EPS)
    return (centred * inverse, inverse)


def norm_back(normed, inverse, grad_normed):
    return inverse * (
        grad_normed
        - jnp.mean(grad_normed, axis=-1, keepdims=True)
        - normed * jnp.mean(grad_normed * normed, axis=-1, keepdims=True)
    )


def split_pairs(tensor):
    return tensor.reshape(tensor.shape[0], HEADS // 2, 2 * HD).transpose(1, 0, 2)


def join_pairs(tensor):
    return tensor.transpose(1, 0, 2).reshape(tensor.shape[1], HEADS * HD)


def pair_scores(pair_query, pair_key, usable):
    query_view = pair_query.reshape(pair_query.shape[0], 2, HD)
    key_view = pair_key.reshape(pair_key.shape[0], 2, HD)
    scores = jnp.einsum(
        "qhd,khd->hqk", query_view, key_view, preferred_element_type=jnp.float32
    ) * HD ** (-0.5)
    if usable is not None:
        scores = jnp.where(usable[None, None, :], scores, -1e30)
    return scores


def attend_forward(queries, keyset, valueset, usable):

    def one_pair(packed):
        pair_query, pair_key, pair_value = packed
        scores = pair_scores(pair_query, pair_key, usable)
        log_total = jax.nn.logsumexp(scores, axis=-1, keepdims=True)
        probability = jnp.exp(scores - log_total).astype(jnp.bfloat16)
        value_view = pair_value.reshape(pair_value.shape[0], 2, HD)
        mixture = jnp.einsum(
            "hqk,khd->qhd", probability, value_view, preferred_element_type=jnp.float32
        )
        return (mixture.reshape(pair_query.shape[0], 2 * HD), log_total)

    mixture, log_total = lax.map(
        one_pair, (split_pairs(queries), split_pairs(keyset), split_pairs(valueset))
    )
    return (join_pairs(mixture), log_total)


def attend_backward(queries, keyset, valueset, usable, log_total, grad_out):

    def one_pair(packed):
        pair_query, pair_key, pair_value, pair_total, pair_grad = packed
        scores = pair_scores(pair_query, pair_key, usable)
        probability = jnp.exp(scores - pair_total)
        grad_view = pair_grad.reshape(pair_grad.shape[0], 2, HD)
        value_view = pair_value.reshape(pair_value.shape[0], 2, HD)
        grad_values = jnp.einsum(
            "hqk,qhd->khd",
            probability.astype(jnp.bfloat16),
            grad_view,
            preferred_element_type=jnp.float32,
        )
        grad_probs = jnp.einsum(
            "qhd,khd->hqk", grad_view, value_view, preferred_element_type=jnp.float32
        )
        grad_scores = probability * (
            grad_probs - jnp.sum(probability * grad_probs, axis=-1, keepdims=True)
        )
        scaled = (grad_scores * HD ** (-0.5)).astype(jnp.bfloat16)
        key_view = pair_key.reshape(pair_key.shape[0], 2, HD)
        query_view = pair_query.reshape(pair_query.shape[0], 2, HD)
        grad_queries = jnp.einsum(
            "hqk,khd->qhd", scaled, key_view, preferred_element_type=jnp.float32
        )
        grad_keys = jnp.einsum(
            "hqk,qhd->khd", scaled, query_view, preferred_element_type=jnp.float32
        )
        return (
            grad_queries.reshape(pair_query.shape[0], 2 * HD),
            grad_keys.reshape(pair_key.shape[0], 2 * HD),
            grad_values.reshape(pair_key.shape[0], 2 * HD),
        )

    grad_queries, grad_keys, grad_values = lax.map(
        one_pair,
        (
            split_pairs(queries),
            split_pairs(keyset),
            split_pairs(valueset),
            log_total,
            split_pairs(grad_out),
        ),
    )
    return (join_pairs(grad_queries), join_pairs(grad_keys), join_pairs(grad_values))


def matmul(left_side, right_side):
    return jnp.dot(left_side, right_side, preferred_element_type=jnp.float32)


def local(
    latents,
    captions,
    caption_lengths,
    timesteps,
    cotangent,
    master_weights,
    first_moment,
    second_moment,
):
    clip_count, frames, model_width = latents.shape
    tokens = clip_count * frames
    caption_slots = captions.shape[1]
    share = master_weights.shape[0]
    outer_count = lax.axis_size("dp")
    inner_count = lax.axis_size("fsdp")
    gathered = lax.all_gather(
        master_weights.astype(jnp.bfloat16).reshape(1, share), ("dp", "fsdp"), axis=0, tiled=True
    ).reshape(-1)
    weights = unpack(gathered)
    ada_weight, ada_bias = (weights[0], weights[1])
    triple_weight, output_weight, output_bias = (weights[2], weights[3], weights[4])
    cross_query, cross_keyval, cross_output, cross_bias = (
        weights[5],
        weights[6],
        weights[7],
        weights[8],
    )
    up_weight, up_bias, down_weight, down_bias = (weights[9], weights[10], weights[11], weights[12])
    condition = jax.nn.silu(embed(timesteps)).astype(jnp.bfloat16)
    modulation = matmul(condition, ada_weight) + ada_bias.astype(jnp.float32)
    mod_parts = [
        modulation[:, block_index * model_width : (block_index + 1) * model_width][:, None, :]
        for block_index in range(9)
    ]
    inputs = latents.astype(jnp.float32)
    normed_one, inverse_one = normalize(inputs)
    first_in = (
        (normed_one * (1.0 + mod_parts[1]) + mod_parts[0])
        .astype(jnp.bfloat16)
        .reshape(tokens, model_width)
    )
    triple = (
        matmul(first_in, triple_weight)
        .astype(jnp.bfloat16)
        .reshape(clip_count, frames, 3 * model_width)
    )

    def self_forward(packed):
        return attend_forward(
            packed[:, :model_width],
            packed[:, model_width : 2 * model_width],
            packed[:, 2 * model_width :],
            None,
        )

    attended, total_one = lax.map(self_forward, triple)
    attended = attended.astype(jnp.bfloat16).reshape(tokens, model_width)
    branch_one = (matmul(attended, output_weight) + output_bias.astype(jnp.float32)).reshape(
        clip_count, frames, model_width
    )
    after_self = inputs + mod_parts[2] * branch_one
    normed_two, inverse_two = normalize(after_self)
    second_in = (
        (normed_two * (1.0 + mod_parts[4]) + mod_parts[3])
        .astype(jnp.bfloat16)
        .reshape(tokens, model_width)
    )
    cross_queries = (
        matmul(second_in, cross_query).astype(jnp.bfloat16).reshape(clip_count, frames, model_width)
    )
    caption_flat = captions.reshape(clip_count * caption_slots, captions.shape[2])
    cross_pairs = (
        matmul(caption_flat, cross_keyval)
        .astype(jnp.bfloat16)
        .reshape(clip_count, caption_slots, 2 * model_width)
    )
    usable_keys = jnp.arange(caption_slots, dtype=jnp.int32)[None, :] < caption_lengths[:, None]

    def cross_forward(packed):
        queries, keyvals, usable = packed
        return attend_forward(queries, keyvals[:, :model_width], keyvals[:, model_width:], usable)

    crossed, total_two = lax.map(cross_forward, (cross_queries, cross_pairs, usable_keys))
    crossed = crossed.astype(jnp.bfloat16).reshape(tokens, model_width)
    branch_two = (matmul(crossed, cross_output) + cross_bias.astype(jnp.float32)).reshape(
        clip_count, frames, model_width
    )
    after_cross = after_self + mod_parts[5] * branch_two
    normed_three, inverse_three = normalize(after_cross)
    third_in = (
        (normed_three * (1.0 + mod_parts[7]) + mod_parts[6])
        .astype(jnp.bfloat16)
        .reshape(tokens, model_width)
    )
    hidden = matmul(third_in, up_weight) + up_bias.astype(jnp.float32)
    gelu_tanh = functools.partial(jax.nn.gelu, approximate=True)
    activated, gelu_back = jax.vjp(gelu_tanh, hidden)
    activated = activated.astype(jnp.bfloat16)
    branch_three = (matmul(activated, down_weight) + down_bias.astype(jnp.float32)).reshape(
        clip_count, frames, model_width
    )
    output = after_cross + mod_parts[8] * branch_three
    triple_back, output_back, cross_query_back = (weights[2], weights[3], weights[5])
    cross_output_back, up_back, down_back = (weights[7], weights[9], weights[11])
    grad_out = cotangent.astype(jnp.float32)
    grad_gate_three = jnp.sum(grad_out * branch_three, axis=1)
    grad_branch_three = (mod_parts[8] * grad_out).astype(jnp.bfloat16).reshape(tokens, model_width)
    grad_down_bias = jnp.sum(grad_branch_three.astype(jnp.float32), axis=0)
    grad_down = matmul(activated.T, grad_branch_three)
    grad_act = matmul(grad_branch_three, down_back.T)
    grad_hidden = gelu_back(grad_act)[0].astype(jnp.bfloat16)
    grad_up_bias = jnp.sum(grad_hidden.astype(jnp.float32), axis=0)
    grad_up = matmul(third_in.T, grad_hidden)
    grad_third = matmul(grad_hidden, up_back.T).reshape(clip_count, frames, model_width)
    grad_shift_three = jnp.sum(grad_third, axis=1)
    grad_scale_three = jnp.sum(grad_third * normed_three, axis=1)
    grad_cross = grad_out + norm_back(
        normed_three, inverse_three, grad_third * (1.0 + mod_parts[7])
    )
    grad_gate_two = jnp.sum(grad_cross * branch_two, axis=1)
    grad_branch_two = (mod_parts[5] * grad_cross).astype(jnp.bfloat16).reshape(tokens, model_width)
    grad_cross_bias = jnp.sum(grad_branch_two.astype(jnp.float32), axis=0)
    grad_cross_output = matmul(crossed.T, grad_branch_two)
    grad_crossed = (
        matmul(grad_branch_two, cross_output_back.T)
        .astype(jnp.bfloat16)
        .reshape(clip_count, frames, model_width)
    )

    def cross_backward(packed):
        queries, keyvals, usable, log_total, grad_here = packed
        return attend_backward(
            queries,
            keyvals[:, :model_width],
            keyvals[:, model_width:],
            usable,
            log_total,
            grad_here,
        )

    grad_cq, grad_ck, grad_cv = lax.map(
        cross_backward, (cross_queries, cross_pairs, usable_keys, total_two, grad_crossed)
    )
    grad_cq = grad_cq.astype(jnp.bfloat16).reshape(tokens, model_width)
    grad_pairs = (
        jnp.concatenate([grad_ck, grad_cv], axis=-1)
        .astype(jnp.bfloat16)
        .reshape(clip_count * caption_slots, 2 * model_width)
    )
    grad_cross_query = matmul(second_in.T, grad_cq)
    grad_cross_keyval = matmul(caption_flat.T, grad_pairs)
    grad_second = matmul(grad_cq, cross_query_back.T).reshape(clip_count, frames, model_width)
    grad_shift_two = jnp.sum(grad_second, axis=1)
    grad_scale_two = jnp.sum(grad_second * normed_two, axis=1)
    grad_self = grad_cross + norm_back(normed_two, inverse_two, grad_second * (1.0 + mod_parts[4]))
    grad_gate_one = jnp.sum(grad_self * branch_one, axis=1)
    grad_branch_one = (mod_parts[2] * grad_self).astype(jnp.bfloat16).reshape(tokens, model_width)
    grad_output_bias = jnp.sum(grad_branch_one.astype(jnp.float32), axis=0)
    grad_output_weight = matmul(attended.T, grad_branch_one)
    grad_attended = (
        matmul(grad_branch_one, output_back.T)
        .astype(jnp.bfloat16)
        .reshape(clip_count, frames, model_width)
    )

    def self_backward(packed):
        packed_triple, log_total, grad_here = packed
        return attend_backward(
            packed_triple[:, :model_width],
            packed_triple[:, model_width : 2 * model_width],
            packed_triple[:, 2 * model_width :],
            None,
            log_total,
            grad_here,
        )

    grad_sq, grad_sk, grad_sv = lax.map(self_backward, (triple, total_one, grad_attended))
    grad_triple = (
        jnp.concatenate([grad_sq, grad_sk, grad_sv], axis=-1)
        .astype(jnp.bfloat16)
        .reshape(tokens, 3 * model_width)
    )
    grad_triple_weight = matmul(first_in.T, grad_triple)
    grad_first = matmul(grad_triple, triple_back.T).reshape(clip_count, frames, model_width)
    grad_shift_one = jnp.sum(grad_first, axis=1)
    grad_scale_one = jnp.sum(grad_first * normed_one, axis=1)
    grad_inputs = grad_self + norm_back(normed_one, inverse_one, grad_first * (1.0 + mod_parts[1]))
    grad_mod = jnp.concatenate(
        [
            grad_shift_one,
            grad_scale_one,
            grad_gate_one,
            grad_shift_two,
            grad_scale_two,
            grad_gate_two,
            grad_shift_three,
            grad_scale_three,
            grad_gate_three,
        ],
        axis=1,
    ).astype(jnp.bfloat16)
    grad_ada = matmul(condition.T, grad_mod)
    grad_ada_bias = jnp.sum(grad_mod.astype(jnp.float32), axis=0)
    gradient_list = [
        grad_ada,
        grad_ada_bias,
        grad_triple_weight,
        grad_output_weight,
        grad_output_bias,
        grad_cross_query,
        grad_cross_keyval,
        grad_cross_output,
        grad_cross_bias,
        grad_up,
        grad_up_bias,
        grad_down,
        grad_down_bias,
    ]
    flat_grad = jnp.concatenate([piece.reshape(-1) for piece in gradient_list])
    owner_rows = flat_grad.reshape(outer_count * inner_count, share)
    grad_shard = lax.psum_scatter(
        owner_rows, ("dp", "fsdp"), scatter_dimension=0, tiled=True
    ).reshape(share)
    squares = lax.psum(jnp.sum(grad_shard * grad_shard), ("dp", "fsdp"))
    grad_norm = jnp.sqrt(squares)
    clipped = grad_shard * (CLIP / jnp.maximum(grad_norm, CLIP))
    new_first = BETA_ONE * first_moment + (1.0 - BETA_ONE) * clipped
    new_second = BETA_TWO * second_moment + (1.0 - BETA_TWO) * clipped * clipped
    step_first = new_first / (1.0 - BETA_ONE**STEP)
    step_second = new_second / (1.0 - BETA_TWO**STEP)
    new_master = master_weights - RATE * (
        step_first / (jnp.sqrt(step_second) + ADAM_EPS) + DECAY * master_weights
    )
    return (
        output.astype(jnp.bfloat16),
        grad_inputs.astype(jnp.bfloat16),
        grad_norm,
        new_master,
        new_first,
        new_second,
    )


def solution(mesh):
    placed = (
        P(("dp", "fsdp"), None, None),
        P(("dp", "fsdp"), None, None),
        P(("dp", "fsdp")),
        P(("dp", "fsdp")),
        P(("dp", "fsdp"), None, None),
        P(("dp", "fsdp")),
        P(("dp", "fsdp")),
        P(("dp", "fsdp")),
    )
    return jax.shard_map(
        local,
        mesh=mesh,
        in_specs=placed,
        out_specs=(
            P(("dp", "fsdp"), None, None),
            P(("dp", "fsdp"), None, None),
            P(),
            P(("dp", "fsdp")),
            P(("dp", "fsdp")),
            P(("dp", "fsdp")),
        ),
        check_vma=False,
    )
```

profile of v0, /device:TPU:0, one launch (start us, length us, event | category | flops | bytes accessed | tf_op | source)
XLA Modules:
  0.0 3196.9 jit_solution(14990653445764741940)
XLA Ops:
  26.4 322.1 %all-gather.4.cloned.1.call-done = bf16[32,1,473472]{2,1,0:T(2,128)(2,1)} async-done(((bf16[1,1,473472]{2,1,0:T(2,128)(2,1)}), bf16[32,1,473472]{2,1,0:T(2,128)(2,1)}) %all-gather.4.cloned.1.call-update) | async-done | bytes 30302224 | tf_op jit(solution)/shard_map/all_gather | solution.py:181
  348.5 177.9 %reduce.6 = bf16[32,473472]{1,0:T(8,128)(2,1)} reduce(bf16[32,1,473472]{2,1,0:T(2,128)(2,1)} %all-gather.4.cloned.1.call-done, bf16[]{:T(256)} %constant.220), dimensions={1}, to_apply=%all-gather.1.reduce_sub_computation | reduce | bytes 60604416 | tf_op jit(solution)/shard_map/all_gather | solution.py:181
  526.4 69.8 %reshape.497 = bf16[15151104]{0:T(1024)(128)(2,1)} reshape(bf16[32,473472]{1,0:T(8,128)(2,1)} %reduce.6) | data formatting | bytes 60604416
  691.6 20.0 reshape.484
  740.8 87.0 %while.105 = (s32[]{:T(128)}, bf16[2,864,768]{2,1,0:T(8,128)(2,1)}, f32[2,6,2,864,1]{3,2,1,4,0:T(2,128)S(1)}, bf16[2,864,2304]{1,2,0:T(8,128)(2,1)}, s32[]{:T(128)}, /*index=5*/s32[]{:T(128)}, s32[]{:T(128)}) while((s32[]{:T(128)}, bf16[2,864,768]{2,1,0:T(8,128)(2,1)}, f32[2,6,2,864,1]{3,2,1,4,0:T(2,128)S(1)}, ...), condition=%wide.region_7.8_spmd, body=%wide.region_2.7_spmd.sunk | while | flops 394163712 | bytes 41981956 | solution.py:221
  745.2 36.1 %while.112 = (s32[]{:T(128)}, bf16[6,864,128]{1,2,0:T(8,128)(2,1)}, f32[6,2,864,1]{2,1,3,0:T(2,128)S(1)}, bf16[6,864,128]{1,2,0:T(8,128)(2,1)}, bf16[6,864,128]{...) while((s32[]{:T(128)}, bf16[6,864,128]{1,2,0:T(8,128)(2,1)}, ...), condition=%wide.region_6.6_spmd, body=%wide.region_3.5_spmd.sunk | while | flops 394163712 | bytes 20662116 | solution.py:107
  788.6 36.1 %while.112 = (s32[]{:T(128)}, bf16[6,864,128]{1,2,0:T(8,128)(2,1)}, f32[6,2,864,1]{2,1,3,0:T(2,128)S(1)}, bf16[6,864,128]{1,2,0:T(8,128)(2,1)}, bf16[6,864,128]{...) while((s32[]{:T(128)}, bf16[6,864,128]{1,2,0:T(8,128)(2,1)}, ...), condition=%wide.region_6.6_spmd, body=%wide.region_3.5_spmd.sunk | while | flops 394163712 | bytes 20662116 | solution.py:107
  849.8 41.1 %while.107 = (s32[]{:T(128)}, bf16[2,864,768]{2,1,0:T(8,128)(2,1)}, f32[2,6,2,864,1]{3,2,1,4,0:T(2,128)S(1)}, bf16[2,864,768]{1,2,0:T(8,128)(2,1)}, bf16[2,256,1...) while((s32[]{:T(128)}, bf16[2,864,768]{2,1,0:T(8,128)(2,1)}, ...), condition=%wide.region_15.16_spmd, body=%wide.region_10.15_spmd.sunk | while | flops 116356608 | bytes 18316076 | solution.py:248
  852.5 14.7 while.113
  903.5 19.9 multiply_convert_fusion.2
  923.4 16.3 fusion.110
  939.7 26.1 convert_reduce_fusion
  990.0 15.8 multiply_reduce_fusion.3
  1023.1 175.5 %while.109 = (s32[]{:T(128)}, bf16[2,864,768]{1,2,0:T(8,128)(2,1)}, bf16[2,256,768]{1,2,0:T(8,128)(2,1)}, bf16[2,256,768]{1,2,0:T(8,128)(2,1)}, bf16[2,864,768]{...) while((s32[]{:T(128)}, bf16[2,864,768]{1,2,0:T(8,128)(2,1)}, ...), condition=%wide.region_24.25_spmd, body=%wide.region_20.24_spmd.sunk | while | flops 289312640 | bytes 31218056 | solution.py:306
  1030.8 75.2 %while.114 = (s32[]{:T(128)}, bf16[6,864,128]{1,2,0:T(8,128)(2,1)}, bf16[6,256,128]{1,2,0:T(8,128)(2,1)}, bf16[6,256,128]{1,2,0:T(8,128)(2,1)}, bf16[6,256,128]{...) while((s32[]{:T(128)}, bf16[6,864,128]{1,2,0:T(8,128)(2,1)}, ...), condition=%wide.region_23.23_spmd, body=%wide.region_21.22_spmd.sunk | while | flops 289312640 | bytes 15700625 | solution.py:148
  1118.4 75.2 %while.114 = (s32[]{:T(128)}, bf16[6,864,128]{1,2,0:T(8,128)(2,1)}, bf16[6,256,128]{1,2,0:T(8,128)(2,1)}, bf16[6,256,128]{1,2,0:T(8,128)(2,1)}, bf16[6,256,128]{...) while((s32[]{:T(128)}, bf16[6,864,128]{1,2,0:T(8,128)(2,1)}, ...), condition=%wide.region_23.23_spmd, body=%wide.region_21.22_spmd.sunk | while | flops 289312640 | bytes 15700625 | solution.py:148
  1231.9 488.9 %while.111 = (s32[]{:T(128)}, bf16[2,864,768]{2,1,0:T(8,128)(2,1)}, bf16[2,864,768]{2,1,0:T(8,128)(2,1)}, bf16[2,864,768]{2,1,0:T(8,128)(2,1)}, bf16[2,864,2304]...) while((s32[]{:T(128)}, bf16[2,864,768]{2,1,0:T(8,128)(2,1)}, ...), condition=%wide.region_31.32_spmd, body=%wide.region_27.31_spmd.sunk | while | flops 986872832 | bytes 84413528 | solution.py:342
  1239.4 226.6 %while.115 = (s32[]{:T(128)}, bf16[6,864,128]{1,2,0:T(8,128)(2,1)}, bf16[6,864,128]{1,2,0:T(8,128)(2,1)}, bf16[6,864,128]{1,2,0:T(8,128)(2,1)}, bf16[6,864,128]{...) while((s32[]{:T(128)}, bf16[6,864,128]{1,2,0:T(8,128)(2,1)}, ...), condition=%wide.region_30.30_spmd, body=%wide.region_28.29_spmd.sunk | while | flops 986872832 | bytes 47171464 | solution.py:148
  1483.7 226.6 %while.115 = (s32[]{:T(128)}, bf16[6,864,128]{1,2,0:T(8,128)(2,1)}, bf16[6,864,128]{1,2,0:T(8,128)(2,1)}, bf16[6,864,128]{1,2,0:T(8,128)(2,1)}, bf16[6,864,128]{...) while((s32[]{:T(128)}, bf16[6,864,128]{1,2,0:T(8,128)(2,1)}, ...), condition=%wide.region_30.30_spmd, body=%wide.region_28.29_spmd.sunk | while | flops 986872832 | bytes 47171464 | solution.py:148
  1818.1 22.1 reshape.473
  1840.2 14.8 constant_dynamic-update-slice_fusion.22
  1856.4 60.7 %dynamic-update-slice.2 = f32[15151104]{0:T(1024)} dynamic-update-slice(f32[15151104]{0:T(1024)} %constant_dynamic-update-slice_fusion.27, f32[1769472]{0:T(1024)} %reshape.474, s32[]{} %constant.224) | dynamic-update-slice | bytes 14155780
  1917.1 21.3 dynamic-update-slice.3
  1939.7 21.2 dynamic-update-slice.5
  1960.9 54.1 %dynamic-update-slice.6 = f32[15151104]{0:T(1024)} dynamic-update-slice(f32[15151104]{0:T(1024)} %dynamic-update-slice.5, f32[1572864]{0:T(1024)} %reshape.477, s32[]{} %constant.228) | dynamic-update-slice | bytes 12582916
  2015.0 20.2 dynamic-update-slice.7
  2036.5 80.3 %dynamic-update-slice.9 = f32[15151104]{0:T(1024)} dynamic-update-slice(f32[15151104]{0:T(1024)} %constant_dynamic-update-slice_fusion.25, f32[2359296]{0:T(1024)} %bitcast.423, s32[]{} %constant.231) | dynamic-update-slice | bytes 18874372
  2118.1 80.3 %dynamic-update-slice.11 = f32[15151104]{0:T(1024)} dynamic-update-slice(f32[15151104]{0:T(1024)} %constant_dynamic-update-slice_fusion.24, f32[2359296]{0:T(1024)} %reshape.480, s32[]{} %constant.233) | dynamic-update-slice | bytes 18874372
  2199.7 59.5 %reshape.481 = f32[32,473472]{1,0:T(8,128)} reshape(f32[15151104]{0:T(1024)} %constant_dynamic-update-slice_fusion.23) | data formatting | bytes 121208832 | tf_op jit(solution)/shard_map/reshape | solution.py:385
  2259.2 854.2 %all-reduce.3.cloned.1.call-done = f32[32,473472]{1,0:T(8,128)} async-done(((f32[32,473472]{1,0:T(8,128)}), f32[32,473472]{1,0:T(8,128)}) %all-reduce.3.cloned.1.call-update) | async-done | bytes 60604432
  3121.5 39.7 %psum.7 = f32[]{:T(128)} all-reduce(f32[]{:T(128)} %multiply_reduce_fusion.15), channel_id=1, replica_groups=mesh['dp'=4,'fsdp'=8] {'dp','fsdp'}, use_global_device_ids=true, to_apply=%region_50.51 | all-reduce | flops 1 | bytes 8 | tf_op jit(solution)/shard_map/psum | solution.py:389
  3162.0 21.8 multiply_reduce_fusion.14
  (865 shorter events, 1172.9 us)
Async XLA Ops:
  7.2 663.9 %copy-start = (bf16[2,256,1024]{2,1,0:T(8,128)(2,1)S(1)}, bf16[2,256,1024]{2,1,0:T(8,128)(2,1)}, u32[]{:S(2)}) copy-start(bf16[2,256,1024]{2,1,0:T(8,128)(2,1)} %param.25) | copy-start | bytes 3145732
  7.2 13.4 copy-start.69
  7.2 13.5 copy-start.70
  7.2 341.3 %all-gather.4.cloned.1.call-start = ((), (), s32[]{:S(2)}) async-start(), calls=%async_computation | async-start | bytes 62498304 | tf_op jit(solution)/shard_map/all_gather | solution.py:181
  20.5 3092.9 %all-reduce.3.cloned.1.call-start = ((), (), s32[]{:S(2)}) async-start(), calls=%async_computation.1 | async-start | bytes 121208832
  21.4 690.2 %copy-start.49 = (f32[2,384]{1,0:T(2,128)}, f32[2,384]{1,0:T(2,128)S(1)}, u32[]{:S(2)}) copy-start(f32[2,384]{1,0:T(2,128)S(1)} %get-tuple-element.632) | copy-start | bytes 9220
  21.4 690.2 %copy-start.51 = (f32[2,384]{1,0:T(2,128)}, f32[2,384]{1,0:T(2,128)S(1)}, u32[]{:S(2)}) copy-start(f32[2,384]{1,0:T(2,128)S(1)} %get-tuple-element.633) | copy-start | bytes 9220
  23.6 694.3 %copy-start.29 = (f32[2,864]{1,0:T(2,128)}, f32[2,864]{1,0:T(2,128)S(1)}, u32[]{:S(2)}) copy-start(f32[2,864]{1,0:T(2,128)S(1)} %broadcast_multiply_fusion.8) | copy-start | bytes 20740
  26.4 691.6 %copy-start.35 = (f32[2,864]{1,0:T(2,128)}, f32[2,864]{1,0:T(2,128)S(1)}, u32[]{:S(2)}) copy-start(f32[2,864]{1,0:T(2,128)S(1)} %add_rsqrt_fusion.2) | copy-start | bytes 20740
  740.8 87.6 %copy-start.64 = (f32[768]{0:T(1024)S(1)}, f32[768]{0:T(1024)}, u32[]{:S(2)}) copy-start(f32[768]{0:T(1024)} %get-tuple-element.609) | copy-start | bytes 9220
  849.8 41.1 %copy-start.63 = (f32[768]{0:T(1024)S(1)}, f32[768]{0:T(1024)}, u32[]{:S(2)}) copy-start(f32[768]{0:T(1024)} %get-tuple-element.608) | copy-start | bytes 9220
  901.4 38.3 %slice-start.8 = ((s8[4718592]{0:T(1024)(128)(4,1)}), s8[4194304]{0:T(1024)(128)(4,1)S(1)}, s32[]{:S(2)}) async-start(s8[4718592]{0:T(1024)(128)(4,1)} %bitcast.448), calls=%async_computation.10 | async-start | bytes 8388608
  903.5 36.2 %slice-start.9 = ((s8[4718592]{0:T(1024)(128)(4,1)}), s8[524288]{0:T(1024)(128)(4,1)S(1)}, s32[]{:S(2)}) async-start(s8[4718592]{0:T(1024)(128)(4,1)} %bitcast.448), calls=%async_computation.11 | async-start | bytes 1048576
  923.4 16.3 copy-start.14
  939.7 26.1 copy-start.62
  965.8 12.8 copy-start.19
  965.8 12.8 copy-start.71
  990.0 15.9 copy-start.10
  990.0 15.9 copy-start.40
  1198.7 15.5 slice-start
  1198.7 15.5 slice-start.2
  1198.7 15.5 slice-start.4
  1720.8 13.9 copy-start.4
  1720.8 13.8 copy-start.30
  1720.8 13.8 copy-start.36
  1720.8 13.8 copy-start.42
  1917.1 21.3 copy-start.57
  2015.0 20.2 copy-start.56
  2036.5 80.3 %copy-start.60 = (f32[3072]{0:T(1024)S(1)}, f32[3072]{0:T(1024)}, u32[]{:S(2)}) copy-start(f32[3072]{0:T(1024)} %get-tuple-element.639) | copy-start | bytes 36868
  2118.1 80.3 %copy-start.55 = (f32[768]{0:T(1024)S(1)}, f32[768]{0:T(1024)}, u32[]{:S(2)}) copy-start(f32[768]{0:T(1024)} %get-tuple-element.569) | copy-start | bytes 9220
  2259.2 924.6 %copy-start.11 = (f32[473472]{0:T(1024)S(1)}, f32[473472]{0:T(1024)}, u32[]{:S(2)}) copy-start(f32[473472]{0:T(1024)} %param.29) | copy-start | bytes 5681668
  3162.0 21.8 copy-start.20
  (52 other events, 259.9 us)
Sparse Core Ops, SparseCore 0:
  20.6 327.8 all-gather.3
  2259.3 854.0 all-reduce.2
where the time goes:
time: 3230 us; the launch traced here: 3200 us
  waiting for transfers between devices  1180 us (37%)
  local copies, waits for them, and re-layouts  947 us (29%)
  matrix products  735 us (23%)
  other arithmetic  279 us (9%)
  blocking collectives  39.7 us (1%)
    unnamed x3, waiting for transfers between devices  854 us
    unnamed x187, local copies, waits for them, and re-layouts  451 us
    all_gather x1, waiting for transfers between devices, local(): lax.all_gather(master_weights.astype(jnp.bfloat16).reshape(1, share), ('d...  322 us
    dot_general x22, matrix products, matmul(): return jnp.dot(left_side, right_side, preferred_element_type=jnp.float32)  205 us
    all_gather x1, other arithmetic, local(): lax.all_gather(master_weights.astype(jnp.bfloat16).reshape(1, share), ('d...  178 us
    dot_general x24, matrix products, one_pair(): jnp.einsum('hqk,khd->qhd', scaled, key_view, preferred_element_type=jnp.f...  163 us
    dot_general x24, matrix products, one_pair(): jnp.einsum('hqk,qhd->khd', scaled, query_view, preferred_element_type=jnp...  163 us
    dynamic_slice x144, local copies, waits for them, and re-layouts, attend_forward(): lax.map(one_pair, (split_pairs(queries), split_pairs(keyset), split_pairs...  102 us
  transfers between devices with their start and end apart: 2, of which 2 were waited for; matrix products, arithmetic and copies ran while one was open for 0% of the time, Pallas kernels for 0%

commit v1 on v0

v1 whole, which is shorter than its diff:
```python
import functools
import math

import jax
import jax.numpy as jnp
from jax import lax
from jax.experimental import pallas as pl
from jax.experimental.pallas import tpu as pltpu
from jax.sharding import PartitionSpec as P

D = 768
HEADS = 12
HD = 64
FF = 3072
CTX = 1024
STEP = 5


NORM_EPS = 1e-06
BETA_ONE = 0.9
BETA_TWO = 0.999
ADAM_EPS = 1e-08
RATE = 0.03
DECAY = 0.01
CLIP = 500.0


def layout_sizes():
    return [
        (D, 9 * D),
        (9 * D,),
        (D, 3 * D),
        (D, D),
        (D,),
        (D, D),
        (CTX, 2 * D),
        (D, D),
        (D,),
        (D, FF),
        (FF,),
        (FF, D),
        (D,),
    ]


def unpack(flat_vector):
    pieces = []
    offset = 0
    for layout_shape in layout_sizes():
        number = math.prod(layout_shape)
        pieces.append(flat_vector[offset : offset + number].reshape(layout_shape))
        offset += number
    return pieces


def embed(steps_in):
    half_width = D // 2
    frequency = jnp.exp(-math.log(10000.0) * jnp.arange(half_width, dtype=jnp.float32) / half_width)
    angles = steps_in.astype(jnp.float32)[:, None] * frequency[None, :]
    return jnp.concatenate([jnp.cos(angles), jnp.sin(angles)], axis=1)


def normalize(hidden):
    centred = hidden - jnp.mean(hidden, axis=-1, keepdims=True)
    inverse = lax.rsqrt(jnp.mean(centred * centred, axis=-1, keepdims=True) + NORM_EPS)
    return (centred * inverse, inverse)


def norm_back(normed, inverse, grad_normed):
    return inverse * (
        grad_normed
        - jnp.mean(grad_normed, axis=-1, keepdims=True)
        - normed * jnp.mean(grad_normed * normed, axis=-1, keepdims=True)
    )


F32 = jnp.float32
BF = jnp.bfloat16
VMEM_LIMIT = 60 << 20


def nn(left_side, right_side):
    return lax.dot_general(
        left_side, right_side, (((1,), (0,)), ((), ())), preferred_element_type=F32
    )


def nt(left_side, right_side):
    return lax.dot_general(
        left_side, right_side, (((1,), (1,)), ((), ())), preferred_element_type=F32
    )


def tn(left_side, right_side):
    return lax.dot_general(
        left_side, right_side, (((0,), (0,)), ((), ())), preferred_element_type=F32
    )


def call(body, grid, in_specs, out_specs, out_shape, name, scratch=()):
    return pl.pallas_call(
        body,
        grid=grid,
        in_specs=in_specs,
        out_specs=out_specs,
        out_shape=out_shape,
        scratch_shapes=list(scratch),
        compiler_params=pltpu.CompilerParams(vmem_limit_bytes=VMEM_LIMIT),
        name=name,
    )


def struct(shape, dtype):
    return jax.ShapeDtypeStruct(shape, dtype)


def rows_spec(rows, width):
    return pl.BlockSpec((1, rows, width), lambda i, j: (i, j, 0))


def clip_spec(count, width):
    return pl.BlockSpec((1, count, width), lambda i, j: (i, 0, 0))


def whole_spec(shape):
    return pl.BlockSpec(shape, lambda *_: (0,) * len(shape))


def row_block(frames):
    for parts in (2, 3, 4, 6):
        if frames % (16 * parts) == 0:
            return frames // parts
    return frames


def add_to(ref, first, value):
    @pl.when(first)
    def _():
        ref[...] = value

    @pl.when(jnp.logical_not(first))
    def _():
        ref[...] += value


def column_sum(value):
    return jnp.sum(value, axis=0, keepdims=True)


def qkv_kernel(x_ref, mod_ref, w_ref, out_ref):
    normed, _ = normalize(x_ref[0].astype(F32))
    first_in = (normed * (1.0 + mod_ref[0, 1:2]) + mod_ref[0, 0:1]).astype(BF)
    out_ref[0] = nn(first_in, w_ref[...]).astype(BF)


def qkv_forward(latents, mod, weight):
    clips, frames, width = latents.shape
    rows = row_block(frames)
    wide = weight.shape[1]
    return call(
        qkv_kernel,
        (clips, frames // rows),
        [rows_spec(rows, width), clip_spec(9, width), whole_spec(weight.shape)],
        rows_spec(rows, wide),
        struct((clips, frames, wide), BF),
        "qkv_forward",
    )(latents, mod, weight)


def head_lanes():
    lane = lax.broadcasted_iota(jnp.int32, (1, 2 * HD), 1)
    return lane, lane < HD


def usable_bias(length, count):
    row = lax.broadcasted_iota(jnp.int32, (count, 2 * HD), 0)
    return jnp.where(row < length, 0.0, -1e30).astype(BF)


def attend_kernel(*refs, masked):
    if masked:
        len_ref, q_ref, k_ref, v_ref, o_ref, l_ref = refs
    else:
        q_ref, k_ref, v_ref, o_ref, l_ref = refs
    k, v = k_ref[0], v_ref[0]
    scaled = q_ref[0] * jnp.asarray(HD**-0.5, BF)
    lane, low = head_lanes()
    one = jnp.ones((), BF)
    zero = jnp.zeros((), BF)
    values = [jnp.where(low, v, one), jnp.where(low, one, v)]
    if masked:
        bias = usable_bias(len_ref[pl.program_id(0)], k.shape[0])
        tag = jnp.where(lane % HD == 0, one, zero)
        queries = [jnp.where(low, scaled, tag), jnp.where(low, tag, scaled)]
        keys = [jnp.where(low, k, bias), jnp.where(low, bias, k)]
    else:
        queries = [jnp.where(low, scaled, zero), jnp.where(low, zero, scaled)]
        keys = [k, k]
    tops, mixes = [], []
    for head in range(2):
        scores = nt(queries[head], keys[head])
        top = jnp.max(scores, axis=1, keepdims=True)
        mixes.append(nn(jnp.exp(scores - top).astype(BF), values[head]))
        tops.append(top)
    total = jnp.where(low, mixes[1], mixes[0])
    l_ref[0, 0] = jnp.where(low, tops[1], tops[0]) + jnp.log(total)
    o_ref[0] = (jnp.where(low, mixes[0], mixes[1]) / pltpu.roll(total, HD, 1)).astype(BF)


def pair_spec(rows, offset):
    return pl.BlockSpec((1, rows, 2 * HD), lambda i, j: (i, 0, j + offset))


def lse_spec(rows):
    return pl.BlockSpec((1, 1, rows, 2 * HD), lambda i, j: (i, j, 0, 0))


def attend_forward(queries, key_offset, pairs, value_offset, lengths, name):
    clips, frames = queries.shape[:2]
    slots = pairs.shape[1]
    groups = HEADS // 2
    masked = lengths is not None
    specs = [
        pair_spec(frames, 0),
        pair_spec(slots, key_offset),
        pair_spec(slots, value_offset),
    ]
    args = [queries, pairs, pairs]
    if masked:
        specs.insert(0, pl.BlockSpec(memory_space=pltpu.SMEM))
        args.insert(0, lengths)
    return call(
        functools.partial(attend_kernel, masked=masked),
        (clips, groups),
        specs,
        [pair_spec(frames, 0), lse_spec(frames)],
        [struct((clips, frames, D), BF), struct((clips, groups, frames, 2 * HD), F32)],
        name,
    )(*args)


def three_parts(value):
    high = value.astype(BF)
    rest = value - high.astype(F32)
    middle = rest.astype(BF)
    return high, middle, (rest - middle.astype(F32)).astype(BF)


def attend_back_kernel(*refs, masked):
    if masked:
        len_ref, q_ref, k_ref, v_ref, do_ref, o_ref, l_ref, dq_ref, dk_ref, dv_ref = refs
    else:
        q_ref, k_ref, v_ref, do_ref, o_ref, l_ref, dq_ref, dk_ref, dv_ref = refs
    k, v, grad = k_ref[0], v_ref[0], do_ref[0]
    scaled = q_ref[0] * jnp.asarray(HD**-0.5, BF)
    lane, low = head_lanes()
    spot = lane % HD
    one = jnp.ones((), BF)
    zero = jnp.zeros((), BF)
    product = grad.astype(F32) * o_ref[0].astype(F32)
    delta_low = jnp.sum(jnp.where(low, product, 0.0), axis=1, keepdims=True)
    delta_high = jnp.sum(jnp.where(low, 0.0, product), axis=1, keepdims=True)

    def negated(value, last):
        high, middle, rest = three_parts(-value)
        return jnp.where(
            spot == 0,
            high,
            jnp.where(spot == 1, middle, jnp.where(spot == 2, rest, last)),
        )

    tag = jnp.where(spot == 3, one, zero) if masked else zero
    lse_lanes = negated(l_ref[0, 0], tag)
    delta_lanes = negated(jnp.where(low, delta_high, delta_low), zero)
    ones = jnp.broadcast_to(jnp.where(spot < 3, one, zero), k.shape)
    key_lanes = ones
    if masked:
        bias = usable_bias(len_ref[pl.program_id(0)], k.shape[0])
        key_lanes = jnp.where(spot == 3, bias, ones)
    transposed = k.astype(F32).T.astype(BF)
    grad_queries, grad_keys, grad_values = [], [], []
    for head in range(2):

        def merge(own, other):
            return jnp.where(low, own, other) if head == 0 else jnp.where(low, other, own)

        probability = jnp.exp(nt(merge(k, key_lanes), merge(scaled, lse_lanes)))
        centred = nt(merge(v, ones), merge(grad, delta_lanes))
        grad_scores = (probability * centred).astype(BF)
        grad_values.append(nn(probability.astype(BF), grad))
        grad_keys.append(nn(grad_scores, scaled))
        grad_queries.append(nn(transposed[HD * head : HD * (head + 1)], grad_scores))
    dv_ref[0] = jnp.where(low, grad_values[0], grad_values[1]).astype(BF)
    dk_ref[0] = jnp.where(low, grad_keys[0], grad_keys[1]).astype(BF)
    dq_ref[0] = (jnp.concatenate(grad_queries, axis=0).T * HD**-0.5).astype(BF)


def attend_backward(queries, key_offset, pairs, value_offset, lengths, grad, mixed, lse, name):
    clips, frames = queries.shape[:2]
    slots = pairs.shape[1]
    groups = HEADS // 2
    masked = lengths is not None
    specs = [
        pair_spec(frames, 0),
        pair_spec(slots, key_offset),
        pair_spec(slots, value_offset),
        pair_spec(frames, 0),
        pair_spec(frames, 0),
        lse_spec(frames),
    ]
    args = [queries, pairs, pairs, grad, mixed, lse]
    if masked:
        specs.insert(0, pl.BlockSpec(memory_space=pltpu.SMEM))
        args.insert(0, lengths)
    return call(
        functools.partial(attend_back_kernel, masked=masked),
        (clips, groups),
        specs,
        [pair_spec(frames, 0), pair_spec(slots, 0), pair_spec(slots, 0)],
        [
            struct((clips, frames, D), BF),
            struct((clips, slots, D), BF),
            struct((clips, slots, D), BF),
        ],
        name,
    )(*args)


def after_self_kernel(o_ref, x_ref, mod_ref, wo_ref, bo_ref, wq_ref, z_ref, h_ref, q_ref):
    branch = nn(o_ref[0], wo_ref[...]) + bo_ref[...]
    hidden = x_ref[0].astype(F32) + mod_ref[0, 2:3] * branch
    normed, _ = normalize(hidden)
    second_in = (normed * (1.0 + mod_ref[0, 4:5]) + mod_ref[0, 3:4]).astype(BF)
    z_ref[0] = branch.astype(BF)
    h_ref[0] = hidden
    q_ref[0] = nn(second_in, wq_ref[...]).astype(BF)


def after_self(mixed, latents, mod, weight, bias, query_weight):
    clips, frames, width = latents.shape
    rows = row_block(frames)
    spec = rows_spec(rows, width)
    square = whole_spec((width, width))
    return call(
        after_self_kernel,
        (clips, frames // rows),
        [spec, spec, clip_spec(9, width), square, whole_spec((1, width)), square],
        [spec, spec, spec],
        [
            struct(latents.shape, BF),
            struct(latents.shape, F32),
            struct(latents.shape, BF),
        ],
        "after_self",
    )(mixed, latents, mod, weight, bias, query_weight)


def after_cross_kernel(o_ref, h_ref, mod_ref, wo_ref, bo_ref, z_ref, out_ref):
    branch = nn(o_ref[0], wo_ref[...]) + bo_ref[...]
    z_ref[0] = branch.astype(BF)
    out_ref[0] = h_ref[0] + mod_ref[0, 5:6] * branch


def after_cross(mixed, hidden, mod, weight, bias):
    clips, frames, width = hidden.shape
    rows = row_block(frames)
    spec = rows_spec(rows, width)
    return call(
        after_cross_kernel,
        (clips, frames // rows),
        [
            spec,
            spec,
            clip_spec(9, width),
            whole_spec((width, width)),
            whole_spec((1, width)),
        ],
        [spec, spec],
        [struct(hidden.shape, BF), struct(hidden.shape, F32)],
        "after_cross",
    )(mixed, hidden, mod, weight, bias)


GELU_ROOT = math.sqrt(2.0 / math.pi)


def feed_kernel(
    h_ref,
    dy_ref,
    mod_ref,
    up_ref,
    upb_ref,
    down_ref,
    downb_ref,
    out_ref,
    dh_ref,
    dup_ref,
    ddown_ref,
    dupb_ref,
    ddownb_ref,
    sums_ref,
    in_s,
    int_s,
    dz_s,
    dzt_s,
    z_s,
    *,
    clips,
    frames,
    rows,
):
    step = pl.program_id(0)
    last = pl.num_programs(0) - 1
    spans = [
        (clip, start, clip * frames + start)
        for clip in range(clips)
        for start in range(0, frames, rows)
    ]

    @pl.when(step == 0)
    def _():
        bias_sum = jnp.zeros((1, h_ref.shape[2]), F32)
        for clip, start, at in spans:
            normed, _ = normalize(h_ref[clip, start : start + rows])
            third_in = normed * (1.0 + mod_ref[clip, 7:8]) + mod_ref[clip, 6:7]
            dz = (mod_ref[clip, 8:9] * dy_ref[clip, start : start + rows].astype(F32)).astype(BF)
            in_s[at : at + rows] = third_in.astype(BF)
            dz_s[at : at + rows] = dz
            bias_sum += column_sum(dz.astype(F32))
        ddownb_ref[...] = bias_sum
        int_s[...] = in_s[...].T
        dzt_s[...] = dz_s[...].T

    up, down = up_ref[...], down_ref[...]
    grad_up = grad_down = grad_bias = None
    for clip, start, at in spans:
        here = pl.ds(at, rows)
        hidden = nn(in_s[here], up) + upb_ref[...]
        square = hidden * hidden
        tanh = jnp.tanh(GELU_ROOT * hidden * (1.0 + 0.044715 * square))
        half = 0.5 + 0.5 * tanh
        activated = (hidden * half).astype(BF)
        slope = half + hidden * half * (1.0 - tanh) * (
            GELU_ROOT * (1.0 + 3 * 0.044715 * square)
        )
        dz = dz_s[here]
        grad_hidden = (nt(dz, down) * slope).astype(BF)
        branch = nn(activated, down)
        grad_in = nt(grad_hidden, up)

        @pl.when(step == 0)
        def _(branch=branch, grad_in=grad_in, here=here, clip=clip, start=start):
            z_s[here] = branch
            dh_ref[clip, start : start + rows] = grad_in

        @pl.when(step > 0)
        def _(branch=branch, grad_in=grad_in, here=here, clip=clip, start=start):
            z_s[here] += branch
            dh_ref[clip, start : start + rows] += grad_in

        one_up = nn(int_s[:, at : at + rows], grad_hidden)
        one_down = nn(dzt_s[:, at : at + rows], activated)
        one_bias = column_sum(grad_hidden.astype(F32))
        grad_up = one_up if grad_up is None else grad_up + one_up
        grad_down = one_down if grad_down is None else grad_down + one_down
        grad_bias = one_bias if grad_bias is None else grad_bias + one_bias
    dup_ref[...] = grad_up.astype(BF)
    ddown_ref[...] = grad_down.T.astype(BF)
    dupb_ref[...] = grad_bias

    @pl.when(step == last)
    def _():
        for clip in range(clips):
            sums = None
            for start in range(0, frames, rows):
                at = clip * frames + start
                block = slice(start, start + rows)
                hidden = h_ref[clip, block]
                dy = dy_ref[clip, block].astype(F32)
                branch = z_s[at : at + rows] + downb_ref[...]
                out_ref[clip, block] = (hidden + mod_ref[clip, 8:9] * branch).astype(BF)
                normed, inverse = normalize(hidden)
                grad_in = dh_ref[clip, block]
                dh_ref[clip, block] = dy + norm_back(
                    normed, inverse, grad_in * (1.0 + mod_ref[clip, 7:8])
                )
                here = [
                    column_sum(grad_in),
                    column_sum(grad_in * normed),
                    column_sum(dy * branch),
                ]
                sums = here if sums is None else [a + b for a, b in zip(sums, here)]
            for index in range(3):
                sums_ref[clip, index : index + 1] = sums[index]


def feed(hidden, cotangent, mod, up, up_bias, down, down_bias, block=512):
    clips, frames, width = hidden.shape
    inner = up.shape[1]
    rows = row_block(frames)
    tokens = clips * frames

    def once(shape):
        return pl.BlockSpec(
            shape, lambda j: (0,) * len(shape), pipeline_mode=pl.Buffered(1)
        )

    def columns(count):
        return pl.BlockSpec((count, block), lambda j: (0, j))

    lines = pl.BlockSpec((block, width), lambda j: (j, 0))
    cube = once((clips, frames, width))
    return call(
        functools.partial(feed_kernel, clips=clips, frames=frames, rows=rows),
        (inner // block,),
        [
            cube,
            cube,
            once(mod.shape),
            columns(width),
            columns(1),
            lines,
            once((1, width)),
        ],
        [
            cube,
            cube,
            columns(width),
            lines,
            columns(1),
            once((1, width)),
            once((clips, 3, width)),
        ],
        [
            struct(hidden.shape, BF),
            struct(hidden.shape, F32),
            struct(up.shape, BF),
            struct(down.shape, BF),
            struct((1, inner), F32),
            struct((1, width), F32),
            struct((clips, 3, width), F32),
        ],
        "feed",
        [
            pltpu.VMEM((tokens, width), BF),
            pltpu.VMEM((width, tokens), BF),
            pltpu.VMEM((tokens, width), BF),
            pltpu.VMEM((width, tokens), BF),
            pltpu.VMEM((tokens, width), F32),
        ],
    )(hidden, cotangent, mod, up, up_bias, down, down_bias)


def ends():
    i, j = pl.program_id(0), pl.program_id(1)
    first = (i == 0) & (j == 0)
    last = (i == pl.num_programs(0) - 1) & (j == pl.num_programs(1) - 1)
    return j == 0, first, last


def before_cross_kernel(
    dh_ref, z_ref, o_ref, mod_ref, w_ref, do_ref, dw_ref, db_ref, sums_ref, dw_s
):
    new_clip, first, last = ends()
    dh = dh_ref[0]
    dz = (mod_ref[0, 5:6] * dh).astype(BF)
    add_to(sums_ref, new_clip, column_sum(dh * z_ref[0].astype(F32))[None])
    add_to(db_ref, first, column_sum(dz.astype(F32)))
    do_ref[0] = nt(dz, w_ref[...]).astype(BF)
    add_to(dw_s, first, tn(o_ref[0], dz))

    @pl.when(last)
    def _():
        dw_ref[...] = dw_s[...].astype(BF)


def before_cross(dh, branch, mixed, mod, weight):
    clips, frames, width = dh.shape
    rows = row_block(frames)
    spec = rows_spec(rows, width)
    square = whole_spec((width, width))
    return call(
        before_cross_kernel,
        (clips, frames // rows),
        [spec, spec, spec, clip_spec(9, width), square],
        [spec, square, whole_spec((1, width)), clip_spec(1, width)],
        [
            struct(dh.shape, BF),
            struct((width, width), BF),
            struct((1, width), F32),
            struct((clips, 1, width), F32),
        ],
        "before_cross",
        [pltpu.VMEM((width, width), F32)],
    )(dh, branch, mixed, mod, weight)


def before_self_kernel(
    dq_ref,
    h_ref,
    dh_ref,
    z_ref,
    o_ref,
    mod_ref,
    wq_ref,
    wo_ref,
    out_ref,
    do_ref,
    dwq_ref,
    dwo_ref,
    db_ref,
    sums_ref,
    dwq_s,
    dwo_s,
):
    new_clip, first, last = ends()
    normed, inverse = normalize(h_ref[0])
    second_in = (normed * (1.0 + mod_ref[0, 4:5]) + mod_ref[0, 3:4]).astype(BF)
    grad_query = dq_ref[0]
    add_to(dwq_s, first, tn(second_in, grad_query))
    grad_in = nt(grad_query, wq_ref[...])
    dh = dh_ref[0] + norm_back(normed, inverse, grad_in * (1.0 + mod_ref[0, 4:5]))
    out_ref[0] = dh
    dz = (mod_ref[0, 2:3] * dh).astype(BF)
    sums = jnp.concatenate(
        [
            column_sum(grad_in),
            column_sum(grad_in * normed),
            column_sum(dh * z_ref[0].astype(F32)),
        ],
        axis=0,
    )
    add_to(sums_ref, new_clip, sums[None])
    add_to(db_ref, first, column_sum(dz.astype(F32)))
    do_ref[0] = nt(dz, wo_ref[...]).astype(BF)
    add_to(dwo_s, first, tn(o_ref[0], dz))

    @pl.when(last)
    def _():
        dwq_ref[...] = dwq_s[...].astype(BF)
        dwo_ref[...] = dwo_s[...].astype(BF)


def before_self(grad_query, hidden, dh, branch, mixed, mod, query_weight, weight):
    clips, frames, width = dh.shape
    rows = row_block(frames)
    spec = rows_spec(rows, width)
    square = whole_spec((width, width))
    return call(
        before_self_kernel,
        (clips, frames // rows),
        [spec, spec, spec, spec, spec, clip_spec(9, width), square, square],
        [spec, spec, square, square, whole_spec((1, width)), clip_spec(3, width)],
        [
            struct(dh.shape, F32),
            struct(dh.shape, BF),
            struct((width, width), BF),
            struct((width, width), BF),
            struct((1, width), F32),
            struct((clips, 3, width), F32),
        ],
        "before_self",
        [pltpu.VMEM((width, width), F32), pltpu.VMEM((width, width), F32)],
    )(grad_query, hidden, dh, branch, mixed, mod, query_weight, weight)


def input_kernel(
    dq_ref, dk_ref, dv_ref, x_ref, dh_ref, mod_ref, w_ref, out_ref, dw_ref, sums_ref, dw_s
):
    new_clip, first, last = ends()
    width = x_ref.shape[2]
    normed, inverse = normalize(x_ref[0].astype(F32))
    first_in = (normed * (1.0 + mod_ref[0, 1:2]) + mod_ref[0, 0:1]).astype(BF)
    turned = first_in.T
    grad_in = None
    for index, ref in enumerate((dq_ref, dk_ref, dv_ref)):
        columns = slice(index * width, (index + 1) * width)
        grad = ref[0]
        part = nt(grad, w_ref[:, columns])
        grad_in = part if grad_in is None else grad_in + part
        add_to(dw_s.at[:, columns], first, nn(turned, grad))
    out_ref[0] = (
        dh_ref[0] + norm_back(normed, inverse, grad_in * (1.0 + mod_ref[0, 1:2]))
    ).astype(BF)
    sums = jnp.concatenate([column_sum(grad_in), column_sum(grad_in * normed)], axis=0)
    add_to(sums_ref, new_clip, sums[None])

    @pl.when(last)
    def _():
        dw_ref[...] = dw_s[...].astype(BF)


def input_back(grads, latents, dh, mod, weight):
    clips, frames, width = dh.shape
    rows = row_block(frames)
    spec = rows_spec(rows, width)
    return call(
        input_kernel,
        (clips, frames // rows),
        [spec] * 5 + [clip_spec(9, width), whole_spec(weight.shape)],
        [spec, whole_spec(weight.shape), clip_spec(2, width)],
        [
            struct(dh.shape, BF),
            struct(weight.shape, BF),
            struct((clips, 2, width), F32),
        ],
        "input_back",
        [pltpu.VMEM(weight.shape, F32)],
    )(*grads, latents, dh, mod, weight)


def block_pass(latents, captions, lengths, cotangent, mod, weights):
    (
        triple_weight,
        output_weight,
        output_bias,
        cross_query,
        cross_keyval,
        cross_output,
        cross_bias,
        up_weight,
        up_bias,
        down_weight,
        down_bias,
    ) = weights
    clips, frames, width = latents.shape
    slots = captions.shape[1]
    groups = HEADS // 2
    caption_flat = captions.reshape(clips * slots, captions.shape[2])
    triple = qkv_forward(latents, mod, triple_weight)
    mixed_one, lse_one = attend_forward(triple, groups, triple, 2 * groups, None, "self_forward")
    branch_one, hidden_one, cross_queries = after_self(
        mixed_one, latents, mod, output_weight, output_bias, cross_query
    )
    pairs = (
        jnp.dot(caption_flat, cross_keyval, preferred_element_type=F32)
        .astype(BF)
        .reshape(clips, slots, 2 * width)
    )
    mixed_two, lse_two = attend_forward(cross_queries, 0, pairs, groups, lengths, "cross_forward")
    branch_two, hidden_two = after_cross(mixed_two, hidden_one, mod, cross_output, cross_bias)
    output, dh_two, grad_up, grad_down, grad_up_bias, grad_down_bias, sums_three = feed(
        hidden_two, cotangent, mod, up_weight, up_bias, down_weight, down_bias
    )
    grad_mixed_two, grad_cross_output, grad_cross_bias, gate_two = before_cross(
        dh_two, branch_two, mixed_two, mod, cross_output
    )
    grad_cq, grad_ck, grad_cv = attend_backward(
        cross_queries, 0, pairs, groups, lengths, grad_mixed_two, mixed_two, lse_two, "cross_back"
    )
    grad_pairs = jnp.concatenate([grad_ck, grad_cv], axis=-1).reshape(clips * slots, 2 * width)
    grad_keyval = jnp.dot(caption_flat.T, grad_pairs, preferred_element_type=F32).astype(BF)
    dh_one, grad_mixed_one, grad_cross_query, grad_output, grad_output_bias, sums_two = before_self(
        grad_cq, hidden_one, dh_two, branch_one, mixed_one, mod, cross_query, output_weight
    )
    grads_one = attend_backward(
        triple,
        groups,
        triple,
        2 * groups,
        None,
        grad_mixed_one,
        mixed_one,
        lse_one,
        "self_back",
    )
    input_grad, grad_triple, sums_one = input_back(grads_one, latents, dh_one, mod, triple_weight)
    grad_mod = jnp.concatenate(
        [sums_one, sums_two[:, 2:], sums_two[:, :2], gate_two, sums_three], axis=1
    ).astype(BF)
    return (
        output,
        input_grad,
        grad_mod,
        [
            grad_triple,
            grad_output,
            grad_output_bias,
            grad_cross_query,
            grad_keyval,
            grad_cross_output,
            grad_cross_bias,
            grad_up,
            grad_up_bias,
            grad_down,
            grad_down_bias,
        ],
    )


def local(
    latents,
    captions,
    caption_lengths,
    timesteps,
    cotangent,
    master_weights,
    first_moment,
    second_moment,
):
    clip_count, frames, model_width = latents.shape
    share = master_weights.shape[0]
    outer_count = lax.axis_size("dp")
    inner_count = lax.axis_size("fsdp")
    gathered = lax.all_gather(
        master_weights.astype(BF).reshape(1, share), ("dp", "fsdp"), axis=0, tiled=True
    ).reshape(-1)
    weights = unpack(gathered)
    condition = jax.nn.silu(embed(timesteps)).astype(BF)
    modulation = jnp.dot(condition, weights[0], preferred_element_type=F32) + weights[1].astype(F32)
    mod = modulation.reshape(clip_count, 9, model_width)
    block_weights = [w.astype(F32).reshape(1, -1) if w.ndim == 1 else w for w in weights[2:]]
    output, input_grad, grad_mod, gradients = block_pass(
        latents, captions, caption_lengths, cotangent, mod, block_weights
    )
    grad_mod = grad_mod.reshape(clip_count, 9 * model_width)
    grad_ada = jnp.dot(condition.T, grad_mod, preferred_element_type=F32)
    grad_ada_bias = jnp.sum(grad_mod.astype(F32), axis=0)
    gradient_list = [grad_ada, grad_ada_bias] + gradients
    flat_grad = jnp.concatenate([piece.astype(F32).reshape(-1) for piece in gradient_list])
    owner_rows = flat_grad.reshape(outer_count * inner_count, share)
    grad_shard = lax.psum_scatter(
        owner_rows, ("dp", "fsdp"), scatter_dimension=0, tiled=True
    ).reshape(share)
    squares = lax.psum(jnp.sum(grad_shard * grad_shard), ("dp", "fsdp"))
    grad_norm = jnp.sqrt(squares)
    clipped = grad_shard * (CLIP / jnp.maximum(grad_norm, CLIP))
    new_first = BETA_ONE * first_moment + (1.0 - BETA_ONE) * clipped
    new_second = BETA_TWO * second_moment + (1.0 - BETA_TWO) * clipped * clipped
    step_first = new_first / (1.0 - BETA_ONE**STEP)
    step_second = new_second / (1.0 - BETA_TWO**STEP)
    new_master = master_weights - RATE * (
        step_first / (jnp.sqrt(step_second) + ADAM_EPS) + DECAY * master_weights
    )
    return (output, input_grad, grad_norm, new_master, new_first, new_second)


def solution(mesh):
    placed = (
        P(("dp", "fsdp"), None, None),
        P(("dp", "fsdp"), None, None),
        P(("dp", "fsdp")),
        P(("dp", "fsdp")),
        P(("dp", "fsdp"), None, None),
        P(("dp", "fsdp")),
        P(("dp", "fsdp")),
        P(("dp", "fsdp")),
    )
    return jax.shard_map(
        local,
        mesh=mesh,
        in_specs=placed,
        out_specs=(
            P(("dp", "fsdp"), None, None),
            P(("dp", "fsdp"), None, None),
            P(),
            P(("dp", "fsdp")),
            P(("dp", "fsdp")),
            P(("dp", "fsdp")),
        ),
        check_vma=False,
    )
```

time: 3230 us -> 2480 us (0.77)
  matrix products: 735 us -> 24.8 us
  Pallas kernels: 0 us -> 307 us
  local copies, waits for them, and re-layouts: 947 us -> 662 us
  other arithmetic: 279 us -> 221 us
    dot_general x190 -> x4, matrix products: 735 us -> 24.8 us  [the longest x1 8.7 us: local(): grad_ada = jnp.dot(condition.T, grad_mod, preferred_element_type=F32)]
    pallas_call x0 -> x11, Pallas kernels: none -> 307 us  [the longest x1 84.8 us: feed(): call(functools.partial(feed_kernel, clips=clips, frames=frames, rows=rows...]
    dynamic_slice x160 -> x0, local copies, waits for them, and re-layouts: 122 us -> none  [the longest x144 102 us: attend_forward(): lax.map(one_pair, (split_pairs(queries), split_pairs(keyset), split_pairs...]
    dynamic_update_slice x98 -> x0, local copies, waits for them, and re-layouts: 93.4 us -> none  [the longest x60 43.7 us: attend_forward(): lax.map(one_pair, (split_pairs(queries), split_pairs(keyset), split_pairs...]
    reduce_sum x34 -> x1, other arithmetic: 54.3 us -> 0.01 us  [local(): grad_ada_bias = jnp.sum(grad_mod.astype(F32), axis=0)]
    reshape x7 -> x12, local copies, waits for them, and re-layouts: 56.9 us -> 64.7 us  [the longest x8 62.2 us: local(): piece.astype(F32).reshape(-1)]
    slice x14 -> x12, local copies, waits for them, and re-layouts: 88.1 us -> 80.4 us  [unpack(): pieces.append(flat_vector[offset:offset + number].reshape(layout_shape))]
    unnamed x187 -> x40, local copies, waits for them, and re-layouts: 451 us -> 445 us
where the time goes in v1:
time: 2480 us; the launch traced here: 2450 us
  waiting for transfers between devices  1180 us (48%)
  local copies, waits for them, and re-layouts  662 us (27%)
  Pallas kernels  307 us (12%)
  other arithmetic  221 us (9%)
  blocking collectives  39.5 us (2%)
  matrix products  24.8 us (1%)
    unnamed x3, waiting for transfers between devices  854 us
    unnamed x40, local copies, waits for them, and re-layouts  445 us
    all_gather x1, waiting for transfers between devices, local(): lax.all_gather(master_weights.astype(BF).reshape(1, share), ('dp', 'fsdp'...  328 us
    all_gather x1, other arithmetic, local(): lax.all_gather(master_weights.astype(BF).reshape(1, share), ('dp', 'fsdp'...  178 us
    pallas_call x1, Pallas kernels, feed(): call(functools.partial(feed_kernel, clips=clips, frames=frames, rows=rows...  84.8 us
    slice x12, local copies, waits for them, and re-layouts, unpack(): pieces.append(flat_vector[offset:offset + number].reshape(layout_shape))  80.4 us
    pallas_call x2, Pallas kernels, attend_backward(): call(functools.partial(attend_back_kernel, masked=masked), (clips, groups...  75.8 us
    reshape x8, local copies, waits for them, and re-layouts, local(): piece.astype(F32).reshape(-1)  62.2 us
  transfers between devices with their start and end apart: 2, of which 2 were waited for; matrix products, arithmetic and copies ran while one was open for 0% of the time, Pallas kernels for 0%

profile of v1, /device:TPU:0, one launch (start us, length us, event | category | flops | bytes accessed | tf_op | source)
XLA Modules:
  0.0 2452.4 jit_solution(17449958004639128531)
XLA Ops:
  8.9 11.6 reshape.218
  20.7 327.8 %all-gather.4.cloned.1.call-done = bf16[32,1,473472]{2,1,0:T(2,128)(2,1)} async-done(((bf16[1,1,473472]{2,1,0:T(2,128)(2,1)}), bf16[32,1,473472]{2,1,0:T(2,128)(2,1)}) %all-gather.4.cloned.1.call-update) | async-done | bytes 30302224 | tf_op jit(solution)/shard_map/all_gather | solution.py:805
  348.5 177.9 %reduce.2 = bf16[32,473472]{1,0:T(8,128)(2,1)} reduce(bf16[32,1,473472]{2,1,0:T(2,128)(2,1)} %all-gather.4.cloned.1.call-done, bf16[]{:T(256)} %constant.40), dimensions={1}, to_apply=%all-gather.1.reduce_sub_computation | reduce | bytes 60604416 | tf_op jit(solution)/shard_map/all_gather | solution.py:805
  526.4 69.9 %reshape.219 = bf16[15151104]{0:T(1024)(128)(2,1)} reshape(bf16[32,473472]{1,0:T(8,128)(2,1)} %reduce.2) | data formatting | bytes 60604416
  596.3 9.3 slice.87
  618.1 9.1 fusion.10
  628.5 19.6 reshape.206
  662.0 11.7 qkv_forward.1.refs_0_.refs_1_.refs_2_
  673.7 33.8 %self_forward.1 = (bf16[2,864,768]{2,1,0:T(8,128)(2,1)}, f32[2,6,864,128]{3,2,1,0:T(8,128)}) custom-call(bf16[2,864,2304]{2,1,0:T(8,128)(2,1)} %qkv_forward.1.refs_0_.refs_1_.refs_2_, bf16[2,864,2304]{2,1,0:T(8,128)(2,1)} %qkv_forward.1.refs_0_.refs_1_.refs_2_, bf16[2,864,2304]{2,1,0:T(8,128)(2,1)} %qkv_forward.1.refs_0_.refs_1_.refs_2_), custom_call_target="tpu_custom_call" | custom-call | tf_op jit(solution)/shard_map/self_forward/pallas_call | solution.py:232
  731.3 9.2 reshape.217.down_ref
  745.9 10.8 after_self.1
  756.8 14.2 cross_forward.1
  779.7 84.8 %feed.1 = (bf16[2,864,768]{2,1,0:T(8,128)(2,1)}, f32[2,864,768]{2,1,0:T(8,128)}, bf16[768,3072]{1,0:T(8,128)(2,1)}, bf16[3072,768]{1,0:T(8,128)(2,1)}, f32[1,307...) custom-call(f32[2,864,768]{2,1,0:T(8,128)} %get-tuple-element.45.h_ref, bf16[2,864,768]{2,1,0:T(8,128)(2,1)} %dy_ref.1, ...), custom_call_target="tpu_custom_call" | custom-call | tf_op jit(solution)/shard_map/feed/pallas_call | solution.py:513
  864.5 12.0 before_cross.1
  876.5 23.3 cross_back.1
  899.8 24.5 %before_self.1 = (f32[2,864,768]{2,1,0:T(8,128)}, bf16[2,864,768]{2,1,0:T(8,128)(2,1)}, bf16[768,768]{1,0:T(8,128)(2,1)}, bf16[768,768]{1,0:T(8,128)(2,1)}, f32[1,768]{1,0:T(1,128)}, /*index=5*/f32[2,3,768]{2,1,0:T(4,128)}) custom-call(bf16[2,864,768]{2,1,0:T(8,128)(2,1)} %get-tuple-element.51.dq_ref, f32[2,864,768]{2,1,0:T(8,128)} %get-tuple-element.44.h_ref, ...), custom_call_target="tpu_custom_call" | custom-call | tf_op jit(solution)/shard_map/before_self/pallas_call | solution.py:649
  925.8 52.5 %self_back.1 = (bf16[2,864,768]{2,1,0:T(8,128)(2,1)}, bf16[2,864,768]{2,1,0:T(8,128)(2,1)}, bf16[2,864,768]{2,1,0:T(8,128)(2,1)}) custom-call(bf16[2,864,2304]{2,1,0:T(8,128)(2,1)} %qkv_forward.1.refs_0_.refs_1_.refs_2_, bf16[2,864,2304]{2,1,0:T(8,128)(2,1)} %qkv_forward.1.refs_0_.refs_1_.refs_2_, bf16[2,864,2304]{2,1,0:T(8,128)(2,1)} %qkv_forward.1.refs_0_.refs_1_.refs_2_, ...), custom_call_target="tpu_custom_call" | custom-call | tf_op jit(solution)/shard_map/self_back/pallas_call | solution.py:315
  978.3 30.4 %input_back.1 = (bf16[2,864,768]{2,1,0:T(8,128)(2,1)}, bf16[768,2304]{1,0:T(8,128)(2,1)}, f32[2,2,768]{2,1,0:T(2,128)}) custom-call(bf16[2,864,768]{2,1,0:T(8,128)(2,1)} %get-tuple-element.55.dq_ref, bf16[2,864,768]{2,1,0:T(8,128)(2,1)} %get-tuple-element.56.dk_ref, bf16[2,864,768]{2,1,0:T(8,128)(2,1)} %get-tuple-element.57.dv_ref, ...), custom_call_target="tpu_custom_call" | custom-call | tf_op jit(solution)/shard_map/input_back/pallas_call | solution.py:697
  1018.4 22.1 reshape.161
  1040.4 14.8 constant_dynamic-update-slice_fusion.5
  1100.6 10.0 reshape.202
  1112.0 60.7 %dynamic-update-slice.2 = f32[15151104]{0:T(1024)} dynamic-update-slice(f32[15151104]{0:T(1024)} %constant_dynamic-update-slice_fusion.4, f32[1769472]{0:T(1024)} %reshape.190, s32[]{} %constant.47) | dynamic-update-slice | bytes 14155780
  1172.7 21.3 dynamic-update-slice.3
  1195.3 20.3 dynamic-update-slice.5
  1215.5 54.4 %dynamic-update-slice.6 = f32[15151104]{0:T(1024)} dynamic-update-slice(f32[15151104]{0:T(1024)} %dynamic-update-slice.5, f32[1572864]{0:T(1024)} %reshape.196, s32[]{} %constant.51) | dynamic-update-slice | bytes 12582916
  1269.9 20.3 dynamic-update-slice.7
  1291.4 80.6 %dynamic-update-slice.9 = f32[15151104]{0:T(1024)} dynamic-update-slice(f32[15151104]{0:T(1024)} %constant_dynamic-update-slice_fusion.2, f32[2359296]{0:T(1024)} %bitcast.23, s32[]{} %constant.54) | dynamic-update-slice | bytes 18874372
  1373.4 80.2 %dynamic-update-slice.11 = f32[15151104]{0:T(1024)} dynamic-update-slice(f32[15151104]{0:T(1024)} %constant_dynamic-update-slice_fusion.1, f32[2359296]{0:T(1024)} %reshape.202, s32[]{} %constant.56) | dynamic-update-slice | bytes 18874372
  1454.9 59.7 %reshape.180 = f32[32,473472]{1,0:T(8,128)} reshape(f32[15151104]{0:T(1024)} %constant_dynamic-update-slice_fusion) | data formatting | bytes 121208832 | tf_op jit(solution)/shard_map/reshape | solution.py:821
  1514.6 854.2 %all-reduce.3.cloned.1.call-done = f32[32,473472]{1,0:T(8,128)} async-done(((f32[32,473472]{1,0:T(8,128)}), f32[32,473472]{1,0:T(8,128)}) %all-reduce.3.cloned.1.call-update) | async-done | bytes 60604432
  2376.9 39.5 %psum.7 = f32[]{:T(128)} all-reduce(f32[]{:T(128)} %multiply_reduce_fusion.1), channel_id=1, replica_groups=mesh['dp'=4,'fsdp'=8] {'dp','fsdp'}, use_global_device_ids=true, to_apply=%region_3.4 | all-reduce | flops 1 | bytes 8 | tf_op jit(solution)/shard_map/psum | solution.py:825
  2417.2 21.8 multiply_reduce_fusion
  (77 shorter events, 143.6 us)
Async XLA Ops:
  7.2 734.0 %copy-start = (bf16[2,256,1024]{2,1,0:T(8,128)(2,1)S(1)}, bf16[2,256,1024]{2,1,0:T(8,128)(2,1)}, u32[]{:S(2)}) copy-start(bf16[2,256,1024]{2,1,0:T(8,128)(2,1)} %param.9) | copy-start | bytes 3145732
  7.2 13.4 copy-start.11
  7.2 341.3 %all-gather.4.cloned.1.call-start = ((), (), s32[]{:S(2)}) async-start(), calls=%async_computation | async-start | bytes 62498304 | tf_op jit(solution)/shard_map/all_gather | solution.py:805
  20.5 2348.3 %all-reduce.3.cloned.1.call-start = ((), (), s32[]{:S(2)}) async-start(), calls=%async_computation.1 | async-start | bytes 121208832
  978.3 30.4 %copy-start.5 = (f32[2,3,768]{2,1,0:T(4,128)S(1)}, f32[2,3,768]{2,1,0:T(4,128)}, u32[]{:S(2)}) copy-start(f32[2,3,768]{2,1,0:T(4,128)} %get-tuple-element.63) | copy-start | bytes 55300
  978.3 30.4 %copy-start.7 = (f32[2,1,768]{2,1,0:T(1,128)S(1)}, f32[2,1,768]{2,1,0:T(1,128)}, u32[]{:S(2)}) copy-start(f32[2,1,768]{2,1,0:T(1,128)} %get-tuple-element.62) | copy-start | bytes 18436
  1055.3 8.4 copy-start.4
  1087.9 3.4 copy-start.10
  1087.9 3.4 copy-start.9
  1100.6 10.0 copy-start.8
  1215.5 54.4 %copy-start.1 = (f32[589824]{0:T(1024)S(1)}, f32[589824]{0:T(1024)}, u32[]{:S(2)}) copy-start(f32[589824]{0:T(1024)} %reshape.198) | copy-start | bytes 7077892
  1291.4 80.6 %copy-start.6 = (f32[1,3072]{1,0:T(1,128)S(1)}, f32[1,3072]{1,0:T(1,128)}, u32[]{:S(2)}) copy-start(f32[1,3072]{1,0:T(1,128)} %get-tuple-element.73) | copy-start | bytes 36868
  1514.6 924.4 %copy-start.2 = (f32[473472]{0:T(1024)S(1)}, f32[473472]{0:T(1024)}, u32[]{:S(2)}) copy-start(f32[473472]{0:T(1024)} %param.13) | copy-start | bytes 5681668
  2417.2 21.8 copy-start.3
Sparse Core Ops, SparseCore 0:
  20.6 327.8 all-gather.3
  1514.7 854.0 all-reduce.2

commit v2 on v1

--- a/solution.py
+++ b/solution.py
@@ -788,6 +788,1012 @@
     )
 
 
+LANE = 128
+TILE = 16
+
+
+def linear_layout():
+    spots = []
+    offset = 0
+    for shape in layout_sizes():
+        number = math.prod(shape) // LANE
+        spots.append((offset, number, shape))
+        offset += number
+    return spots
+
+
+class Plan:
+    def __init__(self, devices, share):
+        self.devices, self.share = devices, share
+        spots = linear_layout()
+        self.first_row = spots[2][0]
+        self.rows = spots[-1][0] + spots[-1][1]
+        self.lead = self.first_row // share
+        self.padded = -(-share // TILE) * TILE
+        self.lent = -(-(self.padded // 3) // TILE) * TILE
+        self.kept = self.padded - self.lent
+        self.chunk = 2 * self.lent
+        self.base = (self.first_row - self.lead * share) // TILE * TILE
+
+    def find(self, row):
+        owner, at = divmod(row, self.share)
+        if at < self.kept:
+            base = self.base if owner == self.lead else 0
+            return owner, at - base, self.kept - at
+        if owner == self.lead:
+            return self.lead - 1, at - self.kept, self.share - at
+        lender = owner - self.lead - 1
+        return lender // 2, (lender % 2) * self.lent + at - self.kept, self.share - at
+
+    def segments(self, start, count):
+        found = []
+        row = start
+        while row < start + count:
+            chunk, place, left = self.find(row)
+            take = min(left, start + count - row)
+            found.append((chunk, place, row, take))
+            row += take
+        return found
+
+
+def unpack_kernel(*refs, plan, indices, step):
+    n = len(indices)
+    spots = linear_layout()
+    g_ref, outs, rest = refs[0], refs[1 : 1 + n], refs[1 + n :]
+    lin, in_sem, out_sem = rest[0], rest[1], rest[2]
+    stages, results = rest[3 : 3 + n], rest[3 + n :]
+    loads = []
+    for which, index in enumerate(indices):
+        offset, number, _ = spots[index]
+        place = 0
+        mine = []
+        for slot, (chunk, row, at, take) in enumerate(plan.segments(offset, number)):
+            low = row // TILE * TILE
+            high = -(-(row + take) // TILE) * TILE
+            copy = pltpu.make_async_copy(
+                g_ref.at[chunk, pl.ds(low, high - low)],
+                stages[which].at[pl.ds(place, high - low)],
+                in_sem.at[which, slot],
+            )
+            copy.start()
+            mine.append((copy, place, row - low, high - low, at - offset, take))
+            place += high - low
+        loads.append(mine)
+    stores = []
+    for which, index in enumerate(indices):
+        offset, number, shape = spots[index]
+        for copy, place, skip, size, at, take in loads[which]:
+            copy.wait()
+            first = stages[which][place : place + TILE].astype(F32)
+            lin[at : at + TILE - skip] = first[skip:]
+            blocks, tail = divmod(size - TILE, step)
+
+            def body(i, _, place=place, at=at, skip=skip, which=which):
+                source = pl.multiple_of(place + TILE + i * step, TILE)
+                lin[pl.ds(at + TILE - skip + i * step, step)] = stages[which][
+                    pl.ds(source, step)
+                ].astype(F32)
+                return 0
+
+            lax.fori_loop(0, blocks, body, 0)
+            if tail:
+                source = place + TILE + blocks * step
+                target = at + TILE - skip + blocks * step
+                lin[target : target + tail] = stages[which][source : source + tail].astype(F32)
+        if len(shape) == 1:
+            for c in range(number):
+                results[which][0:1, c * LANE : (c + 1) * LANE] = lin[c : c + 1]
+        else:
+            high, wide = shape
+            count = wide // LANE
+            rows = 64
+
+            def turn(i, _, which=which, count=count):
+                top = pl.multiple_of(i * rows, rows)
+                for c in range(count):
+                    results[which][pl.ds(top, rows), c * LANE : (c + 1) * LANE] = lin[
+                        pl.ds(top * count + c, rows, stride=count)
+                    ].astype(BF)
+                return 0
+
+            lax.fori_loop(0, high // rows, turn, 0)
+        copy = pltpu.make_async_copy(results[which], outs[which], out_sem.at[which])
+        copy.start()
+        stores.append(copy)
+    for copy in stores:
+        copy.wait()
+
+
+def unpack_weights(gathered, plan, indices, step=128):
+    spots = linear_layout()
+    stage_shapes, result_shapes, most, tallest = [], [], 0, 0
+    for index in indices:
+        offset, number, shape = spots[index]
+        found = plan.segments(offset, number)
+        size = sum(-(-(r + t) // TILE) * TILE - r // TILE * TILE for _, r, _, t in found)
+        stage_shapes.append(pltpu.VMEM((size, LANE), BF))
+        most = max(most, len(found))
+        tallest = max(tallest, number)
+        result_shapes.append((shape, BF) if len(shape) == 2 else ((1, shape[0]), F32))
+    anywhere = pl.BlockSpec(memory_space=pl.ANY)
+    return pl.pallas_call(
+        functools.partial(unpack_kernel, plan=plan, indices=indices, step=step),
+        in_specs=[anywhere],
+        out_specs=[anywhere] * len(indices),
+        out_shape=[jax.ShapeDtypeStruct(s, t) for s, t in result_shapes],
+        scratch_shapes=[
+            pltpu.VMEM((tallest + 2 * TILE, LANE), F32),
+            pltpu.SemaphoreType.DMA((len(indices), most)),
+            pltpu.SemaphoreType.DMA((len(indices),)),
+        ]
+        + stage_shapes
+        + [pltpu.VMEM(s, t) for s, t in result_shapes],
+        compiler_params=pltpu.CompilerParams(vmem_limit_bytes=VMEM_LIMIT),
+        name="unpack",
+    )(gathered)
+
+
+def pack_kernel(*refs, plan, indices, step):
+    n = len(indices)
+    spots = linear_layout()
+    ins, out_ref, rest = refs[:n], refs[n], refs[n + 1 :]
+    lin, stage, in_sem, out_sem = rest[:4]
+    held = rest[4:]
+    copies = []
+    for which in range(n):
+        copy = pltpu.make_async_copy(ins[which], held[which], in_sem.at[which])
+        copy.start()
+        copies.append(copy)
+    stores = []
+    begin = spots[indices[0]][0]
+    total = spots[indices[-1]][0] + spots[indices[-1]][1] - begin
+    pieces = plan.segments(begin, total)
+    place = 0
+    done = -TILE
+    lin[0:TILE] = jnp.zeros((TILE, LANE), F32)
+    slot = 0
+    for which, index in enumerate(indices):
+        offset, number, shape = spots[index]
+        copies[which].wait()
+        if len(shape) == 1:
+            for c in range(number):
+                lin[TILE + c : TILE + c + 1] = held[which][0:1, c * LANE : (c + 1) * LANE]
+        else:
+            high, wide = shape
+            count = wide // LANE
+            rows = 64
+
+            def turn(i, _, which=which, count=count):
+                top = pl.multiple_of(i * rows, rows)
+                for c in range(count):
+                    lin[pl.ds(TILE + top * count + c, rows, stride=count)] = held[which][
+                        pl.ds(top, rows), c * LANE : (c + 1) * LANE
+                    ].astype(F32)
+                return 0
+
+            lax.fori_loop(0, high // rows, turn, 0)
+        low, high_row = offset - begin, offset - begin + number
+        last = which == n - 1
+        while slot < len(pieces):
+            chunk, row, at, take = pieces[slot]
+            at -= begin
+            head = row - row // TILE * TILE
+            start, stop = at - head, at + take
+            ceil = start + -(-(stop - start) // TILE) * TILE
+            first = max(start, done)
+            whole = stop <= high_row
+            end = ceil if whole else start + (high_row - start) // TILE * TILE
+            if end > first:
+                base = row - head + first - start
+                blocks, tail = divmod(end - first, step)
+                shift = TILE + first - low
+
+                def body(i, _, place=place, shift=shift):
+                    target = pl.multiple_of(place + i * step, TILE)
+                    stage[pl.ds(target, step)] = lin[pl.ds(shift + i * step, step)].astype(BF)
+                    return 0
+
+                lax.fori_loop(0, blocks, body, 0)
+                if tail:
+                    source = shift + blocks * step
+                    target = place + blocks * step
+                    stage[target : target + tail] = lin[source : source + tail].astype(BF)
+                copy = pltpu.make_async_copy(
+                    stage.at[pl.ds(place, end - first)],
+                    out_ref.at[chunk, pl.ds(base, end - first)],
+                    out_sem.at[len(stores)],
+                )
+                copy.start()
+                stores.append(copy)
+                place += end - first
+                done = end
+            if not whole:
+                break
+            done = stop if slot + 1 == len(pieces) else min(done, stop)
+            slot += 1
+        if not last:
+            lin[0:TILE] = lin[number : number + TILE]
+    for copy in stores:
+        copy.wait()
+
+
+def pack_grads(grads, plan, indices, step=128):
+    spots = linear_layout()
+    tallest = max(spots[i][1] for i in indices)
+    begin = spots[indices[0]][0]
+    total = spots[indices[-1]][0] + spots[indices[-1]][1] - begin
+    count = len(plan.segments(begin, total))
+    anywhere = pl.BlockSpec(memory_space=pl.ANY)
+    return pl.pallas_call(
+        functools.partial(pack_kernel, plan=plan, indices=indices, step=step),
+        in_specs=[anywhere] * len(indices),
+        out_specs=anywhere,
+        out_shape=jax.ShapeDtypeStruct((plan.devices, plan.chunk, LANE), BF),
+        scratch_shapes=[
+            pltpu.VMEM((tallest + 2 * TILE, LANE), F32),
+            pltpu.VMEM((total + 2 * TILE * (count + len(indices)), LANE), BF),
+            pltpu.SemaphoreType.DMA((len(indices),)),
+            pltpu.SemaphoreType.DMA((count + len(indices),)),
+        ]
+        + [pltpu.VMEM(g.shape, g.dtype) for g in grads],
+        compiler_params=pltpu.CompilerParams(vmem_limit_bytes=VMEM_LIMIT),
+        name="pack",
+    )(*grads)
+
+
+MESH = pl.DeviceIdType.MESH
+ROWS = 208
+
+
+def place_of():
+    dp, fs = lax.axis_index("dp"), lax.axis_index("fsdp")
+    return dp, fs, dp // 2, dp % 2, fs // 2, fs % 2
+
+
+def meet_all(me, devices, inner):
+    barrier = pltpu.get_barrier_semaphore()
+
+    def greet(i, _):
+        other = (me + i) % devices
+        pl.semaphore_signal(
+            barrier, inc=1, device_id=(other // inner, other % inner), device_id_type=MESH
+        )
+        return 0
+
+    lax.fori_loop(1, devices, greet, 0)
+    pl.semaphore_wait(barrier, devices - 1)
+
+
+def when_all(conditions):
+    total = None
+    for condition in conditions:
+        if condition is not None:
+            total = condition if total is None else total & condition
+    return total
+
+
+def guarded(condition, body):
+    if condition is None:
+        body()
+    else:
+        pl.when(condition)(body)
+
+
+def gather_kernel(
+    slot_ref, out_ref, own_sem, lend_send, lend_recv, send_sem, recv_sem, *, plan, inner
+):
+    dp, fs, y, x, z, c = place_of()
+    me = dp * inner + fs
+    lead, lent, kept = plan.lead, plan.lent, plan.kept
+    levels = inner // 2
+    meet_all(me, plan.devices, inner)
+
+    def own_copy():
+        start = pl.multiple_of(jnp.where(me == lead, plan.base, 0), TILE)
+        return pltpu.make_async_copy(
+            slot_ref.at[pl.ds(start, plan.chunk)], out_ref.at[me], own_sem
+        )
+
+    def lend(slot, target, part):
+        return pltpu.make_async_remote_copy(
+            src_ref=slot_ref.at[pl.ds(kept, lent)],
+            dst_ref=out_ref.at[target, pl.ds(pl.multiple_of(part * lent, TILE), lent)],
+            send_sem=lend_send.at[slot],
+            recv_sem=lend_recv.at[part],
+            device_id=(target // inner, target % inner),
+            device_id_type=MESH,
+        )
+
+    lender = jnp.maximum(me - lead - 1, 0)
+
+    @pl.when(me > lead)
+    def _():
+        lend(0, lender // 2, lender % 2).start()
+
+    @pl.when(me == lead)
+    def _():
+        lend(0, lead - 1, 0).start()
+        lend(1, lead - 1, 1).start()
+
+    @pl.when(me >= lead)
+    def _():
+        own_copy().start()
+        own_copy().wait()
+
+    @pl.when(me < lead)
+    def _():
+        lend(0, lead - 1, 0).wait_recv()
+        lend(0, lead - 1, 1).wait_recv()
+
+    across = {
+        "up": (dp, fs + 2),
+        "down": (dp, fs - 2),
+        "x": (dp + 1 - 2 * x, fs),
+        "y": (dp + 2 - 4 * y, fs),
+        "twin": (dp, fs + 1 - 2 * c),
+    }
+    kinds = tuple(across)
+    pending = []
+
+    def copy(kind, yy, xx, zz, part, cc=None):
+        core = c if cc is None else cc
+        column = yy * 2 + xx
+        index = column * inner + zz * 2 + core
+        rows = pl.ds(part * lent, lent)
+        return pltpu.make_async_remote_copy(
+            src_ref=out_ref.at[index, rows],
+            dst_ref=out_ref.at[index, rows],
+            send_sem=send_sem.at[kinds.index(kind), column * levels + zz, part],
+            recv_sem=recv_sem.at[index, part],
+            device_id=across[kind],
+            device_id_type=MESH,
+        )
+
+    def send(condition, kind, yy, xx, zz, part):
+        guarded(condition, lambda: copy(kind, yy, xx, zz, part).start())
+        pending.append((condition, kind, yy, xx, zz, part))
+
+    def arrive(condition, yy, xx, zz, part):
+        guarded(condition, lambda: copy("x", yy, xx, zz, part).wait_recv())
+
+    def spread(distance):
+        for sign in (1, -1) if distance else (0,):
+            zz = z + sign * distance
+            inside = when_all(
+                [zz < levels if sign > 0 else None, zz >= 0 if sign < 0 else None]
+            )
+            yield zz, sign, inside
+
+    for turn in range(levels + 2):
+        if turn < levels:
+            for zz, sign, inside in spread(turn):
+                for part in range(2):
+                    if turn:
+                        arrive(inside, y, x, zz, part)
+                    if sign <= 0:
+                        send(when_all([inside, z < levels - 1]), "up", y, x, zz, part)
+                    if sign >= 0:
+                        send(when_all([inside, z > 0]), "down", y, x, zz, part)
+                    for kind in ("x", "y") if part else ("y", "x"):
+                        send(inside, kind, y, x, zz, part)
+                    send(inside, "twin", y, x, zz, part)
+        if 1 <= turn <= levels:
+            for zz, sign, inside in spread(turn - 1):
+                arrive(inside, y, 1 - x, zz, 0)
+                send(inside, "y", y, 1 - x, zz, 0)
+                send(inside, "twin", y, 1 - x, zz, 0)
+                arrive(inside, 1 - y, x, zz, 1)
+                send(inside, "x", 1 - y, x, zz, 1)
+                send(inside, "twin", 1 - y, x, zz, 1)
+                arrive(inside, 1 - y, x, zz, 0)
+                send(inside, "twin", 1 - y, x, zz, 0)
+                arrive(inside, y, 1 - x, zz, 1)
+                send(inside, "twin", y, 1 - x, zz, 1)
+        if turn >= 2:
+            for zz, sign, inside in spread(turn - 2):
+                for part in range(2):
+                    arrive(inside, 1 - y, 1 - x, zz, part)
+                    send(inside, "twin", 1 - y, 1 - x, zz, part)
+
+    def twin_arrivals(i, _):
+        column, zz = i // levels, i % levels
+        for part in range(2):
+            copy("twin", column // 2, column % 2, zz, part, 1 - c).wait_recv()
+        return 0
+
+    lax.fori_loop(0, 4 * levels, twin_arrivals, 0)
+    for condition, kind, yy, xx, zz, part in pending:
+        guarded(condition, lambda: copy(kind, yy, xx, zz, part).wait_send())
+
+    @pl.when(me >= lead)
+    def _():
+        lend(0, lead - 1, 0).wait_send()
+
+    @pl.when(me == lead)
+    def _():
+        lend(1, lead - 1, 1).wait_send()
+
+
+def gather_chunks(slot, plan, inner, collective):
+    anywhere = pl.BlockSpec(memory_space=pl.ANY)
+    dma = pltpu.SemaphoreType.DMA
+    return pl.pallas_call(
+        functools.partial(gather_kernel, plan=plan, inner=inner),
+        in_specs=[anywhere],
+        out_specs=anywhere,
+        out_shape=jax.ShapeDtypeStruct((plan.devices, plan.chunk, LANE), BF),
+        scratch_shapes=[
+            dma,
+            dma((2,)),
+            dma((2,)),
+            dma((5, plan.devices // 2, 2)),
+            dma((plan.devices, 2)),
+        ],
+        compiler_params=pltpu.CompilerParams(collective_id=collective, has_side_effects=True),
+        name="gather_chunks",
+    )(slot)
+
+
+def scatter_kernel(
+    g_ref,
+    out_ref,
+    acc,
+    twin,
+    wide_y,
+    wide_x,
+    slim_x,
+    slim_y,
+    line,
+    load_sem,
+    twin_send,
+    twin_recv,
+    wide_send,
+    wide_recv,
+    slim_send,
+    slim_recv,
+    line_send,
+    line_recv,
+    own_sem,
+    back_send,
+    back_recv,
+    *,
+    plan,
+    inner,
+):
+    dp, fs, y, x, z, c = place_of()
+    me = dp * inner + fs
+    lead, lent, kept = plan.lead, plan.lent, plan.kept
+    levels = inner // 2
+    x_mate = (dp + 1 - 2 * x, fs)
+    y_mate = (dp + 2 - 4 * y, fs)
+    meet_all(me, plan.devices, inner)
+
+    def remote(source, target, send, receive, device):
+        return pltpu.make_async_remote_copy(
+            src_ref=source,
+            dst_ref=target,
+            send_sem=send,
+            recv_sem=receive,
+            device_id=device,
+            device_id_type=MESH,
+        )
+
+    def slot_of(yy, xx, zz):
+        return (yy * 2 + xx) * levels + zz
+
+    def load(yy, xx, zz):
+        slot = slot_of(yy, xx, zz)
+        return pltpu.make_async_copy(
+            g_ref.at[(yy * 2 + xx) * inner + zz * 2 + c], acc.at[slot], load_sem.at[slot]
+        )
+
+    def to_twin(yy, xx, zz):
+        slot = slot_of(yy, xx, zz)
+        return remote(
+            g_ref.at[(yy * 2 + xx) * inner + zz * 2 + 1 - c],
+            twin.at[slot],
+            twin_send.at[slot],
+            twin_recv.at[slot],
+            (dp, fs + 1 - 2 * c),
+        )
+
+    def piece(slot, part):
+        return acc.at[slot, pl.ds(part * lent, lent)]
+
+    def wide(part, other, zz, yy=0, xx=0):
+        buffer, device = (wide_x, x_mate) if part else (wide_y, y_mate)
+        index = other * levels + zz
+        return remote(
+            piece(slot_of(yy, xx, zz), part),
+            buffer.at[index],
+            wide_send.at[part, index],
+            wide_recv.at[part, index],
+            device,
+        )
+
+    def slim(part, zz, yy=0, xx=0):
+        buffer, device = (slim_y, y_mate) if part else (slim_x, x_mate)
+        return remote(
+            piece(slot_of(yy, xx, zz), part),
+            buffer.at[zz],
+            slim_send.at[part, zz],
+            slim_recv.at[part, zz],
+            device,
+        )
+
+    def along(upward, zz, part):
+        way = 0 if upward else 1
+        return remote(
+            piece(slot_of(y, x, zz), part),
+            line.at[way, zz, part],
+            line_send.at[way, zz, part],
+            line_recv.at[way, zz, part],
+            (dp, fs + 2 if upward else fs - 2),
+        )
+
+    def add(slot, first, count, source):
+        def body(i, _):
+            at = pl.multiple_of(i * ROWS, TILE)
+            to = pl.ds(pl.multiple_of(first + i * ROWS, TILE), ROWS)
+            acc[slot, to] = (
+                acc[slot, to].astype(F32) + source[pl.ds(at, ROWS)].astype(F32)
+            ).astype(BF)
+            return 0
+
+        lax.fori_loop(0, count // ROWS, body, 0)
+
+    def add_part(slot, part, source):
+        add(slot, part * lent, lent, source)
+
+    def level(k):
+        return jnp.where(z < levels // 2, z + levels - 1 - k, z + 1 + k) % levels
+
+    columns = ((1 - y, 1 - x), (1 - y, x), (y, 1 - x), (y, x))
+
+    for yy, xx in columns:
+
+        def begin(k, _, yy=yy, xx=xx):
+            to_twin(yy, xx, level(k)).start()
+            load(yy, xx, level(k)).start()
+            return 0
+
+        lax.fori_loop(0, levels, begin, 0)
+
+    def settle(yy, xx, zz):
+        slot = slot_of(yy, xx, zz)
+        load(yy, xx, zz).wait()
+        to_twin(yy, xx, zz).wait_recv()
+        add(slot, 0, plan.chunk, twin.at[slot])
+
+    def diagonal(k, _):
+        zz = level(k)
+        settle(1 - y, 1 - x, zz)
+        wide(0, 1 - x, zz, 1 - y, 1 - x).start()
+        wide(1, 1 - y, zz, 1 - y, 1 - x).start()
+        return 0
+
+    def sides(k, _):
+        zz = level(k)
+        settle(1 - y, x, zz)
+        wide(0, x, zz, 1 - y, x).start()
+        settle(y, 1 - x, zz)
+        wide(1, y, zz, y, 1 - x).start()
+        return 0
+
+    def middle(k, _):
+        zz = level(k)
+        wide(0, 1 - x, zz).wait_recv()
+        add_part(slot_of(y, 1 - x, zz), 0, wide_y.at[(1 - x) * levels + zz])
+        slim(0, zz, y, 1 - x).start()
+        wide(1, 1 - y, zz).wait_recv()
+        add_part(slot_of(1 - y, x, zz), 1, wide_x.at[(1 - y) * levels + zz])
+        slim(1, zz, 1 - y, x).start()
+        return 0
+
+    def home(k, _):
+        zz = level(k)
+        slot = slot_of(y, x, zz)
+        settle(y, x, zz)
+        wide(0, x, zz).wait_recv()
+        add_part(slot, 0, wide_y.at[x * levels + zz])
+        wide(1, y, zz).wait_recv()
+        add_part(slot, 1, wide_x.at[y * levels + zz])
+        return 0
+
+    lax.fori_loop(0, levels, diagonal, 0)
+    lax.fori_loop(0, levels, sides, 0)
+    lax.fori_loop(0, levels, middle, 0)
+    lax.fori_loop(0, levels, home, 0)
+
+    def column_sum_of(zz):
+        slot = slot_of(y, x, zz)
+        slim(0, zz).wait_recv()
+        add_part(slot, 0, slim_x.at[zz])
+        slim(1, zz).wait_recv()
+        add_part(slot, 1, slim_y.at[zz])
+
+    def take(upward, zz, part):
+        along(upward, zz, part).wait_recv()
+        add_part(slot_of(y, x, zz), part, line.at[0 if upward else 1, zz, part])
+
+    sent = []
+    for distance in range(levels - 1, 0, -1):
+        for upward in (True, False):
+            zz = z + distance if upward else z - distance
+            inside = zz < levels if upward else zz >= 0
+            more = z > 0 if upward else z < levels - 1
+
+            @pl.when(inside)
+            def _(upward=upward, zz=zz, more=more):
+                column_sum_of(zz)
+                for part in range(2):
+
+                    @pl.when(more)
+                    def _(part=part):
+                        take(upward, zz, part)
+
+                    along(upward, zz, part).start()
+
+            sent.append((inside, upward, zz))
+    column_sum_of(z)
+    for part in range(2):
+
+        @pl.when(z > 0)
+        def _(part=part):
+            take(True, z, part)
+
+        @pl.when(z < levels - 1)
+        def _(part=part):
+            take(False, z, part)
+
+    mine = slot_of(y, x, z)
+
+    def back(slot, part, owner):
+        return remote(
+            piece(mine, part),
+            out_ref.at[pl.ds(kept, lent)],
+            back_send.at[slot],
+            back_recv,
+            (owner // inner, owner % inner),
+        )
+
+    @pl.when(me < lead - 1)
+    def _():
+        back(0, 0, lead + 1 + 2 * me).start()
+        back(1, 1, lead + 2 + 2 * me).start()
+
+    @pl.when(me == lead - 1)
+    def _():
+        back(0, 0, me + 1).start()
+
+    @pl.when(me == lead)
+    def _():
+        count = kept - plan.base
+        copy = pltpu.make_async_copy(
+            acc.at[mine, pl.ds(0, count)], out_ref.at[pl.ds(plan.base, count)], own_sem
+        )
+        copy.start()
+        copy.wait()
+
+    @pl.when(me > lead)
+    def _():
+        copy = pltpu.make_async_copy(
+            acc.at[mine, pl.ds(0, kept)], out_ref.at[pl.ds(0, kept)], own_sem
+        )
+        copy.start()
+        copy.wait()
+
+    @pl.when(me >= lead)
+    def _():
+        back(0, 0, 0).wait_recv()
+
+    for inside, upward, zz in sent:
+
+        @pl.when(inside)
+        def _(upward=upward, zz=zz):
+            for part in range(2):
+                along(upward, zz, part).wait_send()
+
+    def finish(k, _):
+        zz = level(k)
+        for yy, xx in columns:
+            to_twin(yy, xx, zz).wait_send()
+        wide(0, 1 - x, zz).wait_send()
+        wide(0, x, zz).wait_send()
+        wide(1, 1 - y, zz).wait_send()
+        wide(1, y, zz).wait_send()
+        slim(0, zz).wait_send()
+        slim(1, zz).wait_send()
+        return 0
+
+    lax.fori_loop(0, levels, finish, 0)
+
+    @pl.when(me < lead)
+    def _():
+        back(0, 0, 0).wait_send()
+
+    @pl.when(me < lead - 1)
+    def _():
+        back(1, 1, 0).wait_send()
+
+
+def scatter_chunks(grads, plan, inner, collective):
+    anywhere = pl.BlockSpec(memory_space=pl.ANY)
+    dma = pltpu.SemaphoreType.DMA
+    half, levels = plan.devices // 2, inner // 2
+    part = (plan.lent, LANE)
+    return pl.pallas_call(
+        functools.partial(scatter_kernel, plan=plan, inner=inner),
+        in_specs=[anywhere],
+        out_specs=anywhere,
+        out_shape=jax.ShapeDtypeStruct((plan.padded, LANE), BF),
+        scratch_shapes=[
+            pltpu.VMEM((half, plan.chunk, LANE), BF),
+            pltpu.VMEM((half, plan.chunk, LANE), BF),
+            pltpu.VMEM((2 * levels, *part), BF),
+            pltpu.VMEM((2 * levels, *part), BF),
+            pltpu.VMEM((levels, *part), BF),
+            pltpu.VMEM((levels, *part), BF),
+            pltpu.VMEM((2, levels, 2, *part), BF),
+            dma((half,)),
+            dma((half,)),
+            dma((half,)),
+            dma((2, 2 * levels)),
+            dma((2, 2 * levels)),
+            dma((2, levels)),
+            dma((2, levels)),
+            dma((2, levels, 2)),
+            dma((2, levels, 2)),
+            dma,
+            dma((2,)),
+            dma,
+        ],
+        compiler_params=pltpu.CompilerParams(
+            collective_id=collective, has_side_effects=True, vmem_limit_bytes=VMEM_LIMIT
+        ),
+        name="scatter_chunks",
+    )(grads)
+
+
+def exchange_kernel(in_ref, out_ref, own_sem, send_sem, recv_sem, *, devices, inner, senders, receivers):
+    me = lax.axis_index("dp") * inner + lax.axis_index("fsdp")
+    meet_all(me, devices, inner)
+    many = len(in_ref.shape) == 3
+
+    def copy(source, target):
+        return pltpu.make_async_remote_copy(
+            src_ref=in_ref.at[target] if many else in_ref,
+            dst_ref=out_ref.at[source],
+            send_sem=send_sem.at[target],
+            recv_sem=recv_sem.at[source],
+            device_id=(target // inner, target % inner),
+            device_id_type=MESH,
+        )
+
+    def each(i, _, act):
+        other = (me + i) % devices
+        act(other)
+        return 0
+
+    def start(other):
+        pl.when((me < senders) & (other < receivers))(lambda: copy(me, other).start())
+
+    def landed(other):
+        pl.when((other < senders) & (me < receivers))(lambda: copy(other, other).wait_recv())
+
+    def gone(other):
+        pl.when((me < senders) & (other < receivers))(lambda: copy(me, other).wait_send())
+
+    lax.fori_loop(1, devices, functools.partial(each, act=start), 0)
+
+    @pl.when((me < senders) & (me < receivers))
+    def _():
+        own = pltpu.make_async_copy(in_ref.at[me] if many else in_ref, out_ref.at[me], own_sem)
+        own.start()
+        own.wait()
+
+    lax.fori_loop(1, devices, functools.partial(each, act=landed), 0)
+    lax.fori_loop(1, devices, functools.partial(each, act=gone), 0)
+
+
+def exchange(value, devices, inner, senders, receivers, collective, name):
+    anywhere = pl.BlockSpec(memory_space=pl.ANY)
+    dma = pltpu.SemaphoreType.DMA
+    return pl.pallas_call(
+        functools.partial(
+            exchange_kernel, devices=devices, inner=inner, senders=senders, receivers=receivers
+        ),
+        in_specs=[anywhere],
+        out_specs=anywhere,
+        out_shape=jax.ShapeDtypeStruct((senders, *value.shape[-2:]), value.dtype),
+        scratch_shapes=[dma, dma((devices,)), dma((devices,))],
+        compiler_params=pltpu.CompilerParams(collective_id=collective, has_side_effects=True),
+        name=name,
+    )(value)
+
+
+HALF = 27
+TALL = 72
+SLAB = 112
+CONDITION_ROWS = 832
+
+
+def ada_spots(me, plan):
+    lines = plan.share // HALF
+    odd = me % 2
+    limit = CONDITION_ROWS - TALL
+    return [
+        (odd, jnp.minimum((lines * me + odd) // 2, limit)),
+        (1 - odd, jnp.minimum((lines * me - odd) // 2, limit)),
+    ]
+
+
+def ada_kernel(lin_ref, cond_ref, out_ref, *, plan, inner):
+    me = lax.axis_index("dp") * inner + lax.axis_index("fsdp")
+    for half, (shift, top) in enumerate(ada_spots(me, plan)):
+        condition = cond_ref[pl.ds(top, TALL)].astype(BF)
+
+        def body(c, _, half=half, shift=shift, condition=condition):
+            rows = lin_ref[pl.ds(HALF * shift + c, TALL, stride=2 * HALF)].astype(BF)
+            part = tn(condition, rows)
+            count = plan.devices
+            for clip in range(2):
+                out_ref[pl.ds((2 * clip + half) * HALF + c, count, stride=SLAB)] = part[
+                    clip * count : (clip + 1) * count
+                ]
+            return 0
+
+        lax.fori_loop(0, HALF, body, 0)
+
+
+def ada_partial(lin, cond, plan, inner):
+    return pl.pallas_call(
+        functools.partial(ada_kernel, plan=plan, inner=inner),
+        out_shape=jax.ShapeDtypeStruct((plan.devices * SLAB, LANE), F32),
+        compiler_params=pltpu.CompilerParams(vmem_limit_bytes=VMEM_LIMIT),
+        name="ada_partial",
+    )(lin, cond)
+
+
+def own_grad_kernel(cond_ref, dmod_ref, rest_ref, g_ref, sums_ref, lin, *, plan, inner):
+    me = lax.axis_index("dp") * inner + lax.axis_index("fsdp")
+    count = plan.devices
+    border = jnp.clip(plan.first_row - plan.share * me, 0, plan.share)
+    for half, (shift, top) in enumerate(ada_spots(me, plan)):
+        condition = cond_ref[pl.ds(top, TALL)].astype(BF)
+
+        def body(c, _, half=half, shift=shift, condition=condition):
+            grads = jnp.concatenate(
+                [
+                    dmod_ref[pl.ds((2 * clip + half) * HALF + c, count, stride=SLAB)]
+                    for clip in range(2)
+                ],
+                axis=0,
+            ).astype(BF)
+            lin[pl.ds(HALF * shift + c, TALL, stride=2 * HALF)] = nn(condition, grads)
+            return 0
+
+        @pl.when(border > 0)
+        def _(body=body):
+            lax.fori_loop(0, HALF, body, 0)
+
+    rows = 64
+
+    def merge(i, total):
+        at = pl.multiple_of(i * rows, rows)
+        row = lax.broadcasted_iota(jnp.int32, (rows, LANE), 0) + at
+        rest = jnp.where(row < plan.share, rest_ref[pl.ds(at, rows)].astype(F32), 0.0)
+        value = jnp.where(row < border, lin[pl.ds(at, rows)], rest)
+        g_ref[pl.ds(at, rows)] = value
+        square = value * value
+        return total + sum(square[k : k + 8] for k in range(0, rows, 8))
+
+    sums_ref[...] = lax.fori_loop(0, plan.padded // rows, merge, jnp.zeros((8, LANE), F32))
+
+
+def own_grad(cond, dmod, rest, plan, inner):
+    return pl.pallas_call(
+        functools.partial(own_grad_kernel, plan=plan, inner=inner),
+        out_shape=[
+            jax.ShapeDtypeStruct((plan.padded, LANE), F32),
+            jax.ShapeDtypeStruct((8, LANE), F32),
+        ],
+        scratch_shapes=[pltpu.VMEM((2 * HALF * TALL, LANE), F32)],
+        compiler_params=pltpu.CompilerParams(vmem_limit_bytes=VMEM_LIMIT),
+        name="own_grad",
+    )(cond, dmod, rest)
+
+
+def fits(devices, inner, share):
+    return inner == 8 and devices == 32 and share % (LANE * HALF) == 0
+
+
+def local_fast(
+    latents, captions, lengths, timesteps, cotangent, master, first_moment, second_moment
+):
+    clips, frames, width = latents.shape
+    share = master.shape[0]
+    inner = lax.axis_size("fsdp")
+    devices = inner * lax.axis_size("dp")
+    plan = Plan(devices, share // LANE)
+    lead = plan.lead
+    indices = tuple(range(2, 13))
+
+    condition = jax.nn.silu(embed(timesteps)).astype(BF).astype(F32)
+    conditions = exchange(
+        jnp.pad(condition, ((0, 8 - clips), (0, 0))),
+        devices,
+        inner,
+        devices,
+        devices,
+        1,
+        "conditions",
+    )
+    columns = conditions[:, :clips].transpose(2, 1, 0).reshape(width, clips * devices)
+    columns = jnp.concatenate(
+        [
+            columns,
+            jnp.ones((1, clips * devices), F32),
+            jnp.zeros((CONDITION_ROWS - width - 1, clips * devices), F32),
+        ],
+        axis=0,
+    )
+    rows = master.reshape(plan.share, LANE)
+    lin = jnp.pad(rows, ((0, 2 * HALF * TALL - plan.share), (0, 0)))
+    slabs = ada_partial(lin, columns, plan, inner).reshape(devices, SLAB, LANE)
+    parts = exchange(slabs, devices, inner, lead + 1, devices, 2, "modulation")
+    mod = jnp.sum(parts, axis=0)[: 54 * clips].reshape(clips, 9, width)
+
+    slot = lin[: plan.padded].astype(BF)
+    gathered = gather_chunks(slot, plan, inner, 3)
+    weights = unpack_weights(gathered, plan, indices)
+    output, input_grad, grad_mod, gradients = block_pass(
+        latents, captions, lengths, cotangent, mod, weights
+    )
+    grad_rows = jnp.pad(
+        grad_mod.astype(F32).reshape(54 * clips, LANE), ((0, SLAB - 54 * clips), (0, 0))
+    )
+    dmod = exchange(grad_rows, devices, inner, devices, lead + 1, 4, "modulation_grads")
+    chunks = pack_grads(gradients, plan, indices)
+    rest = scatter_chunks(chunks, plan, inner, 5)
+    grads, squares = own_grad(
+        columns, dmod.reshape(devices * SLAB, LANE), rest, plan, inner
+    )
+    squares = exchange(squares, devices, inner, devices, devices, 6, "squares")
+    return (
+        output,
+        input_grad,
+        grads[: plan.share].reshape(share),
+        jnp.sum(squares),
+    )
+
+
+def local_any(
+    latents, captions, lengths, timesteps, cotangent, master, first_moment, second_moment
+):
+    clips, frames, width = latents.shape
+    share = master.shape[0]
+    devices = lax.axis_size("dp") * lax.axis_size("fsdp")
+    gathered = lax.all_gather(
+        master.astype(BF).reshape(1, share), ("dp", "fsdp"), axis=0, tiled=True
+    ).reshape(-1)
+    weights = unpack(gathered)
+    condition = jax.nn.silu(embed(timesteps)).astype(BF)
+    mod = jnp.dot(condition, weights[0], preferred_element_type=F32) + weights[1].astype(F32)
+    block_weights = [w.astype(F32).reshape(1, -1) if w.ndim == 1 else w for w in weights[2:]]
+    output, input_grad, grad_mod, gradients = block_pass(
+        latents, captions, lengths, cotangent, mod.reshape(clips, 9, width), block_weights
+    )
+    grad_mod = grad_mod.reshape(clips, 9 * width)
+    grad_ada = jnp.dot(condition.T, grad_mod, preferred_element_type=F32)
+    grad_list = [grad_ada, jnp.sum(grad_mod.astype(F32), axis=0)] + gradients
+    flat = jnp.concatenate([piece.astype(F32).reshape(-1) for piece in grad_list])
+    grad = lax.psum_scatter(
+        flat.reshape(devices, share), ("dp", "fsdp"), scatter_dimension=0, tiled=True
+    ).reshape(share)
+    return output, input_grad, grad, lax.psum(jnp.sum(grad * grad), ("dp", "fsdp"))
+
+
 def local(
     latents,
     captions,
@@ -798,31 +1804,19 @@
     first_moment,
     second_moment,
 ):
-    clip_count, frames, model_width = latents.shape
-    share = master_weights.shape[0]
-    outer_count = lax.axis_size("dp")
-    inner_count = lax.axis_size("fsdp")
-    gathered = lax.all_gather(
-        master_weights.astype(BF).reshape(1, share), ("dp", "fsdp"), axis=0, tiled=True
-    ).reshape(-1)
-    weights = unpack(gathered)
-    condition = jax.nn.silu(embed(timesteps)).astype(BF)
-    modulation = jnp.dot(condition, weights[0], preferred_element_type=F32) + weights[1].astype(F32)
-    mod = modulation.reshape(clip_count, 9, model_width)
-    block_weights = [w.astype(F32).reshape(1, -1) if w.ndim == 1 else w for w in weights[2:]]
-    output, input_grad, grad_mod, gradients = block_pass(
-        latents, captions, caption_lengths, cotangent, mod, block_weights
-    )
-    grad_mod = grad_mod.reshape(clip_count, 9 * model_width)
-    grad_ada = jnp.dot(condition.T, grad_mod, preferred_element_type=F32)
-    grad_ada_bias = jnp.sum(grad_mod.astype(F32), axis=0)
-    gradient_list = [grad_ada, grad_ada_bias] + gradients
-    flat_grad = jnp.concatenate([piece.astype(F32).reshape(-1) for piece in gradient_list])
-    owner_rows = flat_grad.reshape(outer_count * inner_count, share)
-    grad_shard = lax.psum_scatter(
-        owner_rows, ("dp", "fsdp"), scatter_dimension=0, tiled=True
-    ).reshape(share)
-    squares = lax.psum(jnp.sum(grad_shard * grad_shard), ("dp", "fsdp"))
+    inner = lax.axis_size("fsdp")
+    devices = inner * lax.axis_size("dp")
+    run = local_fast if fits(devices, inner, master_weights.shape[0]) else local_any
+    output, input_grad, grad_shard, squares = run(
+        latents,
+        captions,
+        caption_lengths,
+        timesteps,
+        cotangent,
+        master_weights,
+        first_moment,
+        second_moment,
+    )
     grad_norm = jnp.sqrt(squares)
     clipped = grad_shard * (CLIP / jnp.maximum(grad_norm, CLIP))
     new_first = BETA_ONE * first_moment + (1.0 - BETA_ONE) * clipped

time: 2480 us -> 758 us (0.31)
  waiting for transfers between devices: 1180 us -> 0 us
  local copies, waits for them, and re-layouts: 662 us -> 6.03 us
  Pallas kernels: 307 us -> 716 us
  other arithmetic: 221 us -> 12.6 us
  blocking collectives: 39.5 us -> 0 us
    unnamed x3 -> x0, waiting for transfers between devices: 854 us -> none
    unnamed x40 -> x10, local copies, waits for them, and re-layouts: 445 us -> 1.23 us
    pallas_call x0 -> x10, Pallas kernels: none -> 410 us  [the longest x1 133 us: scatter_chunks(): pl.pallas_call(functools.partial(scatter_kernel, plan=plan, inner=inner),...]
    all_gather x1 -> x0, waiting for transfers between devices: 328 us -> none  [local(): lax.all_gather(master_weights.astype(BF).reshape(1, share), ('dp', 'fsdp'...]
    all_gather x1 -> x0, other arithmetic: 178 us -> none  [local(): lax.all_gather(master_weights.astype(BF).reshape(1, share), ('dp', 'fsdp'...]
    reshape x14 -> x2, local copies, waits for them, and re-layouts: 133 us -> 0.81 us  [the longest x1 0.65 us: local_fast(): mod = jnp.sum(parts, axis=0)[:54 * clips].reshape(clips, 9, width)]
    slice x12 -> x0, local copies, waits for them, and re-layouts: 80.4 us -> none  [unpack(): pieces.append(flat_vector[offset:offset + number].reshape(layout_shape))]
    psum x1 -> x0, blocking collectives: 39.5 us -> none  [local(): squares = lax.psum(jnp.sum(grad_shard * grad_shard), ('dp', 'fsdp'))]
  transfers between devices with their start and end apart: 2 -> 0, of which waited for: 2 -> 0; matrix products, arithmetic and copies ran while one was open for 0% -> 0% of each run, Pallas kernels for 0% -> 0%
where the time goes in v2:
time: 758 us; the launch traced here: 748 us
  Pallas kernels  716 us (94%)
  other arithmetic  12.6 us (2%)
  matrix products  9.73 us (1%)
    pallas_call x1, Pallas kernels, scatter_chunks(): pl.pallas_call(functools.partial(scatter_kernel, plan=plan, inner=inner),...  133 us
    pallas_call x1, Pallas kernels, gather_chunks(): pl.pallas_call(functools.partial(gather_kernel, plan=plan, inner=inner),...  116 us
    pallas_call x4, Pallas kernels, exchange(): pl.pallas_call(functools.partial(exchange_kernel, devices=devices, inner=...  104 us
    pallas_call x1, Pallas kernels, feed(): call(functools.partial(feed_kernel, clips=clips, frames=frames, rows=rows...  84.8 us
    pallas_call x2, Pallas kernels, attend_backward(): call(functools.partial(attend_back_kernel, masked=masked), (clips, groups...  75.9 us
    pallas_call x2, Pallas kernels, attend_forward(): call(functools.partial(attend_kernel, masked=masked), (clips, groups), sp...  48.1 us
    pallas_call x1, Pallas kernels, input_back(): call(input_kernel, (clips, frames // rows), [spec] * 5 + [clip_spec(9, wi...  30.3 us
    pallas_call x1, Pallas kernels, before_self(): call(before_self_kernel, (clips, frames // rows), [spec, spec, spec, spec...  24.5 us

profile of v2, /device:TPU:0, one launch (start us, length us, event | category | flops | bytes accessed | tf_op | source)
XLA Modules:
  0.0 747.7 jit_solution(10677895110717107323)
XLA Ops:
  0.7 1.2 copy-done
  3.4 25.3 %conditions.1 = f32[32,8,768]{2,1,0:T(8,128)} custom-call(f32[8,768]{1,0:T(8,128)} %pad_convert_fusion.2.in_ref), custom_call_target="tpu_custom_call" | custom-call | tf_op jit(solution)/shard_map/conditions/pallas_call | solution.py:1602
  28.7 1.2 slice_bitcast_fusion
  30.0 1.0 maximum_maximum_fusion.cond_ref
  31.1 1.0 pad_convert_fusion.slot_ref
  32.1 1.4 pad.16.lin_ref
  33.5 12.6 %ada_partial.1 = f32[3584,128]{1,0:T(8,128)} custom-call(f32[3888,128]{1,0:T(8,128)} %pad.16.lin_ref, f32[832,64]{1,0:T(8,128)} %maximum_maximum_fusion.cond_ref), custom_call_target="tpu_custom_call" | custom-call | tf_op jit(solution)/shard_map/ada_partial/pallas_call | solution.py:1650
  46.2 44.0 %modulation.1 = f32[12,112,128]{2,1,0:T(8,128)} custom-call(f32[32,112,128]{2,1,0:T(8,128)} %bitcast.36), custom_call_target="tpu_custom_call" | custom-call | tf_op jit(solution)/shard_map/modulation/pallas_call | solution.py:1602
  90.2 1.1 reduce_sum.18
  92.0 116.1 %gather_chunks.1.refs_0_ = bf16[32,2496,128]{2,1,0:T(8,128)(2,1)} custom-call(bf16[3712,128]{1,0:T(8,128)(2,1)} %pad_convert_fusion.slot_ref), custom_call_target="tpu_custom_call" | custom-call | tf_op jit(solution)/shard_map/gather_chunks/pallas_call | solution.py:1220
  208.1 16.4 %unpack.1 = (bf16[768,2304]{1,0:T(8,128)(2,1)}, bf16[768,768]{1,0:T(8,128)(2,1)}, f32[1,768]{1,0:T(1,128)}, bf16[768,768]{1,0:T(8,128)(2,1)}, bf16[1024,1536]{1,...) custom-call(bf16[32,2496,128]{2,1,0:T(8,128)(2,1)} %gather_chunks.1., ...), custom_call_target="tpu_custom_call" | custom-call | tf_op jit(solution)/shard_map/unpack/pallas_call | solution.py:919
  224.5 4.8 convolution_convert_fusion
  229.4 11.7 %qkv_forward.1.refs_0_.refs_1_.refs_2_ = bf16[2,864,2304]{2,1,0:T(8,128)(2,1)} custom-call(bf16[2,864,768]{2,1,0:T(8,128)(2,1)} %x_ref.5, f32[2,9,768]{2,1,0:T(8,128)} %reshape.51.mod_ref, bf16[768,2304]{1,0:T(8,128)(2,1)} %get-tuple-element.54.w_ref), custom_call_target="tpu_custom_call" | custom-call | tf_op jit(solution)/shard_map/qkv_forward/pallas_call | solution.py:160
  241.0 33.8 %self_forward.1 = (bf16[2,864,768]{2,1,0:T(8,128)(2,1)}, f32[2,6,864,128]{3,2,1,0:T(8,128)}) custom-call(bf16[2,864,2304]{2,1,0:T(8,128)(2,1)} %qkv_forward.1.refs_0_.refs_1_.refs_2_, bf16[2,864,2304]{2,1,0:T(8,128)(2,1)} %qkv_forward.1.refs_0_.refs_1_.refs_2_, bf16[2,864,2304]{2,1,0:T(8,128)(2,1)} %qkv_forward.1.refs_0_.refs_1_.refs_2_), custom_call_target="tpu_custom_call" | custom-call | tf_op jit(solution)/shard_map/self_forward/pallas_call | solution.py:232
  274.9 10.8 %after_self.1 = (bf16[2,864,768]{2,1,0:T(8,128)(2,1)}, f32[2,864,768]{2,1,0:T(8,128)}, bf16[2,864,768]{2,1,0:T(8,128)(2,1)}) custom-call(bf16[2,864,768]{2,1,0:T(8,128)(2,1)} %get-tuple-element.55.o_ref.refs_4_, bf16[2,864,768]{2,1,0:T(8,128)(2,1)} %x_ref.5, f32[2,9,768]{2,1,0:T(8,128)} %reshape.51.mod_ref, bf16[768,768]{1,0:T(8,128)(2,1)} %get-tuple-element.56.wo_ref, ...), custom_call_target="tpu_custom_call" | custom-call | tf_op jit(solution)/shard_map/after_self/pallas_call | solution.py:344
  285.7 14.2 %cross_forward.1 = (bf16[2,864,768]{2,1,0:T(8,128)(2,1)}, f32[2,6,864,128]{3,2,1,0:T(8,128)}) custom-call(s32[2]{0:T(128)} %refs_0_.3, bf16[2,864,768]{2,1,0:T(8,128)(2,1)} %get-tuple-element.59.refs_1_, bf16[2,256,1536]{2,1,0:T(8,128)(2,1)} %bitcast.29, bf16[2,256,1536]{2,1,0:T(8,128)(2,1)} %bitcast.30), custom_call_target="tpu_custom_call" | custom-call | tf_op jit(solution)/shard_map/cross_forward/pallas_call | solution.py:232
  299.9 8.6 %after_cross.1 = (bf16[2,864,768]{2,1,0:T(8,128)(2,1)}, f32[2,864,768]{2,1,0:T(8,128)}) custom-call(bf16[2,864,768]{2,1,0:T(8,128)(2,1)} %get-tuple-element.61.o_ref.refs_5_, f32[2,864,768]{2,1,0:T(8,128)} %get-tuple-element.62.h_ref, f32[2,9,768]{2,1,0:T(8,128)} %reshape.51.mod_ref, bf16[768,768]{1,0:T(8,128)(2,1)} %get-tuple-element.63.wo_ref.w_ref, ...), custom_call_target="tpu_custom_call" | custom-call | tf_op jit(solution)/shard_map/after_cross/pallas_call | solution.py:368
  308.6 84.8 %feed.1 = (bf16[2,864,768]{2,1,0:T(8,128)(2,1)}, f32[2,864,768]{2,1,0:T(8,128)}, bf16[768,3072]{1,0:T(8,128)(2,1)}, bf16[3072,768]{1,0:T(8,128)(2,1)}, f32[1,307...) custom-call(f32[2,864,768]{2,1,0:T(8,128)} %get-tuple-element.65.h_ref, bf16[2,864,768]{2,1,0:T(8,128)(2,1)} %dy_ref.1, ...), custom_call_target="tpu_custom_call" | custom-call | tf_op jit(solution)/shard_map/feed/pallas_call | solution.py:513
  393.4 11.9 %before_cross.1 = (bf16[2,864,768]{2,1,0:T(8,128)(2,1)}, bf16[768,768]{1,0:T(8,128)(2,1)}, f32[1,768]{1,0:T(1,128)}, f32[2,1,768]{2,1,0:T(1,128)}) custom-call(f32[2,864,768]{2,1,0:T(8,128)} %get-tuple-element.71.dh_ref, bf16[2,864,768]{2,1,0:T(8,128)(2,1)} %get-tuple-element.72.z_ref, bf16[2,864,768]{2,1,0:T(8,128)(2,1)} %get-tuple-element.61.o_ref.refs_5_, ...), custom_call_target="tpu_custom_call" | custom-call | tf_op jit(solution)/shard_map/before_cross/pallas_call | solution.py:582
  405.3 23.3 %cross_back.1 = (bf16[2,864,768]{2,1,0:T(8,128)(2,1)}, bf16[2,256,768]{2,1,0:T(8,128)(2,1)}, bf16[2,256,768]{2,1,0:T(8,128)(2,1)}) custom-call(s32[2]{0:T(128)} %refs_0_.3, bf16[2,864,768]{2,1,0:T(8,128)(2,1)} %get-tuple-element.59.refs_1_, bf16[2,256,1536]{2,1,0:T(8,128)(2,1)} %bitcast.31, bf16[2,256,1536]{2,1,0:T(8,128)(2,1)} %bitcast.32, ...), custom_call_target="tpu_custom_call" | custom-call | tf_op jit(solution)/shard_map/cross_back/pallas_call | solution.py:315
  428.6 24.5 %before_self.1 = (f32[2,864,768]{2,1,0:T(8,128)}, bf16[2,864,768]{2,1,0:T(8,128)(2,1)}, bf16[768,768]{1,0:T(8,128)(2,1)}, bf16[768,768]{1,0:T(8,128)(2,1)}, f32[1,768]{1,0:T(1,128)}, /*index=5*/f32[2,3,768]{2,1,0:T(4,128)}) custom-call(bf16[2,864,768]{2,1,0:T(8,128)(2,1)} %get-tuple-element.75.dq_ref, f32[2,864,768]{2,1,0:T(8,128)} %get-tuple-element.62.h_ref, ...), custom_call_target="tpu_custom_call" | custom-call | tf_op jit(solution)/shard_map/before_self/pallas_call | solution.py:649
  453.1 52.5 %self_back.1 = (bf16[2,864,768]{2,1,0:T(8,128)(2,1)}, bf16[2,864,768]{2,1,0:T(8,128)(2,1)}, bf16[2,864,768]{2,1,0:T(8,128)(2,1)}) custom-call(bf16[2,864,2304]{2,1,0:T(8,128)(2,1)} %qkv_forward.1.refs_0_.refs_1_.refs_2_, bf16[2,864,2304]{2,1,0:T(8,128)(2,1)} %qkv_forward.1.refs_0_.refs_1_.refs_2_, bf16[2,864,2304]{2,1,0:T(8,128)(2,1)} %qkv_forward.1.refs_0_.refs_1_.refs_2_, ...), custom_call_target="tpu_custom_call" | custom-call | tf_op jit(solution)/shard_map/self_back/pallas_call | solution.py:315
  505.7 30.3 %input_back.1 = (bf16[2,864,768]{2,1,0:T(8,128)(2,1)}, bf16[768,2304]{1,0:T(8,128)(2,1)}, f32[2,2,768]{2,1,0:T(2,128)}) custom-call(bf16[2,864,768]{2,1,0:T(8,128)(2,1)} %get-tuple-element.79.dq_ref, bf16[2,864,768]{2,1,0:T(8,128)(2,1)} %get-tuple-element.80.dk_ref, bf16[2,864,768]{2,1,0:T(8,128)(2,1)} %get-tuple-element.81.dv_ref, ...), custom_call_target="tpu_custom_call" | custom-call | tf_op jit(solution)/shard_map/input_back/pallas_call | solution.py:697
  536.0 0.7 convert.24
  537.7 23.8 %modulation_grads.1 = f32[32,112,128]{2,1,0:T(8,128)} custom-call(f32[112,128]{1,0:T(8,128)} %pad_convert_fusion.1.in_ref), custom_call_target="tpu_custom_call" | custom-call | tf_op jit(solution)/shard_map/modulation_grads/pallas_call | solution.py:1602
  561.5 4.9 fusion.refs_4_
  566.4 15.6 %pack.1.g_ref = bf16[32,2496,128]{2,1,0:T(8,128)(2,1)} custom-call(bf16[768,2304]{1,0:T(8,128)(2,1)} %get-tuple-element.88.refs_0_, bf16[768,768]{1,0:T(8,128)(2,1)} %get-tuple-element.89.refs_1_, f32[1,768]{1,0:T(1,128)} %get-tuple-element.90.refs_2_, bf16[768,768]{1,0:T(8,128)(2,1)} %get-tuple-element.91.refs_3_, bf16[1024,1536]{1,0:T(8,128)(2,1)} %fusion.refs_4_, ...), custom_call_target="tpu_custom_call" | custom-call | tf_op jit(solution)/shard_map/pack/pallas_call | solution.py:1027
  582.0 133.0 %scatter_chunks.1.rest_ref = bf16[3712,128]{1,0:T(8,128)(2,1)} custom-call(bf16[32,2496,128]{2,1,0:T(8,128)(2,1)} %pack.1.g_ref), custom_call_target="tpu_custom_call" | custom-call | tf_op jit(solution)/shard_map/scatter_chunks/pallas_call | solution.py:1525
  715.0 11.7 %own_grad.1 = (f32[3712,128]{1,0:T(8,128)}, f32[8,128]{1,0:T(8,128)}) custom-call(f32[832,64]{1,0:T(8,128)} %maximum_maximum_fusion.cond_ref, f32[3584,128]{1,0:T(8,128)} %bitcast.35, bf16[3712,128]{1,0:T(8,128)(2,1)} %scatter_chunks.1.rest_ref), custom_call_target="tpu_custom_call" | custom-call | tf_op jit(solution)/shard_map/own_grad/pallas_call | solution.py:1695
  726.7 11.1 %squares.1 = f32[32,8,128]{2,1,0:T(8,128)} custom-call(f32[8,128]{1,0:T(8,128)} %get-tuple-element.100.in_ref), custom_call_target="tpu_custom_call" | custom-call | tf_op jit(solution)/shard_map/squares/pallas_call | solution.py:1602
  737.8 1.5 reduce_sum.19
  740.1 6.1 multiply_subtract_fusion
  (28 shorter events, 3.3 us)
Async XLA Ops:
  0.6 1.2 copy-start
  0.6 30.4 %copy-start.1 = (f32[473472]{0:T(1024)S(1)}, f32[473472]{0:T(1024)}, u32[]{:S(2)}) copy-start(f32[473472]{0:T(1024)} %param.13) | copy-start | bytes 5681668
  505.7 31.1 %copy-start.4 = (f32[2,1,768]{2,1,0:T(1,128)S(1)}, f32[2,1,768]{2,1,0:T(1,128)}, u32[]{:S(2)}) copy-start(f32[2,1,768]{2,1,0:T(1,128)} %get-tuple-element.86) | copy-start | bytes 18436
  505.7 31.1 %copy-start.3 = (f32[2,3,768]{2,1,0:T(4,128)S(1)}, f32[2,3,768]{2,1,0:T(4,128)}, u32[]{:S(2)}) copy-start(f32[2,3,768]{2,1,0:T(4,128)} %get-tuple-element.85) | copy-start | bytes 55300
  505.7 31.1 %copy-start.2 = (f32[2,3,768]{2,1,0:T(4,128)S(1)}, f32[2,3,768]{2,1,0:T(4,128)}, u32[]{:S(2)}) copy-start(f32[2,3,768]{2,1,0:T(4,128)} %get-tuple-element.87) | copy-start | bytes 55300

commit v3 on v2

--- a/solution.py
+++ b/solution.py
@@ -1064,6 +1064,67 @@
     pl.semaphore_wait(barrier, devices - 1)
 
 
+class Trade:
+    def __init__(self, source, target, own_sem, send_sem, recv_sem, plan, inner, senders, receivers):
+        self.source, self.target, self.own_sem = source, target, own_sem
+        self.send_sem, self.recv_sem = send_sem, recv_sem
+        self.devices, self.inner = plan.devices, inner
+        self.senders, self.receivers = senders, receivers
+        self.me = lax.axis_index("dp") * inner + lax.axis_index("fsdp")
+        self.many = len(source.shape) == 3
+
+    def piece(self, target):
+        return self.source.at[target] if self.many else self.source
+
+    def copy(self, source, target):
+        return pltpu.make_async_remote_copy(
+            src_ref=self.piece(target),
+            dst_ref=self.target.at[source],
+            send_sem=self.send_sem.at[target],
+            recv_sem=self.recv_sem.at[source],
+            device_id=(target // self.inner, target % self.inner),
+            device_id_type=MESH,
+        )
+
+    def own(self):
+        return pltpu.make_async_copy(
+            self.piece(self.me), self.target.at[self.me], self.own_sem
+        )
+
+    def each(self, act):
+        def body(i, _):
+            act((self.me + i) % self.devices)
+            return 0
+
+        lax.fori_loop(1, self.devices, body, 0)
+
+    def both(self):
+        return (self.me < self.senders) & (self.me < self.receivers)
+
+    def start(self):
+        pl.when(self.both())(lambda: self.own().start())
+
+        def act(other):
+            ok = (self.me < self.senders) & (other < self.receivers)
+            pl.when(ok)(lambda: self.copy(self.me, other).start())
+
+        self.each(act)
+
+    def wait(self):
+        pl.when(self.both())(lambda: self.own().wait())
+
+        def landed(other):
+            ok = (other < self.senders) & (self.me < self.receivers)
+            pl.when(ok)(lambda: self.copy(other, other).wait_recv())
+
+        def gone(other):
+            ok = (self.me < self.senders) & (other < self.receivers)
+            pl.when(ok)(lambda: self.copy(self.me, other).wait_send())
+
+        self.each(landed)
+        self.each(gone)
+
+
 def when_all(conditions):
     total = None
     for condition in conditions:
@@ -1079,25 +1140,25 @@
         pl.when(condition)(body)
 
 
-def gather_kernel(
-    slot_ref, out_ref, own_sem, lend_send, lend_recv, send_sem, recv_sem, *, plan, inner
+def start_kernel(
+    cond_ref, slot_ref, all_ref, own_ref, own_sem, lend_send, lend_recv, send_sem, recv_sem,
+    *, plan, inner
 ):
-    dp, fs, y, x, z, c = place_of()
+    dp, fs, _, _, _, _ = place_of()
     me = dp * inner + fs
     lead, lent, kept = plan.lead, plan.lent, plan.kept
-    levels = inner // 2
     meet_all(me, plan.devices, inner)
 
     def own_copy():
         start = pl.multiple_of(jnp.where(me == lead, plan.base, 0), TILE)
         return pltpu.make_async_copy(
-            slot_ref.at[pl.ds(start, plan.chunk)], out_ref.at[me], own_sem
+            slot_ref.at[pl.ds(start, plan.chunk)], own_ref, own_sem.at[0]
         )
 
     def lend(slot, target, part):
         return pltpu.make_async_remote_copy(
             src_ref=slot_ref.at[pl.ds(kept, lent)],
-            dst_ref=out_ref.at[target, pl.ds(pl.multiple_of(part * lent, TILE), lent)],
+            dst_ref=own_ref.at[pl.ds(pl.multiple_of(part * lent, TILE), lent)],
             send_sem=lend_send.at[slot],
             recv_sem=lend_recv.at[part],
             device_id=(target // inner, target % inner),
@@ -1118,12 +1179,65 @@
     @pl.when(me >= lead)
     def _():
         own_copy().start()
+
+    trade = Trade(
+        cond_ref, all_ref, own_sem.at[1], send_sem, recv_sem, plan, inner, plan.devices, plan.devices
+    )
+    trade.start()
+    trade.wait()
+
+    @pl.when(me >= lead)
+    def _():
         own_copy().wait()
+        lend(0, lead - 1, 0).wait_send()
+
+    @pl.when(me == lead)
+    def _():
+        lend(1, lead - 1, 1).wait_send()
 
     @pl.when(me < lead)
     def _():
         lend(0, lead - 1, 0).wait_recv()
         lend(0, lead - 1, 1).wait_recv()
+
+
+def start_chunks(condition, slot, plan, inner, collective):
+    anywhere = pl.BlockSpec(memory_space=pl.ANY)
+    dma = pltpu.SemaphoreType.DMA
+    return pl.pallas_call(
+        functools.partial(start_kernel, plan=plan, inner=inner),
+        in_specs=[anywhere] * 2,
+        out_specs=[anywhere] * 2,
+        out_shape=[
+            jax.ShapeDtypeStruct((plan.devices, *condition.shape), condition.dtype),
+            jax.ShapeDtypeStruct((plan.chunk, LANE), BF),
+        ],
+        scratch_shapes=[
+            dma((2,)),
+            dma((2,)),
+            dma((2,)),
+            dma((plan.devices,)),
+            dma((plan.devices,)),
+        ],
+        compiler_params=pltpu.CompilerParams(collective_id=collective, has_side_effects=True),
+        name="start_chunks",
+    )(condition, slot)
+
+
+def gather_kernel(
+    chunk_ref, slab_ref, out_ref, parts_ref, own_sem, slab_send, slab_recv, send_sem, recv_sem,
+    *, plan, inner
+):
+    dp, fs, y, x, z, c = place_of()
+    me = dp * inner + fs
+    lent = plan.lent
+    levels = inner // 2
+    meet_all(me, plan.devices, inner)
+    own = pltpu.make_async_copy(chunk_ref, out_ref.at[me], own_sem.at[0])
+    own.start()
+    trade = Trade(
+        slab_ref, parts_ref, own_sem.at[1], slab_send, slab_recv, plan, inner, plan.lead + 1, plan.devices
+    )
 
     across = {
         "up": (dp, fs + 2),
@@ -1135,13 +1249,13 @@
     kinds = tuple(across)
     pending = []
 
-    def copy(kind, yy, xx, zz, part, cc=None):
+    def copy(kind, yy, xx, zz, part, cc=None, mine=False):
         core = c if cc is None else cc
         column = yy * 2 + xx
         index = column * inner + zz * 2 + core
         rows = pl.ds(part * lent, lent)
         return pltpu.make_async_remote_copy(
-            src_ref=out_ref.at[index, rows],
+            src_ref=chunk_ref.at[rows] if mine else out_ref.at[index, rows],
             dst_ref=out_ref.at[index, rows],
             send_sem=send_sem.at[kinds.index(kind), column * levels + zz, part],
             recv_sem=recv_sem.at[index, part],
@@ -1149,8 +1263,8 @@
             device_id_type=MESH,
         )
 
-    def send(condition, kind, yy, xx, zz, part):
-        guarded(condition, lambda: copy(kind, yy, xx, zz, part).start())
+    def send(condition, kind, yy, xx, zz, part, mine=False):
+        guarded(condition, lambda: copy(kind, yy, xx, zz, part, mine=mine).start())
         pending.append((condition, kind, yy, xx, zz, part))
 
     def arrive(condition, yy, xx, zz, part):
@@ -1171,12 +1285,14 @@
                     if turn:
                         arrive(inside, y, x, zz, part)
                     if sign <= 0:
-                        send(when_all([inside, z < levels - 1]), "up", y, x, zz, part)
+                        send(when_all([inside, z < levels - 1]), "up", y, x, zz, part, turn == 0)
                     if sign >= 0:
-                        send(when_all([inside, z > 0]), "down", y, x, zz, part)
+                        send(when_all([inside, z > 0]), "down", y, x, zz, part, turn == 0)
                     for kind in ("x", "y") if part else ("y", "x"):
-                        send(inside, kind, y, x, zz, part)
-                    send(inside, "twin", y, x, zz, part)
+                        send(inside, kind, y, x, zz, part, turn == 0)
+                    send(inside, "twin", y, x, zz, part, turn == 0)
+            if turn == 0:
+                trade.start()
         if 1 <= turn <= levels:
             for zz, sign, inside in spread(turn - 1):
                 arrive(inside, y, 1 - x, zz, 0)
@@ -1204,39 +1320,38 @@
     lax.fori_loop(0, 4 * levels, twin_arrivals, 0)
     for condition, kind, yy, xx, zz, part in pending:
         guarded(condition, lambda: copy(kind, yy, xx, zz, part).wait_send())
-
-    @pl.when(me >= lead)
-    def _():
-        lend(0, lead - 1, 0).wait_send()
-
-    @pl.when(me == lead)
-    def _():
-        lend(1, lead - 1, 1).wait_send()
-
-
-def gather_chunks(slot, plan, inner, collective):
+    trade.wait()
+    own.wait()
+
+
+def gather_chunks(chunk, slabs, plan, inner, collective):
     anywhere = pl.BlockSpec(memory_space=pl.ANY)
     dma = pltpu.SemaphoreType.DMA
     return pl.pallas_call(
         functools.partial(gather_kernel, plan=plan, inner=inner),
-        in_specs=[anywhere],
-        out_specs=anywhere,
-        out_shape=jax.ShapeDtypeStruct((plan.devices, plan.chunk, LANE), BF),
+        in_specs=[anywhere] * 2,
+        out_specs=[anywhere] * 2,
+        out_shape=[
+            jax.ShapeDtypeStruct((plan.devices, plan.chunk, LANE), BF),
+            jax.ShapeDtypeStruct((plan.lead + 1, *slabs.shape[1:]), slabs.dtype),
+        ],
         scratch_shapes=[
-            dma,
             dma((2,)),
-            dma((2,)),
+            dma((plan.devices,)),
+            dma((plan.devices,)),
             dma((5, plan.devices // 2, 2)),
             dma((plan.devices, 2)),
         ],
         compiler_params=pltpu.CompilerParams(collective_id=collective, has_side_effects=True),
         name="gather_chunks",
-    )(slot)
+    )(chunk, slabs)
 
 
 def scatter_kernel(
     g_ref,
+    rows_ref,
     out_ref,
+    all_ref,
     acc,
     twin,
     wide_y,
@@ -1256,6 +1371,8 @@
     own_sem,
     back_send,
     back_recv,
+    row_send,
+    row_recv,
     *,
     plan,
     inner,
@@ -1335,9 +1452,7 @@
         def body(i, _):
             at = pl.multiple_of(i * ROWS, TILE)
             to = pl.ds(pl.multiple_of(first + i * ROWS, TILE), ROWS)
-            acc[slot, to] = (
-                acc[slot, to].astype(F32) + source[pl.ds(at, ROWS)].astype(F32)
-            ).astype(BF)
+            acc[slot, to] = acc[slot, to] + source[pl.ds(at, ROWS)]
             return 0
 
         lax.fori_loop(0, count // ROWS, body, 0)
@@ -1358,6 +1473,10 @@
             return 0
 
         lax.fori_loop(0, levels, begin, 0)
+
+    trade = Trade(
+        rows_ref, all_ref, own_sem.at[1], row_send, row_recv, plan, inner, plan.devices, lead + 1
+    )
 
     def settle(yy, xx, zz):
         slot = slot_of(yy, xx, zz)
@@ -1365,22 +1484,20 @@
         to_twin(yy, xx, zz).wait_recv()
         add(slot, 0, plan.chunk, twin.at[slot])
 
-    def diagonal(k, _):
+    def diagonal(k):
         zz = level(k)
         settle(1 - y, 1 - x, zz)
         wide(0, 1 - x, zz, 1 - y, 1 - x).start()
         wide(1, 1 - y, zz, 1 - y, 1 - x).start()
-        return 0
-
-    def sides(k, _):
+
+    def sides(k):
         zz = level(k)
         settle(1 - y, x, zz)
         wide(0, x, zz, 1 - y, x).start()
         settle(y, 1 - x, zz)
         wide(1, y, zz, y, 1 - x).start()
-        return 0
-
-    def middle(k, _):
+
+    def middle(k):
         zz = level(k)
         wide(0, 1 - x, zz).wait_recv()
         add_part(slot_of(y, 1 - x, zz), 0, wide_y.at[(1 - x) * levels + zz])
@@ -1388,9 +1505,8 @@
         wide(1, 1 - y, zz).wait_recv()
         add_part(slot_of(1 - y, x, zz), 1, wide_x.at[(1 - y) * levels + zz])
         slim(1, zz, 1 - y, x).start()
-        return 0
-
-    def home(k, _):
+
+    def home(k):
         zz = level(k)
         slot = slot_of(y, x, zz)
         settle(y, x, zz)
@@ -1398,15 +1514,6 @@
         add_part(slot, 0, wide_y.at[x * levels + zz])
         wide(1, y, zz).wait_recv()
         add_part(slot, 1, wide_x.at[y * levels + zz])
-        return 0
-
-    lax.fori_loop(0, levels, diagonal, 0)
-    lax.fori_loop(0, levels, sides, 0)
-    lax.fori_loop(0, levels, middle, 0)
-    lax.fori_loop(0, levels, home, 0)
-
-    def column_sum_of(zz):
-        slot = slot_of(y, x, zz)
         slim(0, zz).wait_recv()
         add_part(slot, 0, slim_x.at[zz])
         slim(1, zz).wait_recv()
@@ -1416,16 +1523,17 @@
         along(upward, zz, part).wait_recv()
         add_part(slot_of(y, x, zz), part, line.at[0 if upward else 1, zz, part])
 
+    edge = (z == 0) | (z == levels - 1)
     sent = []
-    for distance in range(levels - 1, 0, -1):
+
+    def pass_on(k, allowed):
+        zz = level(k)
         for upward in (True, False):
-            zz = z + distance if upward else z - distance
-            inside = zz < levels if upward else zz >= 0
+            inside = allowed & (zz > z if upward else zz < z)
             more = z > 0 if upward else z < levels - 1
 
             @pl.when(inside)
-            def _(upward=upward, zz=zz, more=more):
-                column_sum_of(zz)
+            def _(upward=upward, more=more):
                 for part in range(2):
 
                     @pl.when(more)
@@ -1435,7 +1543,28 @@
                     along(upward, zz, part).start()
 
             sent.append((inside, upward, zz))
-    column_sum_of(z)
+
+    def once(k):
+        diagonal(k)
+        sides(k)
+
+    once(0)
+    once(1)
+    middle(0)
+    once(2)
+    middle(1)
+    home(0)
+    pass_on(0, edge)
+    once(3)
+    middle(2)
+    middle(3)
+    trade.start()
+    home(1)
+    pass_on(1, z >= 0)
+    home(2)
+    pass_on(2, z >= 0)
+    pass_on(0, jnp.logical_not(edge))
+    home(3)
     for part in range(2):
 
         @pl.when(z > 0)
@@ -1470,7 +1599,7 @@
     def _():
         count = kept - plan.base
         copy = pltpu.make_async_copy(
-            acc.at[mine, pl.ds(0, count)], out_ref.at[pl.ds(plan.base, count)], own_sem
+            acc.at[mine, pl.ds(0, count)], out_ref.at[pl.ds(plan.base, count)], own_sem.at[0]
         )
         copy.start()
         copy.wait()
@@ -1478,7 +1607,7 @@
     @pl.when(me > lead)
     def _():
         copy = pltpu.make_async_copy(
-            acc.at[mine, pl.ds(0, kept)], out_ref.at[pl.ds(0, kept)], own_sem
+            acc.at[mine, pl.ds(0, kept)], out_ref.at[pl.ds(0, kept)], own_sem.at[0]
         )
         copy.start()
         copy.wait()
@@ -1516,17 +1645,22 @@
     def _():
         back(1, 1, 0).wait_send()
 
-
-def scatter_chunks(grads, plan, inner, collective):
+    trade.wait()
+
+
+def scatter_chunks(grads, rows, plan, inner, collective):
     anywhere = pl.BlockSpec(memory_space=pl.ANY)
     dma = pltpu.SemaphoreType.DMA
     half, levels = plan.devices // 2, inner // 2
     part = (plan.lent, LANE)
     return pl.pallas_call(
         functools.partial(scatter_kernel, plan=plan, inner=inner),
-        in_specs=[anywhere],
-        out_specs=anywhere,
-        out_shape=jax.ShapeDtypeStruct((plan.padded, LANE), BF),
+        in_specs=[anywhere] * 2,
+        out_specs=[anywhere] * 2,
+        out_shape=[
+            jax.ShapeDtypeStruct((plan.padded, LANE), BF),
+            jax.ShapeDtypeStruct((plan.devices, *rows.shape), rows.dtype),
+        ],
         scratch_shapes=[
             pltpu.VMEM((half, plan.chunk, LANE), BF),
             pltpu.VMEM((half, plan.chunk, LANE), BF),
@@ -1544,69 +1678,38 @@
             dma((2, levels)),
             dma((2, levels, 2)),
             dma((2, levels, 2)),
-            dma,
+            dma((2,)),
             dma((2,)),
             dma,
+            dma((plan.devices,)),
+            dma((plan.devices,)),
         ],
         compiler_params=pltpu.CompilerParams(
             collective_id=collective, has_side_effects=True, vmem_limit_bytes=VMEM_LIMIT
         ),
         name="scatter_chunks",
-    )(grads)
-
-
-def exchange_kernel(in_ref, out_ref, own_sem, send_sem, recv_sem, *, devices, inner, senders, receivers):
+    )(grads, rows)
+
+
+def exchange_kernel(in_ref, out_ref, own_sem, send_sem, recv_sem, *, plan, inner):
     me = lax.axis_index("dp") * inner + lax.axis_index("fsdp")
-    meet_all(me, devices, inner)
-    many = len(in_ref.shape) == 3
-
-    def copy(source, target):
-        return pltpu.make_async_remote_copy(
-            src_ref=in_ref.at[target] if many else in_ref,
-            dst_ref=out_ref.at[source],
-            send_sem=send_sem.at[target],
-            recv_sem=recv_sem.at[source],
-            device_id=(target // inner, target % inner),
-            device_id_type=MESH,
-        )
-
-    def each(i, _, act):
-        other = (me + i) % devices
-        act(other)
-        return 0
-
-    def start(other):
-        pl.when((me < senders) & (other < receivers))(lambda: copy(me, other).start())
-
-    def landed(other):
-        pl.when((other < senders) & (me < receivers))(lambda: copy(other, other).wait_recv())
-
-    def gone(other):
-        pl.when((me < senders) & (other < receivers))(lambda: copy(me, other).wait_send())
-
-    lax.fori_loop(1, devices, functools.partial(each, act=start), 0)
-
-    @pl.when((me < senders) & (me < receivers))
-    def _():
-        own = pltpu.make_async_copy(in_ref.at[me] if many else in_ref, out_ref.at[me], own_sem)
-        own.start()
-        own.wait()
-
-    lax.fori_loop(1, devices, functools.partial(each, act=landed), 0)
-    lax.fori_loop(1, devices, functools.partial(each, act=gone), 0)
-
-
-def exchange(value, devices, inner, senders, receivers, collective, name):
+    meet_all(me, plan.devices, inner)
+    trade = Trade(
+        in_ref, out_ref, own_sem, send_sem, recv_sem, plan, inner, plan.devices, plan.devices
+    )
+    trade.start()
+    trade.wait()
+
+
+def exchange(value, plan, inner, collective, name):
     anywhere = pl.BlockSpec(memory_space=pl.ANY)
     dma = pltpu.SemaphoreType.DMA
     return pl.pallas_call(
-        functools.partial(
-            exchange_kernel, devices=devices, inner=inner, senders=senders, receivers=receivers
-        ),
+        functools.partial(exchange_kernel, plan=plan, inner=inner),
         in_specs=[anywhere],
         out_specs=anywhere,
-        out_shape=jax.ShapeDtypeStruct((senders, *value.shape[-2:]), value.dtype),
-        scratch_shapes=[dma, dma((devices,)), dma((devices,))],
+        out_shape=jax.ShapeDtypeStruct((plan.devices, *value.shape), value.dtype),
+        scratch_shapes=[dma, dma((plan.devices,)), dma((plan.devices,))],
         compiler_params=pltpu.CompilerParams(collective_id=collective, has_side_effects=True),
         name=name,
     )(value)
@@ -1643,7 +1746,7 @@
                 ]
             return 0
 
-        lax.fori_loop(0, HALF, body, 0)
+        lax.fori_loop(0, HALF, body, 0, unroll=True)
 
 
 def ada_partial(lin, cond, plan, inner):
@@ -1675,7 +1778,7 @@
 
         @pl.when(border > 0)
         def _(body=body):
-            lax.fori_loop(0, HALF, body, 0)
+            lax.fori_loop(0, HALF, body, 0, unroll=True)
 
     rows = 64
 
@@ -1716,20 +1819,21 @@
     inner = lax.axis_size("fsdp")
     devices = inner * lax.axis_size("dp")
     plan = Plan(devices, share // LANE)
-    lead = plan.lead
     indices = tuple(range(2, 13))
 
-    condition = jax.nn.silu(embed(timesteps)).astype(BF).astype(F32)
-    conditions = exchange(
-        jnp.pad(condition, ((0, 8 - clips), (0, 0))),
-        devices,
+    rows = master.reshape(plan.share, LANE)
+    lin = jnp.pad(rows, ((0, 2 * HALF * TALL - plan.share), (0, 0)))
+    steps, chunk = start_chunks(
+        jnp.broadcast_to(
+            jnp.pad(timesteps.astype(F32), (0, 8 - clips))[:, None], (8, LANE)
+        ),
+        lin[: plan.padded].astype(BF),
+        plan,
         inner,
-        devices,
-        devices,
         1,
-        "conditions",
-    )
-    columns = conditions[:, :clips].transpose(2, 1, 0).reshape(width, clips * devices)
+    )
+    steps = steps[:, :clips, 0].T.reshape(devices * clips)
+    columns = jax.nn.silu(embed(steps)).astype(BF).astype(F32).T
     columns = jnp.concatenate(
         [
             columns,
@@ -1738,28 +1842,22 @@
         ],
         axis=0,
     )
-    rows = master.reshape(plan.share, LANE)
-    lin = jnp.pad(rows, ((0, 2 * HALF * TALL - plan.share), (0, 0)))
     slabs = ada_partial(lin, columns, plan, inner).reshape(devices, SLAB, LANE)
-    parts = exchange(slabs, devices, inner, lead + 1, devices, 2, "modulation")
+    gathered, parts = gather_chunks(chunk, slabs, plan, inner, 2)
     mod = jnp.sum(parts, axis=0)[: 54 * clips].reshape(clips, 9, width)
-
-    slot = lin[: plan.padded].astype(BF)
-    gathered = gather_chunks(slot, plan, inner, 3)
     weights = unpack_weights(gathered, plan, indices)
     output, input_grad, grad_mod, gradients = block_pass(
         latents, captions, lengths, cotangent, mod, weights
     )
     grad_rows = jnp.pad(
-        grad_mod.astype(F32).reshape(54 * clips, LANE), ((0, SLAB - 54 * clips), (0, 0))
-    )
-    dmod = exchange(grad_rows, devices, inner, devices, lead + 1, 4, "modulation_grads")
+        grad_mod.reshape(54 * clips, LANE), ((0, SLAB - 54 * clips), (0, 0))
+    )
     chunks = pack_grads(gradients, plan, indices)
-    rest = scatter_chunks(chunks, plan, inner, 5)
+    rest, dmod = scatter_chunks(chunks, grad_rows, plan, inner, 3)
     grads, squares = own_grad(
-        columns, dmod.reshape(devices * SLAB, LANE), rest, plan, inner
-    )
-    squares = exchange(squares, devices, inner, devices, devices, 6, "squares")
+        columns, dmod.reshape(devices * SLAB, LANE).astype(F32), rest, plan, inner
+    )
+    squares = exchange(squares, plan, inner, 4, "squares")
     return (
         output,
         input_grad,

time: 758 us -> 675 us (0.89)
  Pallas kernels: 716 us -> 630 us
    pallas_call x4 -> x2, Pallas kernels: 104 us -> 47.7 us  [the longest x1 26.3 us: start_chunks(): pl.pallas_call(functools.partial(start_kernel, plan=plan, inner=inner), i...]
    pallas_call x1, Pallas kernels: 12.6 us -> 3.65 us  [ada_partial(): pl.pallas_call(functools.partial(ada_kernel, plan=plan, inner=inner), out...]
    pallas_call x1, Pallas kernels: 133 us -> 125 us  [scatter_chunks(): pl.pallas_call(functools.partial(scatter_kernel, plan=plan, inner=inner),...]
where the time goes in v3:
time: 675 us; the launch traced here: 666 us
  Pallas kernels  630 us (93%)
  other arithmetic  14.6 us (2%)
  matrix products  9.71 us (1%)
  local copies, waits for them, and re-layouts  8.56 us (1%)
    pallas_call x1, Pallas kernels, scatter_chunks(): pl.pallas_call(functools.partial(scatter_kernel, plan=plan, inner=inner),...  125 us
    pallas_call x1, Pallas kernels, gather_chunks(): pl.pallas_call(functools.partial(gather_kernel, plan=plan, inner=inner),...  110 us
    pallas_call x1, Pallas kernels, feed(): call(functools.partial(feed_kernel, clips=clips, frames=frames, rows=rows...  84.4 us
    pallas_call x2, Pallas kernels, attend_backward(): call(functools.partial(attend_back_kernel, masked=masked), (clips, groups...  75.8 us
    pallas_call x2, Pallas kernels, attend_forward(): call(functools.partial(attend_kernel, masked=masked), (clips, groups), sp...  48.1 us
    pallas_call x1, Pallas kernels, input_back(): call(input_kernel, (clips, frames // rows), [spec] * 5 + [clip_spec(9, wi...  30.3 us
    pallas_call x1, Pallas kernels, start_chunks(): pl.pallas_call(functools.partial(start_kernel, plan=plan, inner=inner), i...  26.3 us
    pallas_call x1, Pallas kernels, before_self(): call(before_self_kernel, (clips, frames // rows), [spec, spec, spec, spec...  24.5 us

profile of v3, /device:TPU:0, one launch (start us, length us, event | category | flops | bytes accessed | tf_op | source)
XLA Modules:
  0.0 666.0 jit_solution(3260413501077390883)
XLA Ops:
  0.6 1.2 copy-done
  3.3 2.5 pad_convert_fusion.slot_ref
  5.8 26.3 %start_chunks.1 = (f32[32,8,128]{2,1,0:T(8,128)}, bf16[2496,128]{1,0:T(8,128)(2,1)}) custom-call(f32[8,128]{1,0:T(8,128)} %broadcast_in_dim.6.cond_ref, bf16[3712,128]{1,0:T(8,128)(2,1)} %pad_convert_fusion.slot_ref), custom_call_target="tpu_custom_call" | custom-call | tf_op jit(solution)/shard_map/start_chunks/pallas_call | solution.py:1207
  32.1 0.9 slice.22
  33.2 0.8 multiply_cosine_fusion
  34.1 1.1 maximum_maximum_fusion.cond_ref
  35.2 1.4 pad.13.lin_ref
  36.6 3.6 ada_partial.1
  40.2 109.8 %gather_chunks.1 = (bf16[32,2496,128]{2,1,0:T(8,128)(2,1)}, f32[12,112,128]{2,1,0:T(8,128)}) custom-call(bf16[2496,128]{1,0:T(8,128)(2,1)} %get-tuple-element.60.chunk_ref, f32[32,112,128]{2,1,0:T(8,128)} %bitcast.39), custom_call_target="tpu_custom_call" | custom-call | tf_op jit(solution)/shard_map/gather_chunks/pallas_call | solution.py:1330
  150.0 1.1 reduce_sum.18
  151.8 16.4 %unpack.1 = (bf16[768,2304]{1,0:T(8,128)(2,1)}, bf16[768,768]{1,0:T(8,128)(2,1)}, f32[1,768]{1,0:T(1,128)}, bf16[768,768]{1,0:T(8,128)(2,1)}, bf16[1024,1536]{1,...) custom-call(bf16[32,2496,128]{2,1,0:T(8,128)(2,1)} %get-tuple-elemen, ...), custom_call_target="tpu_custom_call" | custom-call | tf_op jit(solution)/shard_map/unpack/pallas_call | solution.py:919
  168.2 4.8 convolution_convert_fusion
  173.1 11.7 %qkv_forward.1.refs_0_.refs_1_.refs_2_ = bf16[2,864,2304]{2,1,0:T(8,128)(2,1)} custom-call(bf16[2,864,768]{2,1,0:T(8,128)(2,1)} %x_ref.5, f32[2,9,768]{2,1,0:T(8,128)} %reshape.46.mod_ref, bf16[768,2304]{1,0:T(8,128)(2,1)} %get-tuple-element.64.w_ref), custom_call_target="tpu_custom_call" | custom-call | tf_op jit(solution)/shard_map/qkv_forward/pallas_call | solution.py:160
  184.8 33.8 %self_forward.1 = (bf16[2,864,768]{2,1,0:T(8,128)(2,1)}, f32[2,6,864,128]{3,2,1,0:T(8,128)}) custom-call(bf16[2,864,2304]{2,1,0:T(8,128)(2,1)} %qkv_forward.1.refs_0_.refs_1_.refs_2_, bf16[2,864,2304]{2,1,0:T(8,128)(2,1)} %qkv_forward.1.refs_0_.refs_1_.refs_2_, bf16[2,864,2304]{2,1,0:T(8,128)(2,1)} %qkv_forward.1.refs_0_.refs_1_.refs_2_), custom_call_target="tpu_custom_call" | custom-call | tf_op jit(solution)/shard_map/self_forward/pallas_call | solution.py:232
  218.6 11.1 %after_self.1 = (bf16[2,864,768]{2,1,0:T(8,128)(2,1)}, f32[2,864,768]{2,1,0:T(8,128)}, bf16[2,864,768]{2,1,0:T(8,128)(2,1)}) custom-call(bf16[2,864,768]{2,1,0:T(8,128)(2,1)} %get-tuple-element.65.o_ref.refs_4_, bf16[2,864,768]{2,1,0:T(8,128)(2,1)} %x_ref.5, f32[2,9,768]{2,1,0:T(8,128)} %reshape.46.mod_ref, bf16[768,768]{1,0:T(8,128)(2,1)} %get-tuple-element.66.wo_ref, ...), custom_call_target="tpu_custom_call" | custom-call | tf_op jit(solution)/shard_map/after_self/pallas_call | solution.py:344
  229.8 14.3 %cross_forward.1 = (bf16[2,864,768]{2,1,0:T(8,128)(2,1)}, f32[2,6,864,128]{3,2,1,0:T(8,128)}) custom-call(s32[2]{0:T(128)} %refs_0_.3, bf16[2,864,768]{2,1,0:T(8,128)(2,1)} %get-tuple-element.69.refs_1_, bf16[2,256,1536]{2,1,0:T(8,128)(2,1)} %bitcast.33, bf16[2,256,1536]{2,1,0:T(8,128)(2,1)} %bitcast.34), custom_call_target="tpu_custom_call" | custom-call | tf_op jit(solution)/shard_map/cross_forward/pallas_call | solution.py:232
  244.0 8.7 %after_cross.1 = (bf16[2,864,768]{2,1,0:T(8,128)(2,1)}, f32[2,864,768]{2,1,0:T(8,128)}) custom-call(bf16[2,864,768]{2,1,0:T(8,128)(2,1)} %get-tuple-element.71.o_ref.refs_5_, f32[2,864,768]{2,1,0:T(8,128)} %get-tuple-element.72.h_ref, f32[2,9,768]{2,1,0:T(8,128)} %reshape.46.mod_ref, bf16[768,768]{1,0:T(8,128)(2,1)} %get-tuple-element.73.wo_ref.w_ref, ...), custom_call_target="tpu_custom_call" | custom-call | tf_op jit(solution)/shard_map/after_cross/pallas_call | solution.py:368
  252.7 84.4 %feed.1 = (bf16[2,864,768]{2,1,0:T(8,128)(2,1)}, f32[2,864,768]{2,1,0:T(8,128)}, bf16[768,3072]{1,0:T(8,128)(2,1)}, bf16[3072,768]{1,0:T(8,128)(2,1)}, f32[1,307...) custom-call(f32[2,864,768]{2,1,0:T(8,128)} %get-tuple-element.75.h_ref, bf16[2,864,768]{2,1,0:T(8,128)(2,1)} %dy_ref.1, ...), custom_call_target="tpu_custom_call" | custom-call | tf_op jit(solution)/shard_map/feed/pallas_call | solution.py:513
  337.1 11.9 %before_cross.1 = (bf16[2,864,768]{2,1,0:T(8,128)(2,1)}, bf16[768,768]{1,0:T(8,128)(2,1)}, f32[1,768]{1,0:T(1,128)}, f32[2,1,768]{2,1,0:T(1,128)}) custom-call(f32[2,864,768]{2,1,0:T(8,128)} %get-tuple-element.81.dh_ref, bf16[2,864,768]{2,1,0:T(8,128)(2,1)} %get-tuple-element.82.z_ref, bf16[2,864,768]{2,1,0:T(8,128)(2,1)} %get-tuple-element.71.o_ref.refs_5_, ...), custom_call_target="tpu_custom_call" | custom-call | tf_op jit(solution)/shard_map/before_cross/pallas_call | solution.py:582
  349.1 23.2 %cross_back.1 = (bf16[2,864,768]{2,1,0:T(8,128)(2,1)}, bf16[2,256,768]{2,1,0:T(8,128)(2,1)}, bf16[2,256,768]{2,1,0:T(8,128)(2,1)}) custom-call(s32[2]{0:T(128)} %refs_0_.3, bf16[2,864,768]{2,1,0:T(8,128)(2,1)} %get-tuple-element.69.refs_1_, bf16[2,256,1536]{2,1,0:T(8,128)(2,1)} %bitcast.35, bf16[2,256,1536]{2,1,0:T(8,128)(2,1)} %bitcast.36, ...), custom_call_target="tpu_custom_call" | custom-call | tf_op jit(solution)/shard_map/cross_back/pallas_call | solution.py:315
  372.3 24.5 %before_self.1 = (f32[2,864,768]{2,1,0:T(8,128)}, bf16[2,864,768]{2,1,0:T(8,128)(2,1)}, bf16[768,768]{1,0:T(8,128)(2,1)}, bf16[768,768]{1,0:T(8,128)(2,1)}, f32[1,768]{1,0:T(1,128)}, /*index=5*/f32[2,3,768]{2,1,0:T(4,128)}) custom-call(bf16[2,864,768]{2,1,0:T(8,128)(2,1)} %get-tuple-element.85.dq_ref, f32[2,864,768]{2,1,0:T(8,128)} %get-tuple-element.72.h_ref, ...), custom_call_target="tpu_custom_call" | custom-call | tf_op jit(solution)/shard_map/before_self/pallas_call | solution.py:649
  396.8 52.5 %self_back.1 = (bf16[2,864,768]{2,1,0:T(8,128)(2,1)}, bf16[2,864,768]{2,1,0:T(8,128)(2,1)}, bf16[2,864,768]{2,1,0:T(8,128)(2,1)}) custom-call(bf16[2,864,2304]{2,1,0:T(8,128)(2,1)} %qkv_forward.1.refs_0_.refs_1_.refs_2_, bf16[2,864,2304]{2,1,0:T(8,128)(2,1)} %qkv_forward.1.refs_0_.refs_1_.refs_2_, bf16[2,864,2304]{2,1,0:T(8,128)(2,1)} %qkv_forward.1.refs_0_.refs_1_.refs_2_, ...), custom_call_target="tpu_custom_call" | custom-call | tf_op jit(solution)/shard_map/self_back/pallas_call | solution.py:315
  449.3 30.3 %input_back.1 = (bf16[2,864,768]{2,1,0:T(8,128)(2,1)}, bf16[768,2304]{1,0:T(8,128)(2,1)}, f32[2,2,768]{2,1,0:T(2,128)}) custom-call(bf16[2,864,768]{2,1,0:T(8,128)(2,1)} %get-tuple-element.89.dq_ref, bf16[2,864,768]{2,1,0:T(8,128)(2,1)} %get-tuple-element.90.dk_ref, bf16[2,864,768]{2,1,0:T(8,128)(2,1)} %get-tuple-element.91.dv_ref, ...), custom_call_target="tpu_custom_call" | custom-call | tf_op jit(solution)/shard_map/input_back/pallas_call | solution.py:697
  479.7 0.7 convert.21
  481.3 4.9 fusion.refs_4_
  486.2 15.6 %pack.1.g_ref = bf16[32,2496,128]{2,1,0:T(8,128)(2,1)} custom-call(bf16[768,2304]{1,0:T(8,128)(2,1)} %get-tuple-element.94.refs_0_, bf16[768,768]{1,0:T(8,128)(2,1)} %get-tuple-element.95.refs_1_, f32[1,768]{1,0:T(1,128)} %get-tuple-element.96.refs_2_, bf16[768,768]{1,0:T(8,128)(2,1)} %get-tuple-element.97.refs_3_, bf16[1024,1536]{1,0:T(8,128)(2,1)} %fusion.refs_4_, ...), custom_call_target="tpu_custom_call" | custom-call | tf_op jit(solution)/shard_map/pack/pallas_call | solution.py:1027
  501.8 125.4 %scatter_chunks.1 = (bf16[3712,128]{1,0:T(8,128)(2,1)}, bf16[32,112,128]{2,1,0:T(8,128)(2,1)}) custom-call(bf16[32,2496,128]{2,1,0:T(8,128)(2,1)} %pack.1.g_ref, bf16[112,128]{1,0:T(8,128)(2,1)} %pad.14.rows_ref), custom_call_target="tpu_custom_call" | custom-call | tf_op jit(solution)/shard_map/scatter_chunks/pallas_call | solution.py:1656
  627.2 2.5 bitcast_convert_fusion.1.dmod_ref
  629.7 5.0 own_grad.1
  634.7 21.4 %squares.1 = f32[32,8,128]{2,1,0:T(8,128)} custom-call(f32[8,128]{1,0:T(8,128)} %get-tuple-element.112.in_ref), custom_call_target="tpu_custom_call" | custom-call | tf_op jit(solution)/shard_map/squares/pallas_call | solution.py:1707
  656.1 1.5 reduce_sum.19
  658.4 6.1 multiply_subtract_fusion
  (28 shorter events, 3.3 us)
Async XLA Ops:
  0.6 1.2 copy-start
  5.8 29.3 %copy-start.1 = (f32[473472]{0:T(1024)S(1)}, f32[473472]{0:T(1024)}, u32[]{:S(2)}) copy-start(f32[473472]{0:T(1024)} %param.13) | copy-start | bytes 5681668
  449.3 31.1 %copy-start.4 = (f32[2,1,768]{2,1,0:T(1,128)S(1)}, f32[2,1,768]{2,1,0:T(1,128)}, u32[]{:S(2)}) copy-start(f32[2,1,768]{2,1,0:T(1,128)} %get-tuple-element.108) | copy-start | bytes 18436
  449.3 31.1 %copy-start.3 = (f32[2,3,768]{2,1,0:T(4,128)S(1)}, f32[2,3,768]{2,1,0:T(4,128)}, u32[]{:S(2)}) copy-start(f32[2,3,768]{2,1,0:T(4,128)} %get-tuple-element.107) | copy-start | bytes 55300
  449.3 31.1 %copy-start.2 = (f32[2,3,768]{2,1,0:T(4,128)S(1)}, f32[2,3,768]{2,1,0:T(4,128)}, u32[]{:S(2)}) copy-start(f32[2,3,768]{2,1,0:T(4,128)} %get-tuple-element.109) | copy-start | bytes 55300

commit v4 on v3

--- a/solution.py
+++ b/solution.py
@@ -143,6 +143,18 @@
         ref[...] += value
 
 
+def span_of(rows):
+    start = (pl.program_id(0) * pl.num_programs(1) + pl.program_id(1)) * rows
+    return pl.ds(pl.multiple_of(start, rows), rows)
+
+
+def clear_at(first, *refs):
+    @pl.when(first)
+    def _():
+        for ref in refs:
+            ref[...] = jnp.zeros_like(ref)
+
+
 def column_sum(value):
     return jnp.sum(value, axis=0, keepdims=True)
 
@@ -182,14 +194,30 @@
         len_ref, q_ref, k_ref, v_ref, o_ref, l_ref = refs
     else:
         q_ref, k_ref, v_ref, o_ref, l_ref = refs
-    k, v = k_ref[0], v_ref[0]
-    scaled = q_ref[0] * jnp.asarray(HD**-0.5, BF)
     lane, low = head_lanes()
+    for pair in range(l_ref.shape[1]):
+        columns = slice(pair * 2 * HD, (pair + 1) * 2 * HD)
+        length = len_ref[pl.program_id(0)] if masked else None
+        attend_pair(
+            lane,
+            low,
+            length,
+            q_ref[0, :, columns],
+            k_ref[0, :, columns],
+            v_ref[0, :, columns],
+            o_ref.at[0, :, columns],
+            l_ref.at[0, pair],
+        )
+
+
+def attend_pair(lane, low, length, q, k, v, o_ref, l_ref):
+    masked = length is not None
+    scaled = q * jnp.asarray(HD**-0.5, BF)
     one = jnp.ones((), BF)
     zero = jnp.zeros((), BF)
     values = [jnp.where(low, v, one), jnp.where(low, one, v)]
     if masked:
-        bias = usable_bias(len_ref[pl.program_id(0)], k.shape[0])
+        bias = usable_bias(length, k.shape[0])
         tag = jnp.where(lane % HD == 0, one, zero)
         queries = [jnp.where(low, scaled, tag), jnp.where(low, tag, scaled)]
         keys = [jnp.where(low, k, bias), jnp.where(low, bias, k)]
@@ -203,37 +231,37 @@
         mixes.append(nn(jnp.exp(scores - top).astype(BF), values[head]))
         tops.append(top)
     total = jnp.where(low, mixes[1], mixes[0])
-    l_ref[0, 0] = jnp.where(low, tops[1], tops[0]) + jnp.log(total)
-    o_ref[0] = (jnp.where(low, mixes[0], mixes[1]) / pltpu.roll(total, HD, 1)).astype(BF)
-
-
-def pair_spec(rows, offset):
-    return pl.BlockSpec((1, rows, 2 * HD), lambda i, j: (i, 0, j + offset))
-
-
-def lse_spec(rows):
-    return pl.BlockSpec((1, 1, rows, 2 * HD), lambda i, j: (i, j, 0, 0))
-
-
-def attend_forward(queries, key_offset, pairs, value_offset, lengths, name):
+    l_ref[...] = jnp.where(low, tops[1], tops[0]) + jnp.log(total)
+    o_ref[...] = (jnp.where(low, mixes[0], mixes[1]) / pltpu.roll(total, HD, 1)).astype(BF)
+
+
+def pair_spec(rows, offset, pairs):
+    return pl.BlockSpec((1, rows, 2 * HD * pairs), lambda i, j: (i, 0, j + offset // pairs))
+
+
+def lse_spec(rows, pairs):
+    return pl.BlockSpec((1, pairs, rows, 2 * HD), lambda i, j: (i, j, 0, 0))
+
+
+def attend_forward(queries, key_offset, keyvals, value_offset, lengths, name, pairs=1):
     clips, frames = queries.shape[:2]
-    slots = pairs.shape[1]
+    slots = keyvals.shape[1]
     groups = HEADS // 2
     masked = lengths is not None
     specs = [
-        pair_spec(frames, 0),
-        pair_spec(slots, key_offset),
-        pair_spec(slots, value_offset),
+        pair_spec(frames, 0, pairs),
+        pair_spec(slots, key_offset, pairs),
+        pair_spec(slots, value_offset, pairs),
     ]
-    args = [queries, pairs, pairs]
+    args = [queries, keyvals, keyvals]
     if masked:
         specs.insert(0, pl.BlockSpec(memory_space=pltpu.SMEM))
         args.insert(0, lengths)
     return call(
         functools.partial(attend_kernel, masked=masked),
-        (clips, groups),
+        (clips, groups // pairs),
         specs,
-        [pair_spec(frames, 0), lse_spec(frames)],
+        [pair_spec(frames, 0, pairs), lse_spec(frames, pairs)],
         [struct((clips, frames, D), BF), struct((clips, groups, frames, 2 * HD), F32)],
         name,
     )(*args)
@@ -251,13 +279,33 @@
         len_ref, q_ref, k_ref, v_ref, do_ref, o_ref, l_ref, dq_ref, dk_ref, dv_ref = refs
     else:
         q_ref, k_ref, v_ref, do_ref, o_ref, l_ref, dq_ref, dk_ref, dv_ref = refs
-    k, v, grad = k_ref[0], v_ref[0], do_ref[0]
-    scaled = q_ref[0] * jnp.asarray(HD**-0.5, BF)
     lane, low = head_lanes()
+    for pair in range(l_ref.shape[1]):
+        columns = slice(pair * 2 * HD, (pair + 1) * 2 * HD)
+        length = len_ref[pl.program_id(0)] if masked else None
+        attend_back_pair(
+            lane,
+            low,
+            length,
+            q_ref[0, :, columns],
+            k_ref[0, :, columns],
+            v_ref[0, :, columns],
+            do_ref[0, :, columns],
+            o_ref[0, :, columns],
+            l_ref[0, pair],
+            dq_ref.at[0, :, columns],
+            dk_ref.at[0, :, columns],
+            dv_ref.at[0, :, columns],
+        )
+
+
+def attend_back_pair(lane, low, length, q, k, v, grad, mixed, lse, dq_ref, dk_ref, dv_ref):
+    masked = length is not None
+    scaled = q * jnp.asarray(HD**-0.5, BF)
     spot = lane % HD
     one = jnp.ones((), BF)
     zero = jnp.zeros((), BF)
-    product = grad.astype(F32) * o_ref[0].astype(F32)
+    product = grad.astype(F32) * mixed.astype(F32)
     delta_low = jnp.sum(jnp.where(low, product, 0.0), axis=1, keepdims=True)
     delta_high = jnp.sum(jnp.where(low, 0.0, product), axis=1, keepdims=True)
 
@@ -270,12 +318,12 @@
         )
 
     tag = jnp.where(spot == 3, one, zero) if masked else zero
-    lse_lanes = negated(l_ref[0, 0], tag)
+    lse_lanes = negated(lse, tag)
     delta_lanes = negated(jnp.where(low, delta_high, delta_low), zero)
     ones = jnp.broadcast_to(jnp.where(spot < 3, one, zero), k.shape)
     key_lanes = ones
     if masked:
-        bias = usable_bias(len_ref[pl.program_id(0)], k.shape[0])
+        bias = usable_bias(length, k.shape[0])
         key_lanes = jnp.where(spot == 3, bias, ones)
     transposed = k.astype(F32).T.astype(BF)
     grad_queries, grad_keys, grad_values = [], [], []
@@ -290,33 +338,35 @@
         grad_values.append(nn(probability.astype(BF), grad))
         grad_keys.append(nn(grad_scores, scaled))
         grad_queries.append(nn(transposed[HD * head : HD * (head + 1)], grad_scores))
-    dv_ref[0] = jnp.where(low, grad_values[0], grad_values[1]).astype(BF)
-    dk_ref[0] = jnp.where(low, grad_keys[0], grad_keys[1]).astype(BF)
-    dq_ref[0] = (jnp.concatenate(grad_queries, axis=0).T * HD**-0.5).astype(BF)
-
-
-def attend_backward(queries, key_offset, pairs, value_offset, lengths, grad, mixed, lse, name):
+    dv_ref[...] = jnp.where(low, grad_values[0], grad_values[1]).astype(BF)
+    dk_ref[...] = jnp.where(low, grad_keys[0], grad_keys[1]).astype(BF)
+    dq_ref[...] = (jnp.concatenate(grad_queries, axis=0).T * HD**-0.5).astype(BF)
+
+
+def attend_backward(
+    queries, key_offset, keyvals, value_offset, lengths, grad, mixed, lse, name, pairs=1
+):
     clips, frames = queries.shape[:2]
-    slots = pairs.shape[1]
+    slots = keyvals.shape[1]
     groups = HEADS // 2
     masked = lengths is not None
     specs = [
-        pair_spec(frames, 0),
-        pair_spec(slots, key_offset),
-        pair_spec(slots, value_offset),
-        pair_spec(frames, 0),
-        pair_spec(frames, 0),
-        lse_spec(frames),
+        pair_spec(frames, 0, pairs),
+        pair_spec(slots, key_offset, pairs),
+        pair_spec(slots, value_offset, pairs),
+        pair_spec(frames, 0, pairs),
+        pair_spec(frames, 0, pairs),
+        lse_spec(frames, pairs),
     ]
-    args = [queries, pairs, pairs, grad, mixed, lse]
+    args = [queries, keyvals, keyvals, grad, mixed, lse]
     if masked:
         specs.insert(0, pl.BlockSpec(memory_space=pltpu.SMEM))
         args.insert(0, lengths)
     return call(
         functools.partial(attend_back_kernel, masked=masked),
-        (clips, groups),
+        (clips, groups // pairs),
         specs,
-        [pair_spec(frames, 0), pair_spec(slots, 0), pair_spec(slots, 0)],
+        [pair_spec(frames, 0, pairs), pair_spec(slots, 0, pairs), pair_spec(slots, 0, pairs)],
         [
             struct((clips, frames, D), BF),
             struct((clips, slots, D), BF),
@@ -404,6 +454,8 @@
     dz_s,
     dzt_s,
     z_s,
+    act_s,
+    du_s,
     *,
     clips,
     frames,
@@ -430,43 +482,29 @@
         ddownb_ref[...] = bias_sum
         int_s[...] = in_s[...].T
         dzt_s[...] = dz_s[...].T
+        z_s[...] = jnp.zeros_like(z_s)
+        dh_ref[...] = jnp.zeros_like(dh_ref)
 
     up, down = up_ref[...], down_ref[...]
-    grad_up = grad_down = grad_bias = None
     for clip, start, at in spans:
         here = pl.ds(at, rows)
         hidden = nn(in_s[here], up) + upb_ref[...]
         square = hidden * hidden
-        tanh = jnp.tanh(GELU_ROOT * hidden * (1.0 + 0.044715 * square))
+        tanh = jnp.tanh(hidden * (GELU_ROOT + (GELU_ROOT * 0.044715) * square))
         half = 0.5 + 0.5 * tanh
-        activated = (hidden * half).astype(BF)
-        slope = half + hidden * half * (1.0 - tanh) * (
-            GELU_ROOT * (1.0 + 3 * 0.044715 * square)
+        lifted = hidden * half
+        activated = lifted.astype(BF)
+        slope = half + lifted * (1.0 - tanh) * (
+            GELU_ROOT + (GELU_ROOT * 3 * 0.044715) * square
         )
-        dz = dz_s[here]
-        grad_hidden = (nt(dz, down) * slope).astype(BF)
-        branch = nn(activated, down)
-        grad_in = nt(grad_hidden, up)
-
-        @pl.when(step == 0)
-        def _(branch=branch, grad_in=grad_in, here=here, clip=clip, start=start):
-            z_s[here] = branch
-            dh_ref[clip, start : start + rows] = grad_in
-
-        @pl.when(step > 0)
-        def _(branch=branch, grad_in=grad_in, here=here, clip=clip, start=start):
-            z_s[here] += branch
-            dh_ref[clip, start : start + rows] += grad_in
-
-        one_up = nn(int_s[:, at : at + rows], grad_hidden)
-        one_down = nn(dzt_s[:, at : at + rows], activated)
-        one_bias = column_sum(grad_hidden.astype(F32))
-        grad_up = one_up if grad_up is None else grad_up + one_up
-        grad_down = one_down if grad_down is None else grad_down + one_down
-        grad_bias = one_bias if grad_bias is None else grad_bias + one_bias
-    dup_ref[...] = grad_up.astype(BF)
-    ddown_ref[...] = grad_down.T.astype(BF)
-    dupb_ref[...] = grad_bias
+        grad_hidden = (nt(dz_s[here], down) * slope).astype(BF)
+        z_s[here] += nn(activated, down)
+        dh_ref[clip, start : start + rows] += nt(grad_hidden, up)
+        act_s[here] = activated
+        du_s[here] = grad_hidden
+    dup_ref[...] = nn(int_s[...], du_s[...]).astype(BF)
+    ddown_ref[...] = nn(dzt_s[...], act_s[...]).T.astype(BF)
+    dupb_ref[...] = column_sum(du_s[...].astype(F32))
 
     @pl.when(step == last)
     def _():
@@ -494,7 +532,7 @@
                 sums_ref[clip, index : index + 1] = sums[index]
 
 
-def feed(hidden, cotangent, mod, up, up_bias, down, down_bias, block=512):
+def feed(hidden, cotangent, mod, up, up_bias, down, down_bias, block=768):
     clips, frames, width = hidden.shape
     inner = up.shape[1]
     rows = row_block(frames)
@@ -547,6 +585,8 @@
             pltpu.VMEM((tokens, width), BF),
             pltpu.VMEM((width, tokens), BF),
             pltpu.VMEM((tokens, width), F32),
+            pltpu.VMEM((tokens, block), BF),
+            pltpu.VMEM((tokens, block), BF),
         ],
     )(hidden, cotangent, mod, up, up_bias, down, down_bias)
 
@@ -559,19 +599,23 @@
 
 
 def before_cross_kernel(
-    dh_ref, z_ref, o_ref, mod_ref, w_ref, do_ref, dw_ref, db_ref, sums_ref, dw_s
+    dh_ref, z_ref, o_ref, mod_ref, w_ref, do_ref, dw_ref, db_ref, sums_ref, ot_s, dz_s
 ):
     new_clip, first, last = ends()
+    clear_at(new_clip, sums_ref)
+    clear_at(first, db_ref)
     dh = dh_ref[0]
+    here = span_of(dh.shape[0])
     dz = (mod_ref[0, 5:6] * dh).astype(BF)
-    add_to(sums_ref, new_clip, column_sum(dh * z_ref[0].astype(F32))[None])
-    add_to(db_ref, first, column_sum(dz.astype(F32)))
+    dz_s[here] = dz
+    ot_s[here] = o_ref[0]
+    sums_ref[0] += column_sum(dh * z_ref[0].astype(F32))
+    db_ref[...] += column_sum(dz.astype(F32))
     do_ref[0] = nt(dz, w_ref[...]).astype(BF)
-    add_to(dw_s, first, tn(o_ref[0], dz))
 
     @pl.when(last)
     def _():
-        dw_ref[...] = dw_s[...].astype(BF)
+        dw_ref[...] = tn(ot_s[...], dz_s[...]).astype(BF)
 
 
 def before_cross(dh, branch, mixed, mod, weight):
@@ -591,7 +635,7 @@
             struct((clips, 1, width), F32),
         ],
         "before_cross",
-        [pltpu.VMEM((width, width), F32)],
+        [pltpu.VMEM((clips * frames, width), BF)] * 2,
     )(dh, branch, mixed, mod, weight)
 
 
@@ -610,19 +654,26 @@
     dwo_ref,
     db_ref,
     sums_ref,
-    dwq_s,
-    dwo_s,
+    in_s,
+    dq_s,
+    o_s,
+    dz_s,
 ):
     new_clip, first, last = ends()
+    clear_at(new_clip, sums_ref)
+    clear_at(first, db_ref)
+    here = span_of(dq_ref.shape[1])
     normed, inverse = normalize(h_ref[0])
-    second_in = (normed * (1.0 + mod_ref[0, 4:5]) + mod_ref[0, 3:4]).astype(BF)
+    in_s[here] = (normed * (1.0 + mod_ref[0, 4:5]) + mod_ref[0, 3:4]).astype(BF)
     grad_query = dq_ref[0]
-    add_to(dwq_s, first, tn(second_in, grad_query))
+    dq_s[here] = grad_query
+    o_s[here] = o_ref[0]
     grad_in = nt(grad_query, wq_ref[...])
     dh = dh_ref[0] + norm_back(normed, inverse, grad_in * (1.0 + mod_ref[0, 4:5]))
     out_ref[0] = dh
     dz = (mod_ref[0, 2:3] * dh).astype(BF)
-    sums = jnp.concatenate(
+    dz_s[here] = dz
+    sums_ref[0] += jnp.concatenate(
         [
             column_sum(grad_in),
             column_sum(grad_in * normed),
@@ -630,15 +681,13 @@
         ],
         axis=0,
     )
-    add_to(sums_ref, new_clip, sums[None])
-    add_to(db_ref, first, column_sum(dz.astype(F32)))
+    db_ref[...] += column_sum(dz.astype(F32))
     do_ref[0] = nt(dz, wo_ref[...]).astype(BF)
-    add_to(dwo_s, first, tn(o_ref[0], dz))
 
     @pl.when(last)
     def _():
-        dwq_ref[...] = dwq_s[...].astype(BF)
-        dwo_ref[...] = dwo_s[...].astype(BF)
+        dwq_ref[...] = tn(in_s[...], dq_s[...]).astype(BF)
+        dwo_ref[...] = tn(o_s[...], dz_s[...]).astype(BF)
 
 
 def before_self(grad_query, hidden, dh, branch, mixed, mod, query_weight, weight):
@@ -660,34 +709,39 @@
             struct((clips, 3, width), F32),
         ],
         "before_self",
-        [pltpu.VMEM((width, width), F32), pltpu.VMEM((width, width), F32)],
+        [pltpu.VMEM((clips * frames, width), BF)] * 4,
     )(grad_query, hidden, dh, branch, mixed, mod, query_weight, weight)
 
 
 def input_kernel(
-    dq_ref, dk_ref, dv_ref, x_ref, dh_ref, mod_ref, w_ref, out_ref, dw_ref, sums_ref, dw_s
+    dq_ref, dk_ref, dv_ref, x_ref, dh_ref, mod_ref, w_ref, out_ref, dw_ref, sums_ref, in_s, g_s
 ):
-    new_clip, first, last = ends()
+    new_clip, _, last = ends()
     width = x_ref.shape[2]
+    clear_at(new_clip, sums_ref)
+    here = span_of(x_ref.shape[1])
     normed, inverse = normalize(x_ref[0].astype(F32))
-    first_in = (normed * (1.0 + mod_ref[0, 1:2]) + mod_ref[0, 0:1]).astype(BF)
-    turned = first_in.T
+    in_s[here] = (normed * (1.0 + mod_ref[0, 1:2]) + mod_ref[0, 0:1]).astype(BF)
     grad_in = None
     for index, ref in enumerate((dq_ref, dk_ref, dv_ref)):
         columns = slice(index * width, (index + 1) * width)
         grad = ref[0]
+        g_s[here, columns] = grad
         part = nt(grad, w_ref[:, columns])
         grad_in = part if grad_in is None else grad_in + part
-        add_to(dw_s.at[:, columns], first, nn(turned, grad))
     out_ref[0] = (
         dh_ref[0] + norm_back(normed, inverse, grad_in * (1.0 + mod_ref[0, 1:2]))
     ).astype(BF)
-    sums = jnp.concatenate([column_sum(grad_in), column_sum(grad_in * normed)], axis=0)
-    add_to(sums_ref, new_clip, sums[None])
+    sums_ref[0] += jnp.concatenate(
+        [column_sum(grad_in), column_sum(grad_in * normed)], axis=0
+    )
 
     @pl.when(last)
     def _():
-        dw_ref[...] = dw_s[...].astype(BF)
+        turned = in_s[...].T
+        for index in range(3):
+            columns = slice(index * width, (index + 1) * width)
+            dw_ref[:, columns] = nn(turned, g_s[:, columns]).astype(BF)
 
 
 def input_back(grads, latents, dh, mod, weight):
@@ -705,7 +759,10 @@
             struct((clips, 2, width), F32),
         ],
         "input_back",
-        [pltpu.VMEM(weight.shape, F32)],
+        [
+            pltpu.VMEM((clips * frames, width), BF),
+            pltpu.VMEM((clips * frames, weight.shape[1]), BF),
+        ],
     )(*grads, latents, dh, mod, weight)
 
 
@@ -728,7 +785,7 @@
     groups = HEADS // 2
     caption_flat = captions.reshape(clips * slots, captions.shape[2])
     triple = qkv_forward(latents, mod, triple_weight)
-    mixed_one, lse_one = attend_forward(triple, groups, triple, 2 * groups, None, "self_forward")
+    mixed_one, lse_one = attend_forward(triple, groups, triple, 2 * groups, None, "self_forward", 2)
     branch_one, hidden_one, cross_queries = after_self(
         mixed_one, latents, mod, output_weight, output_bias, cross_query
     )
@@ -746,7 +803,16 @@
         dh_two, branch_two, mixed_two, mod, cross_output
     )
     grad_cq, grad_ck, grad_cv = attend_backward(
-        cross_queries, 0, pairs, groups, lengths, grad_mixed_two, mixed_two, lse_two, "cross_back"
+        cross_queries,
+        0,
+        pairs,
+        groups,
+        lengths,
+        grad_mixed_two,
+        mixed_two,
+        lse_two,
+        "cross_back",
+        2,
     )
     grad_pairs = jnp.concatenate([grad_ck, grad_cv], axis=-1).reshape(clips * slots, 2 * width)
     grad_keyval = jnp.dot(caption_flat.T, grad_pairs, preferred_element_type=F32).astype(BF)
@@ -763,6 +829,7 @@
         mixed_one,
         lse_one,
         "self_back",
+        2,
     )
     input_grad, grad_triple, sums_one = input_back(grads_one, latents, dh_one, mod, triple_weight)
     grad_mod = jnp.concatenate(
@@ -1465,14 +1532,10 @@
 
     columns = ((1 - y, 1 - x), (1 - y, x), (y, 1 - x), (y, x))
 
-    for yy, xx in columns:
-
-        def begin(k, _, yy=yy, xx=xx):
+    for k in range(levels):
+        for yy, xx in columns:
             to_twin(yy, xx, level(k)).start()
             load(yy, xx, level(k)).start()
-            return 0
-
-        lax.fori_loop(0, levels, begin, 0)
 
     trade = Trade(
         rows_ref, all_ref, own_sem.at[1], row_send, row_recv, plan, inner, plan.devices, lead + 1

time: 675 us -> 639 us (0.947)
  Pallas kernels: 630 us -> 596 us
    pallas_call x1, Pallas kernels: 84.4 us -> 71.8 us  [feed(): call(functools.partial(feed_kernel, clips=clips, frames=frames, rows=rows...]
    pallas_call x1, Pallas kernels: 30.3 us -> 22.1 us  [input_back(): call(input_kernel, (clips, frames // rows), [spec] * 5 + [clip_spec(9, wi...]
where the time goes in v4:
time: 639 us; the launch traced here: 632 us
  Pallas kernels  596 us (93%)
  other arithmetic  14.6 us (2%)
  matrix products  9.71 us (2%)
  local copies, waits for them, and re-layouts  8.56 us (1%)
    pallas_call x1, Pallas kernels, scatter_chunks(): pl.pallas_call(functools.partial(scatter_kernel, plan=plan, inner=inner),...  125 us
    pallas_call x1, Pallas kernels, gather_chunks(): pl.pallas_call(functools.partial(gather_kernel, plan=plan, inner=inner),...  110 us
    pallas_call x1, Pallas kernels, feed(): call(functools.partial(feed_kernel, clips=clips, frames=frames, rows=rows...  71.8 us
    pallas_call x2, Pallas kernels, attend_backward(): call(functools.partial(attend_back_kernel, masked=masked), (clips, groups...  71.4 us
    pallas_call x2, Pallas kernels, attend_forward(): call(functools.partial(attend_kernel, masked=masked), (clips, groups // p...  45.2 us
    pallas_call x1, Pallas kernels, start_chunks(): pl.pallas_call(functools.partial(start_kernel, plan=plan, inner=inner), i...  26.3 us
    pallas_call x1, Pallas kernels, input_back(): call(input_kernel, (clips, frames // rows), [spec] * 5 + [clip_spec(9, wi...  22.1 us
    pallas_call x1, Pallas kernels, exchange(): pl.pallas_call(functools.partial(exchange_kernel, plan=plan, inner=inner)...  21.4 us

profile of v4, /device:TPU:0, one launch (start us, length us, event | category | flops | bytes accessed | tf_op | source)
XLA Modules:
  0.0 631.9 jit_solution(13451920481083254768)
XLA Ops:
  0.6 1.2 copy-done
  3.3 2.5 pad_convert_fusion.slot_ref
  5.8 26.3 %start_chunks.1 = (f32[32,8,128]{2,1,0:T(8,128)}, bf16[2496,128]{1,0:T(8,128)(2,1)}) custom-call(f32[8,128]{1,0:T(8,128)} %broadcast_in_dim.6.cond_ref, bf16[3712,128]{1,0:T(8,128)(2,1)} %pad_convert_fusion.slot_ref), custom_call_target="tpu_custom_call" | custom-call | tf_op jit(solution)/shard_map/start_chunks/pallas_call | solution.py:1274
  32.1 0.9 slice.22
  33.2 0.8 multiply_cosine_fusion
  34.1 1.1 maximum_maximum_fusion.cond_ref
  35.2 1.4 pad.13.lin_ref
  36.6 3.6 ada_partial.1
  40.2 109.8 %gather_chunks.1 = (bf16[32,2496,128]{2,1,0:T(8,128)(2,1)}, f32[12,112,128]{2,1,0:T(8,128)}) custom-call(bf16[2496,128]{1,0:T(8,128)(2,1)} %get-tuple-element.60.chunk_ref, f32[32,112,128]{2,1,0:T(8,128)} %bitcast.39), custom_call_target="tpu_custom_call" | custom-call | tf_op jit(solution)/shard_map/gather_chunks/pallas_call | solution.py:1397
  150.0 1.1 reduce_sum.18
  151.8 16.4 %unpack.1 = (bf16[768,2304]{1,0:T(8,128)(2,1)}, bf16[768,768]{1,0:T(8,128)(2,1)}, f32[1,768]{1,0:T(1,128)}, bf16[768,768]{1,0:T(8,128)(2,1)}, bf16[1024,1536]{1,...) custom-call(bf16[32,2496,128]{2,1,0:T(8,128)(2,1)} %get-tuple-elemen, ...), custom_call_target="tpu_custom_call" | custom-call | tf_op jit(solution)/shard_map/unpack/pallas_call | solution.py:986
  168.2 4.8 convolution_convert_fusion
  173.1 11.7 %qkv_forward.1.refs_0_.refs_1_.refs_2_ = bf16[2,864,2304]{2,1,0:T(8,128)(2,1)} custom-call(bf16[2,864,768]{2,1,0:T(8,128)(2,1)} %x_ref.5, f32[2,9,768]{2,1,0:T(8,128)} %reshape.46.mod_ref, bf16[768,2304]{1,0:T(8,128)(2,1)} %get-tuple-element.64.w_ref), custom_call_target="tpu_custom_call" | custom-call | tf_op jit(solution)/shard_map/qkv_forward/pallas_call | solution.py:172
  184.8 30.9 %self_forward.1 = (bf16[2,864,768]{2,1,0:T(8,128)(2,1)}, f32[2,6,864,128]{3,2,1,0:T(8,128)}) custom-call(bf16[2,864,2304]{2,1,0:T(8,128)(2,1)} %qkv_forward.1.refs_0_.refs_1_.refs_2_, bf16[2,864,2304]{2,1,0:T(8,128)(2,1)} %qkv_forward.1.refs_0_.refs_1_.refs_2_, bf16[2,864,2304]{2,1,0:T(8,128)(2,1)} %qkv_forward.1.refs_0_.refs_1_.refs_2_), custom_call_target="tpu_custom_call" | custom-call | tf_op jit(solution)/shard_map/self_forward/pallas_call | solution.py:260
  215.7 10.8 %after_self.1 = (bf16[2,864,768]{2,1,0:T(8,128)(2,1)}, f32[2,864,768]{2,1,0:T(8,128)}, bf16[2,864,768]{2,1,0:T(8,128)(2,1)}) custom-call(bf16[2,864,768]{2,1,0:T(8,128)(2,1)} %get-tuple-element.65.o_ref.refs_4_, bf16[2,864,768]{2,1,0:T(8,128)(2,1)} %x_ref.5, f32[2,9,768]{2,1,0:T(8,128)} %reshape.46.mod_ref, bf16[768,768]{1,0:T(8,128)(2,1)} %get-tuple-element.66.wo_ref, ...), custom_call_target="tpu_custom_call" | custom-call | tf_op jit(solution)/shard_map/after_self/pallas_call | solution.py:394
  226.5 14.3 %cross_forward.1 = (bf16[2,864,768]{2,1,0:T(8,128)(2,1)}, f32[2,6,864,128]{3,2,1,0:T(8,128)}) custom-call(s32[2]{0:T(128)} %refs_0_.3, bf16[2,864,768]{2,1,0:T(8,128)(2,1)} %get-tuple-element.69.refs_1_, bf16[2,256,1536]{2,1,0:T(8,128)(2,1)} %bitcast.33, bf16[2,256,1536]{2,1,0:T(8,128)(2,1)} %bitcast.34), custom_call_target="tpu_custom_call" | custom-call | tf_op jit(solution)/shard_map/cross_forward/pallas_call | solution.py:260
  240.8 8.7 %after_cross.1 = (bf16[2,864,768]{2,1,0:T(8,128)(2,1)}, f32[2,864,768]{2,1,0:T(8,128)}) custom-call(bf16[2,864,768]{2,1,0:T(8,128)(2,1)} %get-tuple-element.71.o_ref.refs_5_, f32[2,864,768]{2,1,0:T(8,128)} %get-tuple-element.72.h_ref, f32[2,9,768]{2,1,0:T(8,128)} %reshape.46.mod_ref, bf16[768,768]{1,0:T(8,128)(2,1)} %get-tuple-element.73.wo_ref.w_ref, ...), custom_call_target="tpu_custom_call" | custom-call | tf_op jit(solution)/shard_map/after_cross/pallas_call | solution.py:418
  249.5 71.8 %feed.1 = (bf16[2,864,768]{2,1,0:T(8,128)(2,1)}, f32[2,864,768]{2,1,0:T(8,128)}, bf16[768,3072]{1,0:T(8,128)(2,1)}, bf16[3072,768]{1,0:T(8,128)(2,1)}, f32[1,307...) custom-call(f32[2,864,768]{2,1,0:T(8,128)} %get-tuple-element.75.h_ref, bf16[2,864,768]{2,1,0:T(8,128)(2,1)} %dy_ref.1, ...), custom_call_target="tpu_custom_call" | custom-call | tf_op jit(solution)/shard_map/feed/pallas_call | solution.py:551
  321.2 10.7 %before_cross.1 = (bf16[2,864,768]{2,1,0:T(8,128)(2,1)}, bf16[768,768]{1,0:T(8,128)(2,1)}, f32[1,768]{1,0:T(1,128)}, f32[2,1,768]{2,1,0:T(1,128)}) custom-call(f32[2,864,768]{2,1,0:T(8,128)} %get-tuple-element.81.dh_ref, bf16[2,864,768]{2,1,0:T(8,128)(2,1)} %get-tuple-element.82.z_ref, bf16[2,864,768]{2,1,0:T(8,128)(2,1)} %get-tuple-element.71.o_ref.refs_5_, ...), custom_call_target="tpu_custom_call" | custom-call | tf_op jit(solution)/shard_map/before_cross/pallas_call | solution.py:626
  331.9 20.7 %cross_back.1 = (bf16[2,864,768]{2,1,0:T(8,128)(2,1)}, bf16[2,256,768]{2,1,0:T(8,128)(2,1)}, bf16[2,256,768]{2,1,0:T(8,128)(2,1)}) custom-call(s32[2]{0:T(128)} %refs_0_.3, bf16[2,864,768]{2,1,0:T(8,128)(2,1)} %get-tuple-element.69.refs_1_, bf16[2,256,1536]{2,1,0:T(8,128)(2,1)} %bitcast.35, bf16[2,256,1536]{2,1,0:T(8,128)(2,1)} %bitcast.36, ...), custom_call_target="tpu_custom_call" | custom-call | tf_op jit(solution)/shard_map/cross_back/pallas_call | solution.py:365
  352.6 20.1 %before_self.1 = (f32[2,864,768]{2,1,0:T(8,128)}, bf16[2,864,768]{2,1,0:T(8,128)(2,1)}, bf16[768,768]{1,0:T(8,128)(2,1)}, bf16[768,768]{1,0:T(8,128)(2,1)}, f32[1,768]{1,0:T(1,128)}, /*index=5*/f32[2,3,768]{2,1,0:T(4,128)}) custom-call(bf16[2,864,768]{2,1,0:T(8,128)(2,1)} %get-tuple-element.85.dq_ref, f32[2,864,768]{2,1,0:T(8,128)} %get-tuple-element.72.h_ref, ...), custom_call_target="tpu_custom_call" | custom-call | tf_op jit(solution)/shard_map/before_self/pallas_call | solution.py:698
  372.7 50.7 %self_back.1 = (bf16[2,864,768]{2,1,0:T(8,128)(2,1)}, bf16[2,864,768]{2,1,0:T(8,128)(2,1)}, bf16[2,864,768]{2,1,0:T(8,128)(2,1)}) custom-call(bf16[2,864,2304]{2,1,0:T(8,128)(2,1)} %qkv_forward.1.refs_0_.refs_1_.refs_2_, bf16[2,864,2304]{2,1,0:T(8,128)(2,1)} %qkv_forward.1.refs_0_.refs_1_.refs_2_, bf16[2,864,2304]{2,1,0:T(8,128)(2,1)} %qkv_forward.1.refs_0_.refs_1_.refs_2_, ...), custom_call_target="tpu_custom_call" | custom-call | tf_op jit(solution)/shard_map/self_back/pallas_call | solution.py:365
  423.5 22.1 %input_back.1 = (bf16[2,864,768]{2,1,0:T(8,128)(2,1)}, bf16[768,2304]{1,0:T(8,128)(2,1)}, f32[2,2,768]{2,1,0:T(2,128)}) custom-call(bf16[2,864,768]{2,1,0:T(8,128)(2,1)} %get-tuple-element.89.dq_ref, bf16[2,864,768]{2,1,0:T(8,128)(2,1)} %get-tuple-element.90.dk_ref, bf16[2,864,768]{2,1,0:T(8,128)(2,1)} %get-tuple-element.91.dv_ref, ...), custom_call_target="tpu_custom_call" | custom-call | tf_op jit(solution)/shard_map/input_back/pallas_call | solution.py:751
  445.6 0.7 convert.21
  447.3 4.9 fusion.refs_4_
  452.2 15.6 %pack.1.g_ref = bf16[32,2496,128]{2,1,0:T(8,128)(2,1)} custom-call(bf16[768,2304]{1,0:T(8,128)(2,1)} %get-tuple-element.94.refs_0_, bf16[768,768]{1,0:T(8,128)(2,1)} %get-tuple-element.95.refs_1_, f32[1,768]{1,0:T(1,128)} %get-tuple-element.96.refs_2_, bf16[768,768]{1,0:T(8,128)(2,1)} %get-tuple-element.97.refs_3_, bf16[1024,1536]{1,0:T(8,128)(2,1)} %fusion.refs_4_, ...), custom_call_target="tpu_custom_call" | custom-call | tf_op jit(solution)/shard_map/pack/pallas_call | solution.py:1094
  467.7 125.4 %scatter_chunks.1 = (bf16[3712,128]{1,0:T(8,128)(2,1)}, bf16[32,112,128]{2,1,0:T(8,128)(2,1)}) custom-call(bf16[32,2496,128]{2,1,0:T(8,128)(2,1)} %pack.1.g_ref, bf16[112,128]{1,0:T(8,128)(2,1)} %pad.14.rows_ref), custom_call_target="tpu_custom_call" | custom-call | tf_op jit(solution)/shard_map/scatter_chunks/pallas_call | solution.py:1719
  593.1 2.5 bitcast_convert_fusion.1.dmod_ref
  595.6 5.0 own_grad.1
  600.6 21.4 %squares.1 = f32[32,8,128]{2,1,0:T(8,128)} custom-call(f32[8,128]{1,0:T(8,128)} %get-tuple-element.112.in_ref), custom_call_target="tpu_custom_call" | custom-call | tf_op jit(solution)/shard_map/squares/pallas_call | solution.py:1770
  622.0 1.5 reduce_sum.19
  624.3 6.1 multiply_subtract_fusion
  (28 shorter events, 3.3 us)
Async XLA Ops:
  0.6 1.2 copy-start
  5.8 29.3 %copy-start.1 = (f32[473472]{0:T(1024)S(1)}, f32[473472]{0:T(1024)}, u32[]{:S(2)}) copy-start(f32[473472]{0:T(1024)} %param.13) | copy-start | bytes 5681668
  423.4 22.9 %copy-start.4 = (f32[2,1,768]{2,1,0:T(1,128)S(1)}, f32[2,1,768]{2,1,0:T(1,128)}, u32[]{:S(2)}) copy-start(f32[2,1,768]{2,1,0:T(1,128)} %get-tuple-element.108) | copy-start | bytes 18436
  423.4 22.9 %copy-start.3 = (f32[2,3,768]{2,1,0:T(4,128)S(1)}, f32[2,3,768]{2,1,0:T(4,128)}, u32[]{:S(2)}) copy-start(f32[2,3,768]{2,1,0:T(4,128)} %get-tuple-element.107) | copy-start | bytes 55300
  423.5 22.9 %copy-start.2 = (f32[2,3,768]{2,1,0:T(4,128)S(1)}, f32[2,3,768]{2,1,0:T(4,128)}, u32[]{:S(2)}) copy-start(f32[2,3,768]{2,1,0:T(4,128)} %get-tuple-element.109) | copy-start | bytes 55300

commit v5 on v4

--- a/solution.py
+++ b/solution.py
@@ -279,10 +279,16 @@
         len_ref, q_ref, k_ref, v_ref, do_ref, o_ref, l_ref, dq_ref, dk_ref, dv_ref = refs
     else:
         q_ref, k_ref, v_ref, do_ref, o_ref, l_ref, dq_ref, dk_ref, dv_ref = refs
+    length = len_ref[pl.program_id(0)] if masked else None
+    attend_back_step(
+        length, q_ref, k_ref, v_ref, do_ref, o_ref, l_ref, dq_ref, dk_ref, dv_ref
+    )
+
+
+def attend_back_step(length, q_ref, k_ref, v_ref, do_ref, o_ref, l_ref, dq_ref, dk_ref, dv_ref):
     lane, low = head_lanes()
     for pair in range(l_ref.shape[1]):
         columns = slice(pair * 2 * HD, (pair + 1) * 2 * HD)
-        length = len_ref[pl.program_id(0)] if masked else None
         attend_back_pair(
             lane,
             low,
@@ -486,7 +492,11 @@
         dh_ref[...] = jnp.zeros_like(dh_ref)
 
     up, down = up_ref[...], down_ref[...]
-    for clip, start, at in spans:
+
+    per = frames // rows
+
+    def one(index):
+        at = pl.multiple_of(index * rows, rows)
         here = pl.ds(at, rows)
         hidden = nn(in_s[here], up) + upb_ref[...]
         square = hidden * hidden
@@ -499,9 +509,17 @@
         )
         grad_hidden = (nt(dz_s[here], down) * slope).astype(BF)
         z_s[here] += nn(activated, down)
-        dh_ref[clip, start : start + rows] += nt(grad_hidden, up)
+        spot = pl.ds(pl.multiple_of(index % per * rows, rows), rows)
+        dh_ref[index // per, spot] += nt(grad_hidden, up)
         act_s[here] = activated
         du_s[here] = grad_hidden
+
+    def one_clip(clip, _):
+        for part in range(per):
+            one(clip * per + part)
+        return 0
+
+    lax.fori_loop(0, clips, one_clip, 0)
     dup_ref[...] = nn(int_s[...], du_s[...]).astype(BF)
     ddown_ref[...] = nn(dzt_s[...], act_s[...]).T.astype(BF)
     dupb_ref[...] = column_sum(du_s[...].astype(F32))
@@ -766,9 +784,9 @@
     )(*grads, latents, dh, mod, weight)
 
 
-def block_pass(latents, captions, lengths, cotangent, mod, weights):
+def block_pass(latents, captions, lengths, cotangent, mod, triple_weight, front, back):
+    triple, mixed_one, lse_one, weights = front(latents, mod, triple_weight)
     (
-        triple_weight,
         output_weight,
         output_bias,
         cross_query,
@@ -784,8 +802,6 @@
     slots = captions.shape[1]
     groups = HEADS // 2
     caption_flat = captions.reshape(clips * slots, captions.shape[2])
-    triple = qkv_forward(latents, mod, triple_weight)
-    mixed_one, lse_one = attend_forward(triple, groups, triple, 2 * groups, None, "self_forward", 2)
     branch_one, hidden_one, cross_queries = after_self(
         mixed_one, latents, mod, output_weight, output_bias, cross_query
     )
@@ -819,40 +835,39 @@
     dh_one, grad_mixed_one, grad_cross_query, grad_output, grad_output_bias, sums_two = before_self(
         grad_cq, hidden_one, dh_two, branch_one, mixed_one, mod, cross_query, output_weight
     )
-    grads_one = attend_backward(
-        triple,
-        groups,
-        triple,
-        2 * groups,
-        None,
-        grad_mixed_one,
-        mixed_one,
-        lse_one,
-        "self_back",
-        2,
-    )
+    gradients = [
+        grad_output,
+        grad_output_bias,
+        grad_cross_query,
+        grad_keyval,
+        grad_cross_output,
+        grad_cross_bias,
+        grad_up,
+        grad_up_bias,
+        grad_down,
+        grad_down_bias,
+    ]
+    grads_one, rest = back(triple, grad_mixed_one, mixed_one, lse_one, gradients)
     input_grad, grad_triple, sums_one = input_back(grads_one, latents, dh_one, mod, triple_weight)
     grad_mod = jnp.concatenate(
         [sums_one, sums_two[:, 2:], sums_two[:, :2], gate_two, sums_three], axis=1
     ).astype(BF)
-    return (
-        output,
-        input_grad,
-        grad_mod,
-        [
-            grad_triple,
-            grad_output,
-            grad_output_bias,
-            grad_cross_query,
-            grad_keyval,
-            grad_cross_output,
-            grad_cross_bias,
-            grad_up,
-            grad_up_bias,
-            grad_down,
-            grad_down_bias,
-        ],
-    )
+    return output, input_grad, grad_mod, grad_triple, gradients, rest
+
+
+def plain_front(weights, latents, mod, triple_weight):
+    groups = HEADS // 2
+    triple = qkv_forward(latents, mod, triple_weight)
+    mixed, lse = attend_forward(triple, groups, triple, 2 * groups, None, "self_forward", 2)
+    return triple, mixed, lse, weights
+
+
+def plain_back(triple, grad_mixed, mixed, lse, gradients):
+    groups = HEADS // 2
+    grads = attend_backward(
+        triple, groups, triple, 2 * groups, None, grad_mixed, mixed, lse, "self_back", 2
+    )
+    return grads, None
 
 
 LANE = 128
@@ -869,28 +884,49 @@
     return spots
 
 
-class Plan:
-    def __init__(self, devices, share):
-        self.devices, self.share = devices, share
-        spots = linear_layout()
-        self.first_row = spots[2][0]
-        self.rows = spots[-1][0] + spots[-1][1]
-        self.lead = self.first_row // share
+class Group:
+    def __init__(self, devices, inner, share, first, last):
+        self.devices, self.share, self.first, self.last = devices, share, first, last
         self.padded = -(-share // TILE) * TILE
-        self.lent = -(-(self.padded // 3) // TILE) * TILE
-        self.kept = self.padded - self.lent
-        self.chunk = 2 * self.lent
-        self.base = (self.first_row - self.lead * share) // TILE * TILE
+        owners, total = {}, 0
+        for owner in range(first // share, (last - 1) // share + 1):
+            low = max(first - owner * share, 0) // TILE
+            high = -(-min(last - owner * share, share) // TILE)
+            owners[owner] = [low, high]
+            total += high - low
+        self.tiles = 2 * -(-total // (2 * devices))
+        self.chunk = self.tiles * TILE
+        self.half = self.chunk // 2
+        self.folds = next(
+            n
+            for n in range(1, 99)
+            if self.half % (n * TILE) == 0 and self.half // n <= 512
+        )
+        room = [self.tiles] * devices
+        self.pieces = []
+
+        def give(owner, device):
+            low, high = owners[owner]
+            take = min(high - low, room[device])
+            if take > 0:
+                place = self.tiles - room[device]
+                self.pieces.append((owner, device, low * TILE, place * TILE, take * TILE))
+                room[device] -= take
+                owners[owner][0] += take
+
+        for flip in (0, 2 * inner, inner):
+            for owner in owners:
+                give(owner, owner ^ flip)
+        for owner in owners:
+            while owners[owner][0] < owners[owner][1]:
+                give(owner, max(range(devices), key=lambda device: room[device]))
 
     def find(self, row):
         owner, at = divmod(row, self.share)
-        if at < self.kept:
-            base = self.base if owner == self.lead else 0
-            return owner, at - base, self.kept - at
-        if owner == self.lead:
-            return self.lead - 1, at - self.kept, self.share - at
-        lender = owner - self.lead - 1
-        return lender // 2, (lender % 2) * self.lent + at - self.kept, self.share - at
+        for holder, device, start, place, count in self.pieces:
+            if holder == owner and start <= at < start + count:
+                return device, place + at - start, min(self.share, start + count) - at
+        raise ValueError(row)
 
     def segments(self, start, count):
         found = []
@@ -901,6 +937,9 @@
             found.append((chunk, place, row, take))
             row += take
         return found
+
+    def moves(self):
+        return self.pieces
 
 
 def unpack_kernel(*refs, plan, indices, step):
@@ -1109,7 +1148,6 @@
 
 
 MESH = pl.DeviceIdType.MESH
-ROWS = 208
 
 
 def place_of():
@@ -1132,10 +1170,10 @@
 
 
 class Trade:
-    def __init__(self, source, target, own_sem, send_sem, recv_sem, plan, inner, senders, receivers):
+    def __init__(self, source, target, own_sem, send_sem, recv_sem, group, inner, senders, receivers):
         self.source, self.target, self.own_sem = source, target, own_sem
         self.send_sem, self.recv_sem = send_sem, recv_sem
-        self.devices, self.inner = plan.devices, inner
+        self.devices, self.inner = group.devices, inner
         self.senders, self.receivers = senders, receivers
         self.me = lax.axis_index("dp") * inner + lax.axis_index("fsdp")
         self.many = len(source.shape) == 3
@@ -1207,218 +1245,361 @@
         pl.when(condition)(body)
 
 
+class Deal:
+    def __init__(self, group, source, target, send_sem, recv_sem, inner, back):
+        self.source, self.target, self.back = source, target, back
+        self.send_sem, self.recv_sem, self.inner = send_sem, recv_sem, inner
+        self.me = lax.axis_index("dp") * inner + lax.axis_index("fsdp")
+        self.moves = []
+        for owner, device, row, place, count in group.moves():
+            if back:
+                self.moves.append((device, owner, place, row, count))
+            else:
+                self.moves.append((owner, device, row, place, count))
+
+    def copy(self, move):
+        source, target, start, place, count = move
+        out = [m for m in self.moves if m[0] == source].index(move)
+        into = [m for m in self.moves if m[1] == target].index(move)
+        from_ref = self.source.at[pl.ds(start, count)]
+        to_ref = self.target.at[pl.ds(place, count)]
+        if source == target:
+            return pltpu.make_async_copy(from_ref, to_ref, self.recv_sem.at[into])
+        return pltpu.make_async_remote_copy(
+            src_ref=from_ref,
+            dst_ref=to_ref,
+            send_sem=self.send_sem.at[out],
+            recv_sem=self.recv_sem.at[into],
+            device_id=(target // self.inner, target % self.inner),
+            device_id_type=MESH,
+        )
+
+    def each(self, key, act):
+        for device in sorted({m[key] for m in self.moves}):
+            mine = [m for m in self.moves if m[key] == device]
+
+            @pl.when(self.me == device)
+            def _(mine=mine):
+                for move in mine:
+                    act(move)
+
+    def start(self):
+        self.each(0, lambda move: self.copy(move).start())
+
+    def landed(self):
+        def act(move):
+            if move[0] == move[1]:
+                self.copy(move).wait()
+            else:
+                self.copy(move).wait_recv()
+
+        self.each(1, act)
+
+    def gone(self):
+        def act(move):
+            if move[0] != move[1]:
+                self.copy(move).wait_send()
+
+        self.each(0, act)
+
+    @staticmethod
+    def semaphores(group, back):
+        sends = recvs = 0
+        for device in range(group.devices):
+            sends = max(sends, sum(1 for m in group.moves() if m[1 if back else 0] == device))
+            recvs = max(recvs, sum(1 for m in group.moves() if m[0 if back else 1] == device))
+        dma = pltpu.SemaphoreType.DMA
+        return [dma((sends,)), dma((recvs,))]
+
+
+def remote_call(body, in_specs, out_specs, out_shape, scratch, collective, name, grid=()):
+    return pl.pallas_call(
+        body,
+        grid=grid,
+        in_specs=in_specs,
+        out_specs=out_specs,
+        out_shape=out_shape,
+        scratch_shapes=scratch,
+        compiler_params=pltpu.CompilerParams(
+            collective_id=collective, has_side_effects=True, vmem_limit_bytes=VMEM_LIMIT
+        ),
+        name=name,
+    )
+
+
+ANYWHERE = pl.BlockSpec(memory_space=pl.ANY)
+
+
 def start_kernel(
-    cond_ref, slot_ref, all_ref, own_ref, own_sem, lend_send, lend_recv, send_sem, recv_sem,
-    *, plan, inner
+    step_ref, slot_ref, all_ref, chunk_ref, own_sem, send_sem, recv_sem, deal_send, deal_recv,
+    *, group, inner
 ):
-    dp, fs, _, _, _, _ = place_of()
-    me = dp * inner + fs
-    lead, lent, kept = plan.lead, plan.lent, plan.kept
-    meet_all(me, plan.devices, inner)
-
-    def own_copy():
-        start = pl.multiple_of(jnp.where(me == lead, plan.base, 0), TILE)
-        return pltpu.make_async_copy(
-            slot_ref.at[pl.ds(start, plan.chunk)], own_ref, own_sem.at[0]
-        )
-
-    def lend(slot, target, part):
+    me = lax.axis_index("dp") * inner + lax.axis_index("fsdp")
+    meet_all(me, group.devices, inner)
+    deal = Deal(group, slot_ref, chunk_ref, deal_send, deal_recv, inner, False)
+    trade = Trade(
+        step_ref, all_ref, own_sem, send_sem, recv_sem, group, inner, group.devices, group.devices
+    )
+    trade.start()
+    deal.start()
+    trade.wait()
+    deal.landed()
+    deal.gone()
+
+
+def start_chunks(steps, slot, group, inner, collective):
+    dma = pltpu.SemaphoreType.DMA
+    return remote_call(
+        functools.partial(start_kernel, group=group, inner=inner),
+        [ANYWHERE] * 2,
+        [ANYWHERE] * 2,
+        [
+            jax.ShapeDtypeStruct((group.devices, *steps.shape), steps.dtype),
+            jax.ShapeDtypeStruct((group.chunk, LANE), BF),
+        ],
+        [dma, dma((group.devices,)), dma((group.devices,))] + Deal.semaphores(group, False),
+        collective,
+        "start_chunks",
+    )(steps, slot)
+
+
+class Gather:
+    def __init__(self, group, inner, chunk_ref, out_ref, own_sem, send_sem, recv_sem):
+        self.group, self.inner = group, inner
+        self.chunk_ref, self.out_ref = chunk_ref, out_ref
+        self.send_sem, self.recv_sem = send_sem, recv_sem
+        dp, fs, self.y, self.x, self.z, self.c = place_of()
+        self.levels = inner // 2
+        self.own = pltpu.make_async_copy(chunk_ref, out_ref.at[dp * inner + fs], own_sem)
+        self.across = {
+            "up": (dp, fs + 2),
+            "down": (dp, fs - 2),
+            "x": (dp + 1 - 2 * self.x, fs),
+            "y": (dp + 2 - 4 * self.y, fs),
+            "twin": (dp, fs + 1 - 2 * self.c),
+        }
+        self.kinds = tuple(self.across)
+        self.closing = False
+
+    @staticmethod
+    def semaphores(group):
+        dma = pltpu.SemaphoreType.DMA
+        return [dma, dma((5, group.devices // 2, 2)), dma((group.devices, 2))]
+
+    def copy(self, kind, yy, xx, zz, part, cc=None, mine=False):
+        core = self.c if cc is None else cc
+        column = yy * 2 + xx
+        index = column * self.inner + zz * 2 + core
+        rows = pl.ds(part * self.group.half, self.group.half)
         return pltpu.make_async_remote_copy(
-            src_ref=slot_ref.at[pl.ds(kept, lent)],
-            dst_ref=own_ref.at[pl.ds(pl.multiple_of(part * lent, TILE), lent)],
-            send_sem=lend_send.at[slot],
-            recv_sem=lend_recv.at[part],
-            device_id=(target // inner, target % inner),
+            src_ref=self.chunk_ref.at[rows] if mine else self.out_ref.at[index, rows],
+            dst_ref=self.out_ref.at[index, rows],
+            send_sem=self.send_sem.at[
+                self.kinds.index(kind), column * self.levels + zz, part
+            ],
+            recv_sem=self.recv_sem.at[index, part],
+            device_id=self.across[kind],
             device_id_type=MESH,
         )
 
-    lender = jnp.maximum(me - lead - 1, 0)
-
-    @pl.when(me > lead)
-    def _():
-        lend(0, lender // 2, lender % 2).start()
-
-    @pl.when(me == lead)
-    def _():
-        lend(0, lead - 1, 0).start()
-        lend(1, lead - 1, 1).start()
-
-    @pl.when(me >= lead)
-    def _():
-        own_copy().start()
-
-    trade = Trade(
-        cond_ref, all_ref, own_sem.at[1], send_sem, recv_sem, plan, inner, plan.devices, plan.devices
-    )
-    trade.start()
-    trade.wait()
-
-    @pl.when(me >= lead)
-    def _():
-        own_copy().wait()
-        lend(0, lead - 1, 0).wait_send()
-
-    @pl.when(me == lead)
-    def _():
-        lend(1, lead - 1, 1).wait_send()
-
-    @pl.when(me < lead)
-    def _():
-        lend(0, lead - 1, 0).wait_recv()
-        lend(0, lead - 1, 1).wait_recv()
-
-
-def start_chunks(condition, slot, plan, inner, collective):
-    anywhere = pl.BlockSpec(memory_space=pl.ANY)
-    dma = pltpu.SemaphoreType.DMA
-    return pl.pallas_call(
-        functools.partial(start_kernel, plan=plan, inner=inner),
-        in_specs=[anywhere] * 2,
-        out_specs=[anywhere] * 2,
-        out_shape=[
-            jax.ShapeDtypeStruct((plan.devices, *condition.shape), condition.dtype),
-            jax.ShapeDtypeStruct((plan.chunk, LANE), BF),
-        ],
-        scratch_shapes=[
-            dma((2,)),
-            dma((2,)),
-            dma((2,)),
-            dma((plan.devices,)),
-            dma((plan.devices,)),
-        ],
-        compiler_params=pltpu.CompilerParams(collective_id=collective, has_side_effects=True),
-        name="start_chunks",
-    )(condition, slot)
-
-
-def gather_kernel(
-    chunk_ref, slab_ref, out_ref, parts_ref, own_sem, slab_send, slab_recv, send_sem, recv_sem,
-    *, plan, inner
-):
-    dp, fs, y, x, z, c = place_of()
-    me = dp * inner + fs
-    lent = plan.lent
-    levels = inner // 2
-    meet_all(me, plan.devices, inner)
-    own = pltpu.make_async_copy(chunk_ref, out_ref.at[me], own_sem.at[0])
-    own.start()
-    trade = Trade(
-        slab_ref, parts_ref, own_sem.at[1], slab_send, slab_recv, plan, inner, plan.lead + 1, plan.devices
-    )
-
-    across = {
-        "up": (dp, fs + 2),
-        "down": (dp, fs - 2),
-        "x": (dp + 1 - 2 * x, fs),
-        "y": (dp + 2 - 4 * y, fs),
-        "twin": (dp, fs + 1 - 2 * c),
-    }
-    kinds = tuple(across)
-    pending = []
-
-    def copy(kind, yy, xx, zz, part, cc=None, mine=False):
-        core = c if cc is None else cc
-        column = yy * 2 + xx
-        index = column * inner + zz * 2 + core
-        rows = pl.ds(part * lent, lent)
-        return pltpu.make_async_remote_copy(
-            src_ref=chunk_ref.at[rows] if mine else out_ref.at[index, rows],
-            dst_ref=out_ref.at[index, rows],
-            send_sem=send_sem.at[kinds.index(kind), column * levels + zz, part],
-            recv_sem=recv_sem.at[index, part],
-            device_id=across[kind],
-            device_id_type=MESH,
-        )
-
-    def send(condition, kind, yy, xx, zz, part, mine=False):
-        guarded(condition, lambda: copy(kind, yy, xx, zz, part, mine=mine).start())
-        pending.append((condition, kind, yy, xx, zz, part))
-
-    def arrive(condition, yy, xx, zz, part):
-        guarded(condition, lambda: copy("x", yy, xx, zz, part).wait_recv())
-
-    def spread(distance):
+    def send(self, condition, kind, yy, xx, zz, part, mine=False):
+        copy = functools.partial(self.copy, kind, yy, xx, zz, part, mine=mine)
+        if self.closing:
+            guarded(condition, lambda: copy().wait_send())
+        else:
+            guarded(condition, lambda: copy().start())
+
+    def arrive(self, condition, yy, xx, zz, part):
+        if self.closing:
+            return
+        guarded(condition, lambda: self.copy("x", yy, xx, zz, part).wait_recv())
+
+    def spread(self, distance):
         for sign in (1, -1) if distance else (0,):
-            zz = z + sign * distance
+            zz = self.z + sign * distance
             inside = when_all(
-                [zz < levels if sign > 0 else None, zz >= 0 if sign < 0 else None]
+                [zz < self.levels if sign > 0 else None, zz >= 0 if sign < 0 else None]
             )
             yield zz, sign, inside
 
-    for turn in range(levels + 2):
+    def turn(self, turn):
+        y, x, z, levels = self.y, self.x, self.z, self.levels
+        if turn == 0 and not self.closing:
+            self.own.start()
         if turn < levels:
-            for zz, sign, inside in spread(turn):
+            for zz, sign, inside in self.spread(turn):
+                mine = turn == 0
                 for part in range(2):
                     if turn:
-                        arrive(inside, y, x, zz, part)
+                        self.arrive(inside, y, x, zz, part)
                     if sign <= 0:
-                        send(when_all([inside, z < levels - 1]), "up", y, x, zz, part, turn == 0)
+                        self.send(when_all([inside, z < levels - 1]), "up", y, x, zz, part, mine)
                     if sign >= 0:
-                        send(when_all([inside, z > 0]), "down", y, x, zz, part, turn == 0)
+                        self.send(when_all([inside, z > 0]), "down", y, x, zz, part, mine)
                     for kind in ("x", "y") if part else ("y", "x"):
-                        send(inside, kind, y, x, zz, part, turn == 0)
-                    send(inside, "twin", y, x, zz, part, turn == 0)
-            if turn == 0:
-                trade.start()
+                        self.send(inside, kind, y, x, zz, part, mine)
+                    self.send(inside, "twin", y, x, zz, part, mine)
         if 1 <= turn <= levels:
-            for zz, sign, inside in spread(turn - 1):
-                arrive(inside, y, 1 - x, zz, 0)
-                send(inside, "y", y, 1 - x, zz, 0)
-                send(inside, "twin", y, 1 - x, zz, 0)
-                arrive(inside, 1 - y, x, zz, 1)
-                send(inside, "x", 1 - y, x, zz, 1)
-                send(inside, "twin", 1 - y, x, zz, 1)
-                arrive(inside, 1 - y, x, zz, 0)
-                send(inside, "twin", 1 - y, x, zz, 0)
-                arrive(inside, y, 1 - x, zz, 1)
-                send(inside, "twin", y, 1 - x, zz, 1)
+            for zz, sign, inside in self.spread(turn - 1):
+                self.arrive(inside, y, 1 - x, zz, 0)
+                self.send(inside, "y", y, 1 - x, zz, 0)
+                self.send(inside, "twin", y, 1 - x, zz, 0)
+                self.arrive(inside, 1 - y, x, zz, 1)
+                self.send(inside, "x", 1 - y, x, zz, 1)
+                self.send(inside, "twin", 1 - y, x, zz, 1)
+                self.arrive(inside, 1 - y, x, zz, 0)
+                self.send(inside, "twin", 1 - y, x, zz, 0)
+                self.arrive(inside, y, 1 - x, zz, 1)
+                self.send(inside, "twin", y, 1 - x, zz, 1)
         if turn >= 2:
-            for zz, sign, inside in spread(turn - 2):
+            for zz, sign, inside in self.spread(turn - 2):
                 for part in range(2):
-                    arrive(inside, 1 - y, 1 - x, zz, part)
-                    send(inside, "twin", 1 - y, 1 - x, zz, part)
-
-    def twin_arrivals(i, _):
-        column, zz = i // levels, i % levels
-        for part in range(2):
-            copy("twin", column // 2, column % 2, zz, part, 1 - c).wait_recv()
-        return 0
-
-    lax.fori_loop(0, 4 * levels, twin_arrivals, 0)
-    for condition, kind, yy, xx, zz, part in pending:
-        guarded(condition, lambda: copy(kind, yy, xx, zz, part).wait_send())
+                    self.arrive(inside, 1 - y, 1 - x, zz, part)
+                    self.send(inside, "twin", 1 - y, 1 - x, zz, part)
+
+    def finish(self):
+        def twin_arrivals(i, _):
+            column, zz = i // self.levels, i % self.levels
+            for part in range(2):
+                self.copy("twin", column // 2, column % 2, zz, part, 1 - self.c).wait_recv()
+            return 0
+
+        lax.fori_loop(0, 4 * self.levels, twin_arrivals, 0)
+        self.closing = True
+        for turn in range(self.levels + 2):
+            self.turn(turn)
+        self.own.wait()
+
+
+class PairTrade:
+    def __init__(self, slab_ref, out_ref, mine, theirs, sems, inner, devices):
+        self.slab_ref, self.out_ref, self.mine, self.theirs = slab_ref, out_ref, mine, theirs
+        self.pair_sem, self.send_sem, self.recv_sem = sems
+        self.inner, self.chips, self.senders = inner, devices // 2, out_ref.shape[0]
+        dp, fs, _, _, _, self.core = place_of()
+        self.twin = (dp, fs + 1 - 2 * self.core)
+        self.chip = (dp * inner + fs) // 2
+
+    def load(self):
+        return pltpu.make_async_copy(self.slab_ref.at[self.core], self.mine, self.pair_sem.at[0])
+
+    def pair(self):
+        return pltpu.make_async_remote_copy(
+            src_ref=self.slab_ref.at[1 - self.core],
+            dst_ref=self.theirs,
+            send_sem=self.pair_sem.at[1],
+            recv_sem=self.pair_sem.at[2],
+            device_id=self.twin,
+            device_id_type=MESH,
+        )
+
+    def copy(self, source, target):
+        device = 2 * target + self.core
+        return pltpu.make_async_remote_copy(
+            src_ref=self.mine.at[target],
+            dst_ref=self.out_ref.at[source],
+            send_sem=self.send_sem.at[target],
+            recv_sem=self.recv_sem.at[source],
+            device_id=(device // self.inner, device % self.inner),
+            device_id_type=MESH,
+        )
+
+    def own(self):
+        return pltpu.make_async_copy(
+            self.mine.at[self.chip], self.out_ref.at[self.chip], self.pair_sem.at[3]
+        )
+
+    def each(self, act):
+        def body(i, _):
+            act((self.chip + i) % self.chips)
+            return 0
+
+        lax.fori_loop(1, self.chips, body, 0)
+
+    def begin(self):
+        @pl.when(self.chip < self.senders)
+        def _():
+            self.pair().start()
+            self.load().start()
+
+    def start(self):
+        @pl.when(self.chip < self.senders)
+        def _():
+            self.load().wait()
+            self.pair().wait_recv()
+
+            def add(i, _):
+                self.mine[i] = self.mine[i] + self.theirs[i]
+                return 0
+
+            lax.fori_loop(0, self.chips, add, 0)
+            self.own().start()
+            self.each(lambda other: self.copy(self.chip, other).start())
+
+    def wait(self):
+        def landed(other):
+            pl.when(other < self.senders)(lambda: self.copy(other, other).wait_recv())
+
+        self.each(landed)
+
+        @pl.when(self.chip < self.senders)
+        def _():
+            self.own().wait()
+            self.pair().wait_send()
+            self.each(lambda other: self.copy(self.chip, other).wait_send())
+
+
+def gather_kernel(
+    chunk_ref, slab_ref, slot_ref, out_ref, parts_ref, next_ref, mine, theirs, *sems,
+    group, later, inner
+):
+    me = lax.axis_index("dp") * inner + lax.axis_index("fsdp")
+    meet_all(me, group.devices, inner)
+    trade = PairTrade(slab_ref, parts_ref, mine, theirs, sems[:3], inner, group.devices)
+    gather = Gather(group, inner, chunk_ref, out_ref, *sems[3:6])
+    deal = Deal(later, slot_ref, next_ref, *sems[6:], inner, False)
+    trade.begin()
+    gather.turn(0)
+    trade.start()
+    gather.turn(1)
+    deal.start()
+    for turn in range(2, inner // 2 + 2):
+        gather.turn(turn)
+    gather.finish()
     trade.wait()
-    own.wait()
-
-
-def gather_chunks(chunk, slabs, plan, inner, collective):
-    anywhere = pl.BlockSpec(memory_space=pl.ANY)
+    deal.landed()
+    deal.gone()
+
+
+def gather_chunks(chunk, slabs, slot, group, later, inner, senders, collective):
     dma = pltpu.SemaphoreType.DMA
-    return pl.pallas_call(
-        functools.partial(gather_kernel, plan=plan, inner=inner),
-        in_specs=[anywhere] * 2,
-        out_specs=[anywhere] * 2,
-        out_shape=[
-            jax.ShapeDtypeStruct((plan.devices, plan.chunk, LANE), BF),
-            jax.ShapeDtypeStruct((plan.lead + 1, *slabs.shape[1:]), slabs.dtype),
+    return remote_call(
+        functools.partial(gather_kernel, group=group, later=later, inner=inner),
+        [ANYWHERE] * 3,
+        [ANYWHERE] * 3,
+        [
+            jax.ShapeDtypeStruct((group.devices, group.chunk, LANE), BF),
+            jax.ShapeDtypeStruct((senders // 2, *slabs.shape[2:]), slabs.dtype),
+            jax.ShapeDtypeStruct((later.chunk, LANE), BF),
         ],
-        scratch_shapes=[
-            dma((2,)),
-            dma((plan.devices,)),
-            dma((plan.devices,)),
-            dma((5, plan.devices // 2, 2)),
-            dma((plan.devices, 2)),
-        ],
-        compiler_params=pltpu.CompilerParams(collective_id=collective, has_side_effects=True),
-        name="gather_chunks",
-    )(chunk, slabs)
-
-
-def scatter_kernel(
+        [
+            pltpu.VMEM(slabs.shape[1:], slabs.dtype),
+            pltpu.VMEM(slabs.shape[1:], slabs.dtype),
+            dma((4,)),
+            dma((group.devices // 2,)),
+            dma((group.devices // 2,)),
+        ]
+        + Gather.semaphores(group)
+        + Deal.semaphores(later, False),
+        collective,
+        "gather_chunks",
+    )(chunk, slabs, slot)
+
+
+def scatter_stages(
+    group,
+    inner,
     g_ref,
-    rows_ref,
-    out_ref,
-    all_ref,
     acc,
     twin,
     wide_y,
@@ -1435,22 +1616,13 @@
     slim_recv,
     line_send,
     line_recv,
-    own_sem,
-    back_send,
-    back_recv,
-    row_send,
-    row_recv,
-    *,
-    plan,
-    inner,
 ):
     dp, fs, y, x, z, c = place_of()
     me = dp * inner + fs
-    lead, lent, kept = plan.lead, plan.lent, plan.kept
+    lent = group.half
     levels = inner // 2
     x_mate = (dp + 1 - 2 * x, fs)
     y_mate = (dp + 2 - 4 * y, fs)
-    meet_all(me, plan.devices, inner)
 
     def remote(source, target, send, receive, device):
         return pltpu.make_async_remote_copy(
@@ -1515,14 +1687,16 @@
             (dp, fs + 2 if upward else fs - 2),
         )
 
+    block = lent // group.folds
+
     def add(slot, first, count, source):
         def body(i, _):
-            at = pl.multiple_of(i * ROWS, TILE)
-            to = pl.ds(pl.multiple_of(first + i * ROWS, TILE), ROWS)
-            acc[slot, to] = acc[slot, to] + source[pl.ds(at, ROWS)]
+            at = pl.multiple_of(i * block, TILE)
+            to = pl.ds(pl.multiple_of(first + i * block, TILE), block)
+            acc[slot, to] = acc[slot, to] + source[pl.ds(at, block)]
             return 0
 
-        lax.fori_loop(0, count // ROWS, body, 0)
+        lax.fori_loop(0, count // block, body, 0)
 
     def add_part(slot, part, source):
         add(slot, part * lent, lent, source)
@@ -1532,20 +1706,17 @@
 
     columns = ((1 - y, 1 - x), (1 - y, x), (y, 1 - x), (y, x))
 
-    for k in range(levels):
-        for yy, xx in columns:
-            to_twin(yy, xx, level(k)).start()
-            load(yy, xx, level(k)).start()
-
-    trade = Trade(
-        rows_ref, all_ref, own_sem.at[1], row_send, row_recv, plan, inner, plan.devices, lead + 1
-    )
+    def begin():
+        for k in range(levels):
+            for yy, xx in columns:
+                to_twin(yy, xx, level(k)).start()
+                load(yy, xx, level(k)).start()
 
     def settle(yy, xx, zz):
         slot = slot_of(yy, xx, zz)
         load(yy, xx, zz).wait()
         to_twin(yy, xx, zz).wait_recv()
-        add(slot, 0, plan.chunk, twin.at[slot])
+        add(slot, 0, group.chunk, twin.at[slot])
 
     def diagonal(k):
         zz = level(k)
@@ -1586,195 +1757,355 @@
         along(upward, zz, part).wait_recv()
         add_part(slot_of(y, x, zz), part, line.at[0 if upward else 1, zz, part])
 
-    edge = (z == 0) | (z == levels - 1)
-    sent = []
-
-    def pass_on(k, allowed):
+    def ways(k, allowed):
         zz = level(k)
         for upward in (True, False):
-            inside = allowed & (zz > z if upward else zz < z)
-            more = z > 0 if upward else z < levels - 1
+            yield zz, upward, allowed() & (zz > z if upward else zz < z)
+
+    def pass_on(k, allowed):
+        more = {True: z > 0, False: z < levels - 1}
+        for zz, upward, inside in ways(k, allowed):
 
             @pl.when(inside)
-            def _(upward=upward, more=more):
+            def _(zz=zz, upward=upward):
                 for part in range(2):
 
-                    @pl.when(more)
+                    @pl.when(more[upward])
                     def _(part=part):
                         take(upward, zz, part)
 
                     along(upward, zz, part).start()
 
-            sent.append((inside, upward, zz))
+    def close_pass(k, allowed):
+        for zz, upward, inside in ways(k, allowed):
+
+            @pl.when(inside)
+            def _(zz=zz, upward=upward):
+                for part in range(2):
+                    along(upward, zz, part).wait_send()
+
+    def at_edge():
+        return (z == 0) | (z == levels - 1)
+
+    def off_edge():
+        return (z > 0) & (z < levels - 1)
+
+    def anywhere():
+        return z >= 0
 
     def once(k):
         diagonal(k)
         sides(k)
 
-    once(0)
-    once(1)
-    middle(0)
-    once(2)
-    middle(1)
-    home(0)
-    pass_on(0, edge)
-    once(3)
-    middle(2)
-    middle(3)
-    trade.start()
-    home(1)
-    pass_on(1, z >= 0)
-    home(2)
-    pass_on(2, z >= 0)
-    pass_on(0, jnp.logical_not(edge))
-    home(3)
-    for part in range(2):
-
-        @pl.when(z > 0)
-        def _(part=part):
-            take(True, z, part)
-
-        @pl.when(z < levels - 1)
-        def _(part=part):
-            take(False, z, part)
-
-    mine = slot_of(y, x, z)
-
-    def back(slot, part, owner):
-        return remote(
-            piece(mine, part),
-            out_ref.at[pl.ds(kept, lent)],
-            back_send.at[slot],
-            back_recv,
-            (owner // inner, owner % inner),
-        )
-
-    @pl.when(me < lead - 1)
+    def final():
+        for part in range(2):
+
+            @pl.when(z > 0)
+            def _(part=part):
+                take(True, z, part)
+
+            @pl.when(z < levels - 1)
+            def _(part=part):
+                take(False, z, part)
+
+    stages = {
+        "begin": begin,
+        "once0": lambda: once(0),
+        "once1": lambda: once(1),
+        "middle0": lambda: middle(0),
+        "once2": lambda: once(2),
+        "middle1": lambda: middle(1),
+        "home0": lambda: home(0),
+        "pass0": lambda: pass_on(0, at_edge),
+        "once3": lambda: once(3),
+        "middle2": lambda: middle(2),
+        "middle3": lambda: middle(3),
+        "home1": lambda: home(1),
+        "pass1": lambda: pass_on(1, anywhere),
+        "home2": lambda: home(2),
+        "pass2": lambda: pass_on(2, anywhere),
+        "inner0": lambda: pass_on(0, off_edge),
+        "home3": lambda: home(3),
+        "final": final,
+    }
+
+    def finish():
+        for k, allowed in ((0, at_edge), (1, anywhere), (2, anywhere), (0, off_edge)):
+            close_pass(k, allowed)
+
+        def close(k, _):
+            zz = level(k)
+            for yy, xx in columns:
+                to_twin(yy, xx, zz).wait_send()
+            wide(0, 1 - x, zz).wait_send()
+            wide(0, x, zz).wait_send()
+            wide(1, 1 - y, zz).wait_send()
+            wide(1, y, zz).wait_send()
+            slim(0, zz).wait_send()
+            slim(1, zz).wait_send()
+            return 0
+
+        lax.fori_loop(0, levels, close, 0)
+
+    return stages, finish, acc.at[slot_of(y, x, z)]
+
+
+def scatter_scratch(group, inner):
+    dma = pltpu.SemaphoreType.DMA
+    half, levels = group.devices // 2, inner // 2
+    part = (group.half, LANE)
+    return [
+        pltpu.VMEM((half, group.chunk, LANE), BF),
+        pltpu.VMEM((half, group.chunk, LANE), BF),
+        pltpu.VMEM((2 * levels, *part), BF),
+        pltpu.VMEM((2 * levels, *part), BF),
+        pltpu.VMEM((levels, *part), BF),
+        pltpu.VMEM((levels, *part), BF),
+        pltpu.VMEM((2, levels, 2, *part), BF),
+        dma((half,)),
+        dma((half,)),
+        dma((half,)),
+        dma((2, 2 * levels)),
+        dma((2, 2 * levels)),
+        dma((2, levels)),
+        dma((2, levels)),
+        dma((2, levels, 2)),
+        dma((2, levels, 2)),
+    ]
+
+
+def scatter_kernel(
+    g_ref, rows_ref, out_ref, all_ref, own_sem, row_send, row_recv, *rest, group, inner, receivers
+):
+    me = lax.axis_index("dp") * inner + lax.axis_index("fsdp")
+    meet_all(me, group.devices, inner)
+    stages, finish, total = scatter_stages(group, inner, g_ref, *rest[:-2])
+    trade = Trade(
+        rows_ref, all_ref, own_sem, row_send, row_recv, group, inner, group.devices, receivers
+    )
+    for name, stage in stages.items():
+        stage()
+        if name == "once0":
+            trade.start()
+    deal = Deal(group, total, out_ref, *rest[-2:], inner, True)
+    deal.start()
+    finish()
+    trade.wait()
+    deal.landed()
+    deal.gone()
+
+
+def scatter_chunks(grads, rows, group, inner, receivers, collective):
+    dma = pltpu.SemaphoreType.DMA
+    return remote_call(
+        functools.partial(scatter_kernel, group=group, inner=inner, receivers=receivers),
+        [ANYWHERE] * 2,
+        [ANYWHERE] * 2,
+        [
+            jax.ShapeDtypeStruct((group.padded, LANE), BF),
+            jax.ShapeDtypeStruct((group.devices, *rows.shape), rows.dtype),
+        ],
+        [dma, dma((group.devices,)), dma((group.devices,))]
+        + scatter_scratch(group, inner)
+        + Deal.semaphores(group, True),
+        collective,
+        "scatter_chunks",
+    )(grads, rows)
+
+
+def front_kernel(
+    x_ref, mod_ref, w_ref, chunk_ref, qkv_ref, o_ref, l_ref, out_ref, qkv_s, *sems,
+    group, inner, leads, pairs
+):
+    step = pl.program_id(0)
+    last = pl.num_programs(0) - 1
+    clips, frames, _ = qkv_s.shape
+    rows = x_ref.shape[1]
+    gather = Gather(group, inner, chunk_ref, out_ref, *sems)
+    me = lax.axis_index("dp") * inner + lax.axis_index("fsdp")
+
+    @pl.when(step == 0)
     def _():
-        back(0, 0, lead + 1 + 2 * me).start()
-        back(1, 1, lead + 2 + 2 * me).start()
-
-    @pl.when(me == lead - 1)
+        meet_all(me, group.devices, inner)
+        gather.turn(0)
+
+    for turn, at in ((1, leads), (2, leads + 2), (3, leads + 4)):
+
+        @pl.when(step == at)
+        def _(turn=turn):
+            gather.turn(turn)
+
+    @pl.when(step < leads)
     def _():
-        back(0, 0, me + 1).start()
-
-    @pl.when(me == lead)
+        normed, _ = normalize(x_ref[0].astype(F32))
+        first_in = (normed * (1.0 + mod_ref[0, 1:2]) + mod_ref[0, 0:1]).astype(BF)
+        block = nn(first_in, w_ref[...]).astype(BF)
+        qkv_ref[0] = block
+        start = pl.multiple_of(step * rows % frames, rows)
+        qkv_s[step * rows // frames, pl.ds(start, rows)] = block
+
+    @pl.when(step >= leads)
     def _():
-        count = kept - plan.base
-        copy = pltpu.make_async_copy(
-            acc.at[mine, pl.ds(0, count)], out_ref.at[pl.ds(plan.base, count)], own_sem.at[0]
-        )
-        copy.start()
-        copy.wait()
-
-    @pl.when(me > lead)
+        lane, low = head_lanes()
+        count = HEADS // 2 // pairs
+        clip, group_index = (step - leads) // count, (step - leads) % count
+        for pair in range(pairs):
+
+            def columns(part):
+                at = (group_index * pairs + pair + part * HEADS // 2) * 2 * HD
+                return qkv_s[clip, :, pl.ds(pl.multiple_of(at, 2 * HD), 2 * HD)]
+
+            attend_pair(
+                lane,
+                low,
+                None,
+                columns(0),
+                columns(1),
+                columns(2),
+                o_ref.at[0, :, pair * 2 * HD : (pair + 1) * 2 * HD],
+                l_ref.at[0, pair],
+            )
+
+    @pl.when(step == last)
     def _():
-        copy = pltpu.make_async_copy(
-            acc.at[mine, pl.ds(0, kept)], out_ref.at[pl.ds(0, kept)], own_sem.at[0]
-        )
-        copy.start()
-        copy.wait()
-
-    @pl.when(me >= lead)
+        for turn in range(4, inner // 2 + 2):
+            gather.turn(turn)
+        gather.finish()
+
+
+def front_and_gather(latents, mod, weight, chunk, group, inner, collective, pairs=2):
+    clips, frames, width = latents.shape
+    rows = row_block(frames)
+    per = frames // rows
+    leads = clips * per
+    count = HEADS // 2 // pairs
+
+    def lead(s):
+        return jnp.minimum(s, leads - 1)
+
+    def tail(s):
+        return jnp.maximum(s - leads, 0)
+
+    wide = weight.shape[1]
+    return remote_call(
+        functools.partial(front_kernel, group=group, inner=inner, leads=leads, pairs=pairs),
+        [
+            pl.BlockSpec((1, rows, width), lambda s: (lead(s) // per, lead(s) % per, 0)),
+            pl.BlockSpec((1, 9, width), lambda s: (lead(s) // per, 0, 0)),
+            whole_spec(weight.shape),
+            ANYWHERE,
+        ],
+        [
+            pl.BlockSpec((1, rows, wide), lambda s: (lead(s) // per, lead(s) % per, 0)),
+            pl.BlockSpec(
+                (1, frames, 2 * HD * pairs), lambda s: (tail(s) // count, 0, tail(s) % count)
+            ),
+            pl.BlockSpec(
+                (1, pairs, frames, 2 * HD), lambda s: (tail(s) // count, tail(s) % count, 0, 0)
+            ),
+            ANYWHERE,
+        ],
+        [
+            struct((clips, frames, wide), BF),
+            struct((clips, frames, width), BF),
+            struct((clips, HEADS // 2, frames, 2 * HD), F32),
+            struct((group.devices, group.chunk, LANE), BF),
+        ],
+        [pltpu.VMEM((clips, frames, wide), BF)] + Gather.semaphores(group),
+        collective,
+        "front_and_gather",
+        (leads + clips * count,),
+    )(latents, mod, weight, chunk)
+
+
+def back_kernel(
+    q_ref, k_ref, v_ref, do_ref, o_ref, l_ref, g_ref, dq_ref, dk_ref, dv_ref, rest_ref, *scratch,
+    group, inner
+):
+    step = pl.program_id(0)
+    last = pl.num_programs(0) - 1
+    stages, finish, total = scatter_stages(group, inner, g_ref, *scratch[:-2])
+    deal = Deal(group, total, rest_ref, *scratch[-2:], inner, True)
+    me = lax.axis_index("dp") * inner + lax.axis_index("fsdp")
+
+    @pl.when(step == 0)
     def _():
-        back(0, 0, 0).wait_recv()
-
-    for inside, upward, zz in sent:
-
-        @pl.when(inside)
-        def _(upward=upward, zz=zz):
-            for part in range(2):
-                along(upward, zz, part).wait_send()
-
-    def finish(k, _):
-        zz = level(k)
-        for yy, xx in columns:
-            to_twin(yy, xx, zz).wait_send()
-        wide(0, 1 - x, zz).wait_send()
-        wide(0, x, zz).wait_send()
-        wide(1, 1 - y, zz).wait_send()
-        wide(1, y, zz).wait_send()
-        slim(0, zz).wait_send()
-        slim(1, zz).wait_send()
-        return 0
-
-    lax.fori_loop(0, levels, finish, 0)
-
-    @pl.when(me < lead)
+        meet_all(me, group.devices, inner)
+
+    plan = (
+        (0, ("begin",)),
+        (1, ("once0", "once1")),
+        (2, ("middle0", "once2")),
+        (3, ("middle1", "once3")),
+        (4, ("home0", "pass0")),
+        (5, ("middle2",)),
+    )
+    for at, names in plan:
+
+        @pl.when(step == at)
+        def _(names=names):
+            for name in names:
+                stages[name]()
+
+    attend_back_step(
+        None, q_ref, k_ref, v_ref, do_ref, o_ref, l_ref, dq_ref, dk_ref, dv_ref
+    )
+
+    @pl.when(step == last)
     def _():
-        back(0, 0, 0).wait_send()
-
-    @pl.when(me < lead - 1)
-    def _():
-        back(1, 1, 0).wait_send()
-
-    trade.wait()
-
-
-def scatter_chunks(grads, rows, plan, inner, collective):
-    anywhere = pl.BlockSpec(memory_space=pl.ANY)
-    dma = pltpu.SemaphoreType.DMA
-    half, levels = plan.devices // 2, inner // 2
-    part = (plan.lent, LANE)
-    return pl.pallas_call(
-        functools.partial(scatter_kernel, plan=plan, inner=inner),
-        in_specs=[anywhere] * 2,
-        out_specs=[anywhere] * 2,
-        out_shape=[
-            jax.ShapeDtypeStruct((plan.padded, LANE), BF),
-            jax.ShapeDtypeStruct((plan.devices, *rows.shape), rows.dtype),
-        ],
-        scratch_shapes=[
-            pltpu.VMEM((half, plan.chunk, LANE), BF),
-            pltpu.VMEM((half, plan.chunk, LANE), BF),
-            pltpu.VMEM((2 * levels, *part), BF),
-            pltpu.VMEM((2 * levels, *part), BF),
-            pltpu.VMEM((levels, *part), BF),
-            pltpu.VMEM((levels, *part), BF),
-            pltpu.VMEM((2, levels, 2, *part), BF),
-            dma((half,)),
-            dma((half,)),
-            dma((half,)),
-            dma((2, 2 * levels)),
-            dma((2, 2 * levels)),
-            dma((2, levels)),
-            dma((2, levels)),
-            dma((2, levels, 2)),
-            dma((2, levels, 2)),
-            dma((2,)),
-            dma((2,)),
-            dma,
-            dma((plan.devices,)),
-            dma((plan.devices,)),
-        ],
-        compiler_params=pltpu.CompilerParams(
-            collective_id=collective, has_side_effects=True, vmem_limit_bytes=VMEM_LIMIT
-        ),
-        name="scatter_chunks",
-    )(grads, rows)
-
-
-def exchange_kernel(in_ref, out_ref, own_sem, send_sem, recv_sem, *, plan, inner):
+        for name in (
+            "middle3", "home1", "pass1", "home2", "pass2", "inner0", "home3", "final"
+        ):
+            stages[name]()
+        deal.start()
+        finish()
+        deal.landed()
+        deal.gone()
+
+
+def back_and_scatter(queries, grad, mixed, lse, chunks, group, inner, collective, pairs=2):
+    clips, frames, wide = queries.shape
+    width = wide // 3
+    count = HEADS // 2 // pairs
+
+    def pair_at(part):
+        return pl.BlockSpec(
+            (1, frames, 2 * HD * pairs), lambda s: (s // count, 0, s % count + part * count)
+        )
+
+    lse_at = pl.BlockSpec((1, pairs, frames, 2 * HD), lambda s: (s // count, s % count, 0, 0))
+    return remote_call(
+        functools.partial(back_kernel, group=group, inner=inner),
+        [pair_at(0), pair_at(1), pair_at(2), pair_at(0), pair_at(0), lse_at, ANYWHERE],
+        [pair_at(0)] * 3 + [ANYWHERE],
+        [struct((clips, frames, width), BF)] * 3 + [struct((group.padded, LANE), BF)],
+        scatter_scratch(group, inner) + Deal.semaphores(group, True),
+        collective,
+        "back_and_scatter",
+        (clips * count,),
+    )(queries, queries, queries, grad, mixed, lse, chunks)
+
+
+def exchange_kernel(in_ref, out_ref, own_sem, send_sem, recv_sem, *, group, inner):
     me = lax.axis_index("dp") * inner + lax.axis_index("fsdp")
-    meet_all(me, plan.devices, inner)
+    meet_all(me, group.devices, inner)
     trade = Trade(
-        in_ref, out_ref, own_sem, send_sem, recv_sem, plan, inner, plan.devices, plan.devices
+        in_ref, out_ref, own_sem, send_sem, recv_sem, group, inner, group.devices, group.devices
     )
     trade.start()
     trade.wait()
 
 
-def exchange(value, plan, inner, collective, name):
-    anywhere = pl.BlockSpec(memory_space=pl.ANY)
+def exchange(value, group, inner, collective, name):
     dma = pltpu.SemaphoreType.DMA
-    return pl.pallas_call(
-        functools.partial(exchange_kernel, plan=plan, inner=inner),
-        in_specs=[anywhere],
-        out_specs=anywhere,
-        out_shape=jax.ShapeDtypeStruct((plan.devices, *value.shape), value.dtype),
-        scratch_shapes=[dma, dma((plan.devices,)), dma((plan.devices,))],
-        compiler_params=pltpu.CompilerParams(collective_id=collective, has_side_effects=True),
-        name=name,
+    return remote_call(
+        functools.partial(exchange_kernel, group=group, inner=inner),
+        [ANYWHERE],
+        ANYWHERE,
+        jax.ShapeDtypeStruct((group.devices, *value.shape), value.dtype),
+        [dma, dma((group.devices,)), dma((group.devices,))],
+        collective,
+        name,
     )(value)
 
 
@@ -1784,8 +2115,8 @@
 CONDITION_ROWS = 832
 
 
-def ada_spots(me, plan):
-    lines = plan.share // HALF
+def ada_spots(me, group):
+    lines = group.share // HALF
     odd = me % 2
     limit = CONDITION_ROWS - TALL
     return [
@@ -1794,15 +2125,15 @@
     ]
 
 
-def ada_kernel(lin_ref, cond_ref, out_ref, *, plan, inner):
+def ada_kernel(lin_ref, cond_ref, out_ref, *, group, inner):
     me = lax.axis_index("dp") * inner + lax.axis_index("fsdp")
-    for half, (shift, top) in enumerate(ada_spots(me, plan)):
+    for half, (shift, top) in enumerate(ada_spots(me, group)):
         condition = cond_ref[pl.ds(top, TALL)].astype(BF)
 
         def body(c, _, half=half, shift=shift, condition=condition):
             rows = lin_ref[pl.ds(HALF * shift + c, TALL, stride=2 * HALF)].astype(BF)
             part = tn(condition, rows)
-            count = plan.devices
+            count = group.devices
             for clip in range(2):
                 out_ref[pl.ds((2 * clip + half) * HALF + c, count, stride=SLAB)] = part[
                     clip * count : (clip + 1) * count
@@ -1812,27 +2143,31 @@
         lax.fori_loop(0, HALF, body, 0, unroll=True)
 
 
-def ada_partial(lin, cond, plan, inner):
+def ada_partial(lin, cond, group, inner):
     return pl.pallas_call(
-        functools.partial(ada_kernel, plan=plan, inner=inner),
-        out_shape=jax.ShapeDtypeStruct((plan.devices * SLAB, LANE), F32),
+        functools.partial(ada_kernel, group=group, inner=inner),
+        out_shape=jax.ShapeDtypeStruct((group.devices * SLAB, LANE), F32),
         compiler_params=pltpu.CompilerParams(vmem_limit_bytes=VMEM_LIMIT),
         name="ada_partial",
     )(lin, cond)
 
 
-def own_grad_kernel(cond_ref, dmod_ref, rest_ref, g_ref, sums_ref, lin, *, plan, inner):
+def own_grad_kernel(cond_ref, dmod_ref, early_ref, late_ref, g_ref, sums_ref, lin, *, group, inner):
     me = lax.axis_index("dp") * inner + lax.axis_index("fsdp")
-    count = plan.devices
-    border = jnp.clip(plan.first_row - plan.share * me, 0, plan.share)
-    for half, (shift, top) in enumerate(ada_spots(me, plan)):
+    count = group.devices // 2
+    border = jnp.clip(group.first - group.share * me, 0, group.share)
+    middle = jnp.clip(group.last - group.share * me, 0, group.share)
+    for half, (shift, top) in enumerate(ada_spots(me, group)):
         condition = cond_ref[pl.ds(top, TALL)].astype(BF)
 
         def body(c, _, half=half, shift=shift, condition=condition):
             grads = jnp.concatenate(
                 [
-                    dmod_ref[pl.ds((2 * clip + half) * HALF + c, count, stride=SLAB)]
+                    dmod_ref[
+                        pl.ds(core * SLAB + (2 * clip + half) * HALF + c, count, stride=2 * SLAB)
+                    ]
                     for clip in range(2)
+                    for core in range(2)
                 ],
                 axis=0,
             ).astype(BF)
@@ -1848,54 +2183,62 @@
     def merge(i, total):
         at = pl.multiple_of(i * rows, rows)
         row = lax.broadcasted_iota(jnp.int32, (rows, LANE), 0) + at
-        rest = jnp.where(row < plan.share, rest_ref[pl.ds(at, rows)].astype(F32), 0.0)
-        value = jnp.where(row < border, lin[pl.ds(at, rows)], rest)
+        early = early_ref[pl.ds(at, rows)].astype(F32)
+        late = jnp.where(row < group.share, late_ref[pl.ds(at, rows)].astype(F32), 0.0)
+        value = jnp.where(
+            row < border, lin[pl.ds(at, rows)], jnp.where(row < middle, early, late)
+        )
         g_ref[pl.ds(at, rows)] = value
         square = value * value
         return total + sum(square[k : k + 8] for k in range(0, rows, 8))
 
-    sums_ref[...] = lax.fori_loop(0, plan.padded // rows, merge, jnp.zeros((8, LANE), F32))
-
-
-def own_grad(cond, dmod, rest, plan, inner):
+    sums_ref[...] = lax.fori_loop(0, group.padded // rows, merge, jnp.zeros((8, LANE), F32))
+
+
+def own_grad(cond, dmod, early, late, group, inner):
     return pl.pallas_call(
-        functools.partial(own_grad_kernel, plan=plan, inner=inner),
+        functools.partial(own_grad_kernel, group=group, inner=inner),
         out_shape=[
-            jax.ShapeDtypeStruct((plan.padded, LANE), F32),
+            jax.ShapeDtypeStruct((group.padded, LANE), F32),
             jax.ShapeDtypeStruct((8, LANE), F32),
         ],
         scratch_shapes=[pltpu.VMEM((2 * HALF * TALL, LANE), F32)],
         compiler_params=pltpu.CompilerParams(vmem_limit_bytes=VMEM_LIMIT),
         name="own_grad",
-    )(cond, dmod, rest)
+    )(cond, dmod, early, late)
 
 
 def fits(devices, inner, share):
     return inner == 8 and devices == 32 and share % (LANE * HALF) == 0
 
 
-def local_fast(
-    latents, captions, lengths, timesteps, cotangent, master, first_moment, second_moment
-):
+def local_fast(latents, captions, lengths, timesteps, cotangent, master):
     clips, frames, width = latents.shape
     share = master.shape[0]
     inner = lax.axis_size("fsdp")
     devices = inner * lax.axis_size("dp")
-    plan = Plan(devices, share // LANE)
-    indices = tuple(range(2, 13))
-
-    rows = master.reshape(plan.share, LANE)
-    lin = jnp.pad(rows, ((0, 2 * HALF * TALL - plan.share), (0, 0)))
+    spots = linear_layout()
+    end = spots[-1][0] + spots[-1][1]
+    early = Group(devices, inner, share // LANE, spots[2][0], spots[3][0])
+    late = Group(devices, inner, share // LANE, spots[3][0], end)
+    holders = spots[2][0] // early.share + 1
+
+    lin = lax.optimization_barrier(
+        jnp.pad(
+            master.reshape(early.share, LANE), ((0, 2 * HALF * TALL - early.share), (0, 0))
+        )
+    )
+    slot = lin[: early.padded].astype(BF)
     steps, chunk = start_chunks(
         jnp.broadcast_to(
             jnp.pad(timesteps.astype(F32), (0, 8 - clips))[:, None], (8, LANE)
         ),
-        lin[: plan.padded].astype(BF),
-        plan,
+        slot,
+        early,
         inner,
         1,
     )
-    steps = steps[:, :clips, 0].T.reshape(devices * clips)
+    steps = steps[:, :clips, 0].reshape(devices // 2, 2, clips).T.reshape(devices * clips)
     columns = jax.nn.silu(embed(steps)).astype(BF).astype(F32).T
     columns = jnp.concatenate(
         [
@@ -1905,33 +2248,52 @@
         ],
         axis=0,
     )
-    slabs = ada_partial(lin, columns, plan, inner).reshape(devices, SLAB, LANE)
-    gathered, parts = gather_chunks(chunk, slabs, plan, inner, 2)
+    slabs = ada_partial(lin, columns, early, inner).reshape(2, devices // 2, SLAB, LANE)
+    gathered, parts, later_chunk = gather_chunks(
+        chunk, slabs, slot, early, late, inner, holders, 2
+    )
     mod = jnp.sum(parts, axis=0)[: 54 * clips].reshape(clips, 9, width)
-    weights = unpack_weights(gathered, plan, indices)
-    output, input_grad, grad_mod, gradients = block_pass(
-        latents, captions, lengths, cotangent, mod, weights
+    (triple_weight,) = unpack_weights(gathered, early, (2,))
+
+    def front(latents, mod, triple_weight):
+        triple, mixed, lse, later = front_and_gather(
+            latents, mod, triple_weight, later_chunk, late, inner, 3
+        )
+        return triple, mixed, lse, unpack_weights(later, late, tuple(range(3, 13)))
+
+    def back(triple, grad_mixed, mixed, lse, gradients):
+        chunks = pack_grads(gradients, late, tuple(range(3, 13)))
+        *grads, rest = back_and_scatter(
+            triple, grad_mixed, mixed, lse, chunks, late, inner, 4
+        )
+        return grads, rest
+
+    output, input_grad, grad_mod, grad_triple, _, late_grads = block_pass(
+        latents, captions, lengths, cotangent, mod, triple_weight, front, back
     )
     grad_rows = jnp.pad(
         grad_mod.reshape(54 * clips, LANE), ((0, SLAB - 54 * clips), (0, 0))
     )
-    chunks = pack_grads(gradients, plan, indices)
-    rest, dmod = scatter_chunks(chunks, grad_rows, plan, inner, 3)
+    chunks = pack_grads([grad_triple], early, (2,))
+    early_grads, dmod = scatter_chunks(chunks, grad_rows, early, inner, holders, 5)
     grads, squares = own_grad(
-        columns, dmod.reshape(devices * SLAB, LANE).astype(F32), rest, plan, inner
-    )
-    squares = exchange(squares, plan, inner, 4, "squares")
+        columns,
+        dmod.reshape(devices * SLAB, LANE).astype(F32),
+        early_grads,
+        late_grads,
+        early,
+        inner,
+    )
+    squares = exchange(squares, early, inner, 6, "squares")
     return (
         output,
         input_grad,
-        grads[: plan.share].reshape(share),
+        grads[: early.share].reshape(share),
         jnp.sum(squares),
     )
 
 
-def local_any(
-    latents, captions, lengths, timesteps, cotangent, master, first_moment, second_moment
-):
+def local_any(latents, captions, lengths, timesteps, cotangent, master):
     clips, frames, width = latents.shape
     share = master.shape[0]
     devices = lax.axis_size("dp") * lax.axis_size("fsdp")
@@ -1942,12 +2304,19 @@
     condition = jax.nn.silu(embed(timesteps)).astype(BF)
     mod = jnp.dot(condition, weights[0], preferred_element_type=F32) + weights[1].astype(F32)
     block_weights = [w.astype(F32).reshape(1, -1) if w.ndim == 1 else w for w in weights[2:]]
-    output, input_grad, grad_mod, gradients = block_pass(
-        latents, captions, lengths, cotangent, mod.reshape(clips, 9, width), block_weights
+    output, input_grad, grad_mod, grad_triple, gradients, _ = block_pass(
+        latents,
+        captions,
+        lengths,
+        cotangent,
+        mod.reshape(clips, 9, width),
+        block_weights[0],
+        functools.partial(plain_front, block_weights[1:]),
+        plain_back,
     )
     grad_mod = grad_mod.reshape(clips, 9 * width)
     grad_ada = jnp.dot(condition.T, grad_mod, preferred_element_type=F32)
-    grad_list = [grad_ada, jnp.sum(grad_mod.astype(F32), axis=0)] + gradients
+    grad_list = [grad_ada, jnp.sum(grad_mod.astype(F32), axis=0), grad_triple] + gradients
     flat = jnp.concatenate([piece.astype(F32).reshape(-1) for piece in grad_list])
     grad = lax.psum_scatter(
         flat.reshape(devices, share), ("dp", "fsdp"), scatter_dimension=0, tiled=True
@@ -1975,8 +2344,6 @@
         timesteps,
         cotangent,
         master_weights,
-        first_moment,
-        second_moment,
     )
     grad_norm = jnp.sqrt(squares)
     clipped = grad_shard * (CLIP / jnp.maximum(grad_norm, CLIP))

time: 639 us -> 575 us (0.90)
  Pallas kernels: 596 us -> 535 us
    pallas_call x2 -> x1, Pallas kernels: 71.4 us -> 20.7 us  [attend_backward(): call(functools.partial(attend_back_kernel, masked=masked), (clips, groups...]
    pallas_call x2 -> x1, Pallas kernels: 45.2 us -> 14.3 us  [attend_forward(): call(functools.partial(attend_kernel, masked=masked), (clips, groups // p...]
    pallas_call x7 -> x8, Pallas kernels: 303 us -> 317 us  [the longest x1 103 us: back_and_scatter(): remote_call(functools.partial(back_kernel, group=group, inner=inner), [pa...]
    pallas_call x1 -> x2, Pallas kernels: 15.6 us -> 18 us  [pack_grads(): pl.pallas_call(functools.partial(pack_kernel, plan=plan, indices=indices,...]
    pallas_call x1 -> x2, Pallas kernels: 16.4 us -> 18.5 us  [unpack_weights(): pl.pallas_call(functools.partial(unpack_kernel, plan=plan, indices=indice...]
where the time goes in v5:
time: 575 us; the launch traced here: 570 us
  Pallas kernels  535 us (93%)
  other arithmetic  15.3 us (3%)
  matrix products  8.49 us (1%)
  local copies, waits for them, and re-layouts  7.56 us (1%)
    pallas_call x1, Pallas kernels, back_and_scatter(): remote_call(functools.partial(back_kernel, group=group, inner=inner), [pa...  103 us
    pallas_call x1, Pallas kernels, front_and_gather(): remote_call(functools.partial(front_kernel, group=group, inner=inner, lea...  79.7 us
    pallas_call x1, Pallas kernels, feed(): call(functools.partial(feed_kernel, clips=clips, frames=frames, rows=rows...  75 us
    pallas_call x1, Pallas kernels, gather_chunks(): remote_call(functools.partial(gather_kernel, group=group, later=later, in...  51.6 us
    pallas_call x1, Pallas kernels, scatter_chunks(): remote_call(functools.partial(scatter_kernel, group=group, inner=inner, r...  42.3 us
    pallas_call x1, Pallas kernels, input_back(): call(input_kernel, (clips, frames // rows), [spec] * 5 + [clip_spec(9, wi...  22.1 us
    pallas_call x1, Pallas kernels, attend_backward(): call(functools.partial(attend_back_kernel, masked=masked), (clips, groups...  20.7 us
    pallas_call x1, Pallas kernels, before_self(): call(before_self_kernel, (clips, frames // rows), [spec, spec, spec, spec...  20.2 us

profile of v5, /device:TPU:0, one launch (start us, length us, event | category | flops | bytes accessed | tf_op | source)
XLA Modules:
  0.0 569.9 jit_solution(4348233074632127067)
XLA Ops:
  0.6 1.2 copy-done
  3.3 1.6 pad.13.lin_ref
  5.0 1.1 slice.37.slot_ref
  6.1 17.3 %start_chunks.1 = (f32[32,8,128]{2,1,0:T(8,128)}, bf16[448,128]{1,0:T(8,128)(2,1)}) custom-call(f32[8,128]{1,0:T(8,128)} %broadcast_in_dim.6.step_ref, bf16[3712,128]{1,0:T(8,128)(2,1)} %slice.37.slot_ref), custom_call_target="tpu_custom_call" | custom-call | tf_op jit(solution)/shard_map/start_chunks/pallas_call | solution.py:1352
  23.4 0.9 slice.22
  24.7 0.8 multiply_cosine_fusion
  25.6 1.1 maximum_maximum_fusion.cond_ref
  26.6 3.6 ada_partial.1
  30.3 51.6 %gather_chunks.1 = (bf16[32,448,128]{2,1,0:T(8,128)(2,1)}, f32[6,112,128]{2,1,0:T(8,128)}, bf16[1984,128]{1,0:T(8,128)(2,1)}) custom-call(bf16[448,128]{1,0:T(8,128)(2,1)} %get-tuple-element.63.chunk_ref, f32[2,16,112,128]{3,2,1,0:T(8,128)} %bitcast.38, bf16[3712,128]{1,0:T(8,128)(2,1)} %slice.37.slot_ref), custom_call_target="tpu_custom_call" | custom-call | tf_op jit(solution)/shard_map/gather_chunks/pallas_call | solution.py:1576
  81.9 1.0 reduce_sum.18
  83.6 4.8 unpack.2.w_ref
  88.4 79.7 %front_and_gather.1 = (bf16[2,864,2304]{2,1,0:T(8,128)(2,1)}, bf16[2,864,768]{2,1,0:T(8,128)(2,1)}, f32[2,6,864,128]{3,2,1,0:T(8,128)}, bf16[32,1984,128]{2,1,0:T(8,128)(2,1)}) custom-call(bf16[2,864,768]{2,1,0:T(8,128)(2,1)} %x_ref.5, f32[2,9,768]{2,1,0:T(8,128)} %reshape.46.mod_ref, bf16[768,2304]{1,0:T(8,128)(2,1)} %unpack.2.w_ref, ...), custom_call_target="tpu_custom_call" | custom-call | tf_op jit(solution)/shard_map/front_and_gather/pallas_call | solution.py:1990
  168.1 13.7 %unpack.3 = (bf16[768,768]{1,0:T(8,128)(2,1)}, f32[1,768]{1,0:T(1,128)}, bf16[768,768]{1,0:T(8,128)(2,1)}, bf16[1024,1536]{1,0:T(8,128)(2,1)}, bf16[768,768]{1,0...) custom-call(bf16[32,1984,128]{2,1,0:T(8,128)(2,1)} %get-tuple-elemen, ...), custom_call_target="tpu_custom_call" | custom-call | tf_op jit(solution)/shard_map/unpack/pallas_call | solution.py:1025
  181.8 4.8 convolution_convert_fusion
  186.6 10.8 %after_self.1 = (bf16[2,864,768]{2,1,0:T(8,128)(2,1)}, f32[2,864,768]{2,1,0:T(8,128)}, bf16[2,864,768]{2,1,0:T(8,128)(2,1)}) custom-call(bf16[2,864,768]{2,1,0:T(8,128)(2,1)} %get-tuple-element.68.o_ref, bf16[2,864,768]{2,1,0:T(8,128)(2,1)} %x_ref.5, f32[2,9,768]{2,1,0:T(8,128)} %reshape.46.mod_ref, bf16[768,768]{1,0:T(8,128)(2,1)} %get-tuple-element.70.wo_ref, ...), custom_call_target="tpu_custom_call" | custom-call | tf_op jit(solution)/shard_map/after_self/pallas_call | solution.py:400
  197.4 14.3 %cross_forward.1 = (bf16[2,864,768]{2,1,0:T(8,128)(2,1)}, f32[2,6,864,128]{3,2,1,0:T(8,128)}) custom-call(s32[2]{0:T(128)} %refs_0_.3, bf16[2,864,768]{2,1,0:T(8,128)(2,1)} %get-tuple-element.73.refs_1_, bf16[2,256,1536]{2,1,0:T(8,128)(2,1)} %bitcast.33, bf16[2,256,1536]{2,1,0:T(8,128)(2,1)} %bitcast.34), custom_call_target="tpu_custom_call" | custom-call | tf_op jit(solution)/shard_map/cross_forward/pallas_call | solution.py:260
  211.7 8.6 %after_cross.1 = (bf16[2,864,768]{2,1,0:T(8,128)(2,1)}, f32[2,864,768]{2,1,0:T(8,128)}) custom-call(bf16[2,864,768]{2,1,0:T(8,128)(2,1)} %get-tuple-element.75.o_ref.refs_5_, f32[2,864,768]{2,1,0:T(8,128)} %get-tuple-element.76.h_ref, f32[2,9,768]{2,1,0:T(8,128)} %reshape.46.mod_ref, bf16[768,768]{1,0:T(8,128)(2,1)} %get-tuple-element.77.wo_ref.w_ref, ...), custom_call_target="tpu_custom_call" | custom-call | tf_op jit(solution)/shard_map/after_cross/pallas_call | solution.py:424
  220.3 75.0 %feed.1 = (bf16[2,864,768]{2,1,0:T(8,128)(2,1)}, f32[2,864,768]{2,1,0:T(8,128)}, bf16[768,3072]{1,0:T(8,128)(2,1)}, bf16[3072,768]{1,0:T(8,128)(2,1)}, f32[1,307...) custom-call(f32[2,864,768]{2,1,0:T(8,128)} %get-tuple-element.79.h_ref, bf16[2,864,768]{2,1,0:T(8,128)(2,1)} %dy_ref.1, ...), custom_call_target="tpu_custom_call" | custom-call | tf_op jit(solution)/shard_map/feed/pallas_call | solution.py:569
  295.3 10.7 %before_cross.1 = (bf16[2,864,768]{2,1,0:T(8,128)(2,1)}, bf16[768,768]{1,0:T(8,128)(2,1)}, f32[1,768]{1,0:T(1,128)}, f32[2,1,768]{2,1,0:T(1,128)}) custom-call(f32[2,864,768]{2,1,0:T(8,128)} %get-tuple-element.86.dh_ref, bf16[2,864,768]{2,1,0:T(8,128)(2,1)} %get-tuple-element.87.z_ref, bf16[2,864,768]{2,1,0:T(8,128)(2,1)} %get-tuple-element.75.o_ref.refs_5_, ...), custom_call_target="tpu_custom_call" | custom-call | tf_op jit(solution)/shard_map/before_cross/pallas_call | solution.py:644
  306.0 20.7 %cross_back.1 = (bf16[2,864,768]{2,1,0:T(8,128)(2,1)}, bf16[2,256,768]{2,1,0:T(8,128)(2,1)}, bf16[2,256,768]{2,1,0:T(8,128)(2,1)}) custom-call(s32[2]{0:T(128)} %refs_0_.3, bf16[2,864,768]{2,1,0:T(8,128)(2,1)} %get-tuple-element.73.refs_1_, bf16[2,256,1536]{2,1,0:T(8,128)(2,1)} %bitcast.35, bf16[2,256,1536]{2,1,0:T(8,128)(2,1)} %bitcast.36, ...), custom_call_target="tpu_custom_call" | custom-call | tf_op jit(solution)/shard_map/cross_back/pallas_call | solution.py:371
  326.7 20.2 %before_self.1 = (f32[2,864,768]{2,1,0:T(8,128)}, bf16[2,864,768]{2,1,0:T(8,128)(2,1)}, bf16[768,768]{1,0:T(8,128)(2,1)}, bf16[768,768]{1,0:T(8,128)(2,1)}, f32[1,768]{1,0:T(1,128)}, /*index=5*/f32[2,3,768]{2,1,0:T(4,128)}) custom-call(bf16[2,864,768]{2,1,0:T(8,128)(2,1)} %get-tuple-element.90.dq_ref, f32[2,864,768]{2,1,0:T(8,128)} %get-tuple-element.76.h_ref, ...), custom_call_target="tpu_custom_call" | custom-call | tf_op jit(solution)/shard_map/before_self/pallas_call | solution.py:716
  347.8 3.7 fusion.refs_3_
  351.4 13.4 %pack.2.g_ref = bf16[32,1984,128]{2,1,0:T(8,128)(2,1)} custom-call(bf16[768,768]{1,0:T(8,128)(2,1)} %get-tuple-element.94.refs_0_, f32[1,768]{1,0:T(1,128)} %get-tuple-element.95.refs_1_, bf16[768,768]{1,0:T(8,128)(2,1)} %get-tuple-element.96.refs_2_, bf16[1024,1536]{1,0:T(8,128)(2,1)} %fusion.refs_3_, bf16[768,768]{1,0:T(8,128)(2,1)} %get-tuple-element.99.refs_4_, ...), custom_call_target="tpu_custom_call" | custom-call | tf_op jit(solution)/shard_map/pack/pallas_call | solution.py:1133
  364.8 103.3 %back_and_scatter.1 = (bf16[2,864,768]{2,1,0:T(8,128)(2,1)}, bf16[2,864,768]{2,1,0:T(8,128)(2,1)}, bf16[2,864,768]{2,1,0:T(8,128)(2,1)}, bf16[3712,128]{1,0:T(8,128)(2,1)}) custom-call(bf16[2,864,2304]{2,1,0:T(8,128)(2,1)} %get-tuple-element.85.q_ref.k_ref.v_ref, bf16[2,864,2304]{2,1,0:T(8,128)(2,1)} %get-tuple-element.85.q_ref.k_ref.v_ref, ...), custom_call_target="tpu_custom_call" | custom-call | tf_op jit(solution)/shard_map/back_and_scatter/pallas_call | solution.py:2077
  468.2 22.1 %input_back.1 = (bf16[2,864,768]{2,1,0:T(8,128)(2,1)}, bf16[768,2304]{1,0:T(8,128)(2,1)}, f32[2,2,768]{2,1,0:T(2,128)}) custom-call(bf16[2,864,768]{2,1,0:T(8,128)(2,1)} %get-tuple-element.105.dq_ref, bf16[2,864,768]{2,1,0:T(8,128)(2,1)} %get-tuple-element.106.dk_ref, bf16[2,864,768]{2,1,0:T(8,128)(2,1)} %get-tuple-element.107.dv_ref, ...), custom_call_target="tpu_custom_call" | custom-call | tf_op jit(solution)/shard_map/input_back/pallas_call | solution.py:769
  491.9 4.6 pack.3.g_ref
  496.5 42.3 %scatter_chunks.1 = (bf16[3712,128]{1,0:T(8,128)(2,1)}, bf16[32,112,128]{2,1,0:T(8,128)(2,1)}) custom-call(bf16[32,448,128]{2,1,0:T(8,128)(2,1)} %pack.3.g_ref, bf16[112,128]{1,0:T(8,128)(2,1)} %pad.14.rows_ref), custom_call_target="tpu_custom_call" | custom-call | tf_op jit(solution)/shard_map/scatter_chunks/pallas_call | solution.py:1900
  538.8 2.5 bitcast_convert_fusion.1.dmod_ref
  541.3 6.2 %own_grad.1 = (f32[3712,128]{1,0:T(8,128)}, f32[8,128]{1,0:T(8,128)}) custom-call(f32[832,64]{1,0:T(8,128)} %maximum_maximum_fusion.cond_ref, f32[3584,128]{1,0:T(8,128)} %bitcast_convert_fusion.1.dmod_ref, bf16[3712,128]{1,0:T(8,128)(2,1)} %get-tuple-element.116.early_ref, bf16[3712,128]{1,0:T(8,128)(2,1)} %get-tuple-element.117.late_ref), custom_call_target="tpu_custom_call" | custom-call | tf_op jit(solution)/shard_map/own_grad/pallas_call | solution.py:2199
  547.6 12.5 %squares.1 = f32[32,8,128]{2,1,0:T(8,128)} custom-call(f32[8,128]{1,0:T(8,128)} %get-tuple-element.118.in_ref), custom_call_target="tpu_custom_call" | custom-call | tf_op jit(solution)/shard_map/squares/pallas_call | solution.py:2101
  560.1 1.5 reduce_sum.19
  562.4 6.2 %multiply_subtract_fusion = (f32[473472]{0:T(1024)}, f32[473472]{0:T(1024)}, f32[473472]{0:T(1024)}) fusion(f32[473472]{0:T(1024)S(1)} %copy-done.3, f32[]{:T(128)S(6)} %div.31, f32[3712,128]{1,0:T(8,128)} %get-tuple-element.119, f32[473472]{0:T(1024)} %param.14, f32[473472]{0:T(1024)} %param.15), kind=kLoop, calls=%fused_computation.8 | loop fusion | flops 7575552 | bytes 13257220 | tf_op jit(solution)/shard_map/sub | solution.py:2354
  (40 shorter events, 4.9 us)
Async XLA Ops:
  0.6 1.2 copy-start
  4.9 20.6 %copy-start.2 = (f32[3888,128]{1,0:T(8,128)}, f32[3888,128]{1,0:T(8,128)S(1)}, u32[]{:S(2)}) copy-start(f32[3888,128]{1,0:T(8,128)S(1)} %pad.13.lin_ref) | copy-start | bytes 5971972
  326.7 20.3 %copy-start.6 = (f32[2,1,768]{2,1,0:T(1,128)S(1)}, f32[2,1,768]{2,1,0:T(1,128)}, u32[]{:S(2)}) copy-start(f32[2,1,768]{2,1,0:T(1,128)} %get-tuple-element.113) | copy-start | bytes 18436
  326.7 21.0 %copy-start.5 = (f32[2,3,768]{2,1,0:T(4,128)S(1)}, f32[2,3,768]{2,1,0:T(4,128)}, u32[]{:S(2)}) copy-start(f32[2,3,768]{2,1,0:T(4,128)} %get-tuple-element.114) | copy-start | bytes 55300
  326.7 21.1 %copy-start.7 = (bf16[2,256,768]{2,1,0:T(8,128)(2,1)S(1)}, bf16[2,256,768]{2,1,0:T(8,128)(2,1)}, u32[]{:S(2)}) copy-start(bf16[2,256,768]{2,1,0:T(8,128)(2,1)} %get-tuple-element.97) | copy-start | bytes 2359300
  326.7 21.1 %copy-start.8 = (bf16[2,256,768]{2,1,0:T(8,128)(2,1)S(1)}, bf16[2,256,768]{2,1,0:T(8,128)(2,1)}, u32[]{:S(2)}) copy-start(bf16[2,256,768]{2,1,0:T(8,128)(2,1)} %get-tuple-element.98) | copy-start | bytes 2359300
  347.7 3.7 copy-start.4
  468.2 22.8 %slice-start = ((bf16[2,3,768]{2,1,0:T(4,128)(2,1)}), bf16[2,2,768]{2,1,0:T(2,128)(2,1)S(1)}, s32[]{:S(2)}) async-start(bf16[2,3,768]{2,1,0:T(4,128)(2,1)} %copy-done.4), calls=%async_computation | async-start | bytes 12288 | tf_op jit(solution)/shard_map/slice | solution.py:853
  541.3 21.0 %copy-start.3 = (f32[473472]{0:T(1024)S(1)}, f32[473472]{0:T(1024)}, u32[]{:S(2)}) copy-start(f32[473472]{0:T(1024)} %param.13) | copy-start | bytes 5681668
  562.4 6.2 %copy-start.1 = (bf16[2,256,1024]{2,1,0:T(8,128)(2,1)S(1)}, bf16[2,256,1024]{2,1,0:T(8,128)(2,1)}, u32[]{:S(2)}) copy-start(bf16[2,256,1024]{2,1,0:T(8,128)(2,1)} %param.9) | copy-start | bytes 3145732

commit v6 on v5

--- a/solution.py
+++ b/solution.py
@@ -847,8 +847,9 @@
         grad_down,
         grad_down_bias,
     ]
-    grads_one, rest = back(triple, grad_mixed_one, mixed_one, lse_one, gradients)
-    input_grad, grad_triple, sums_one = input_back(grads_one, latents, dh_one, mod, triple_weight)
+    input_grad, grad_triple, sums_one, rest = back(
+        triple, grad_mixed_one, mixed_one, lse_one, latents, dh_one, mod, triple_weight, gradients
+    )
     grad_mod = jnp.concatenate(
         [sums_one, sums_two[:, 2:], sums_two[:, :2], gate_two, sums_three], axis=1
     ).astype(BF)
@@ -862,12 +863,12 @@
     return triple, mixed, lse, weights
 
 
-def plain_back(triple, grad_mixed, mixed, lse, gradients):
+def plain_back(triple, grad_mixed, mixed, lse, latents, dh, mod, triple_weight, gradients):
     groups = HEADS // 2
     grads = attend_backward(
         triple, groups, triple, 2 * groups, None, grad_mixed, mixed, lse, "self_back", 2
     )
-    return grads, None
+    return *input_back(grads, latents, dh, mod, triple_weight), None
 
 
 LANE = 128
@@ -1471,6 +1472,107 @@
         self.own.wait()
 
 
+class ShortGather:
+    def __init__(self, group, inner, chunk_ref, out_ref, own_sem, send_sem, recv_sem):
+        self.group, self.inner = group, inner
+        self.chunk_ref, self.out_ref = chunk_ref, out_ref
+        self.send_sem, self.recv_sem = send_sem, recv_sem
+        dp, fs, self.y, self.x, self.z, self.c = place_of()
+        self.levels = inner // 2
+        self.own = pltpu.make_async_copy(chunk_ref, out_ref.at[dp * inner + fs], own_sem)
+        self.across = {
+            "z1": (dp, self.level(-1) * 2 + self.c),
+            "z2": (dp, self.level(-2) * 2 + self.c),
+            "z3": (dp, self.level(-3) * 2 + self.c),
+            "x": (dp + 1 - 2 * self.x, fs),
+            "y": (dp + 2 - 4 * self.y, fs),
+            "twin": (dp, fs + 1 - 2 * self.c),
+        }
+        self.kinds = tuple(self.across)
+        self.closing = False
+
+    @staticmethod
+    def semaphores(group):
+        dma = pltpu.SemaphoreType.DMA
+        return [dma, dma((6, group.devices // 2, 2)), dma((group.devices, 2))]
+
+    def copy(self, kind, yy, xx, zz, part, cc=None, mine=False):
+        core = self.c if cc is None else cc
+        column = yy * 2 + xx
+        index = column * self.inner + zz * 2 + core
+        rows = pl.ds(part * self.group.half, self.group.half)
+        return pltpu.make_async_remote_copy(
+            src_ref=self.chunk_ref.at[rows] if mine else self.out_ref.at[index, rows],
+            dst_ref=self.out_ref.at[index, rows],
+            send_sem=self.send_sem.at[
+                self.kinds.index(kind), column * self.levels + zz, part
+            ],
+            recv_sem=self.recv_sem.at[index, part],
+            device_id=self.across[kind],
+            device_id_type=MESH,
+        )
+
+    def level(self, back):
+        return (self.z - back + self.levels) % self.levels
+
+    def send(self, kind, yy, xx, zz, part, mine=False):
+        copy = self.copy(kind, yy, xx, zz, part, mine=mine)
+        if self.closing:
+            copy.wait_send()
+        else:
+            copy.start()
+
+    def arrive(self, yy, xx, zz, part):
+        if not self.closing:
+            self.copy("x", yy, xx, zz, part).wait_recv()
+
+    def turn(self, turn):
+        y, x, levels = self.y, self.x, self.levels
+        if turn == 0 and not self.closing:
+            self.own.start()
+        if turn < levels:
+            zz = self.level(turn)
+            for part in range(2):
+                if turn:
+                    self.arrive(y, x, zz, part)
+                for kind in ("x", "y") if part else ("y", "x"):
+                    self.send(kind, y, x, zz, part, turn == 0)
+                if turn == 0:
+                    for kind in ("z1", "z2", "z3"):
+                        self.send(kind, y, x, zz, part, True)
+                self.send("twin", y, x, zz, part, turn == 0)
+        if 1 <= turn <= levels:
+            zz = self.level(turn - 1)
+            self.arrive(y, 1 - x, zz, 0)
+            self.send("y", y, 1 - x, zz, 0)
+            self.send("twin", y, 1 - x, zz, 0)
+            self.arrive(1 - y, x, zz, 1)
+            self.send("x", 1 - y, x, zz, 1)
+            self.send("twin", 1 - y, x, zz, 1)
+            self.arrive(1 - y, x, zz, 0)
+            self.send("twin", 1 - y, x, zz, 0)
+            self.arrive(y, 1 - x, zz, 1)
+            self.send("twin", y, 1 - x, zz, 1)
+        if turn >= 2:
+            zz = self.level(turn - 2)
+            for part in range(2):
+                self.arrive(1 - y, 1 - x, zz, part)
+                self.send("twin", 1 - y, 1 - x, zz, part)
+
+    def finish(self):
+        def twin_arrivals(i, _):
+            column, zz = i // self.levels, i % self.levels
+            for part in range(2):
+                self.copy("twin", column // 2, column % 2, zz, part, 1 - self.c).wait_recv()
+            return 0
+
+        lax.fori_loop(0, 4 * self.levels, twin_arrivals, 0)
+        self.closing = True
+        for turn in range(self.levels + 2):
+            self.turn(turn)
+        self.own.wait()
+
+
 class PairTrade:
     def __init__(self, slab_ref, out_ref, mine, theirs, sems, inner, devices):
         self.slab_ref, self.out_ref, self.mine, self.theirs = slab_ref, out_ref, mine, theirs
@@ -1556,7 +1658,7 @@
     me = lax.axis_index("dp") * inner + lax.axis_index("fsdp")
     meet_all(me, group.devices, inner)
     trade = PairTrade(slab_ref, parts_ref, mine, theirs, sems[:3], inner, group.devices)
-    gather = Gather(group, inner, chunk_ref, out_ref, *sems[3:6])
+    gather = ShortGather(group, inner, chunk_ref, out_ref, *sems[3:6])
     deal = Deal(later, slot_ref, next_ref, *sems[6:], inner, False)
     trade.begin()
     gather.turn(0)
@@ -1589,7 +1691,7 @@
             dma((group.devices // 2,)),
             dma((group.devices // 2,)),
         ]
-        + Gather.semaphores(group)
+        + ShortGather.semaphores(group)
         + Deal.semaphores(later, False),
         collective,
         "gather_chunks",
@@ -2019,11 +2121,15 @@
 
 
 def back_kernel(
-    q_ref, k_ref, v_ref, do_ref, o_ref, l_ref, g_ref, dq_ref, dk_ref, dv_ref, rest_ref, *scratch,
-    group, inner
+    q_ref, k_ref, v_ref, do_ref, o_ref, l_ref, x_ref, dh_ref, mod_ref, w_ref, g_ref,
+    out_ref, dw_ref, sums_ref, rest_ref, grad_s, in_s, *scratch,
+    group, inner, pairs, period
 ):
     step = pl.program_id(0)
     last = pl.num_programs(0) - 1
+    clip, turn = step // period, step % period
+    width = x_ref.shape[2]
+    rows = x_ref.shape[1]
     stages, finish, total = scatter_stages(group, inner, g_ref, *scratch[:-2])
     deal = Deal(group, total, rest_ref, *scratch[-2:], inner, True)
     me = lax.axis_index("dp") * inner + lax.axis_index("fsdp")
@@ -2035,10 +2141,14 @@
     plan = (
         (0, ("begin",)),
         (1, ("once0", "once1")),
-        (2, ("middle0", "once2")),
-        (3, ("middle1", "once3")),
-        (4, ("home0", "pass0")),
-        (5, ("middle2",)),
+        (3, ("middle0", "once2")),
+        (5, ("middle1", "once3")),
+        (7, ("home0", "pass0")),
+        (8, ("middle2",)),
+        (11, ("middle3",)),
+        (12, ("home1", "pass1")),
+        (14, ("home2", "pass2")),
+        (16, ("inner0",)),
     )
     for at, names in plan:
 
@@ -2047,15 +2157,66 @@
             for name in names:
                 stages[name]()
 
-    attend_back_step(
-        None, q_ref, k_ref, v_ref, do_ref, o_ref, l_ref, dq_ref, dk_ref, dv_ref
-    )
+    @pl.when(turn < pairs)
+    def _():
+        lane, low = head_lanes()
+
+        def columns(part):
+            at = pl.multiple_of(turn * 2 * HD, 2 * HD)
+            return grad_s.at[:, pl.ds(part * width + at, 2 * HD)]
+
+        attend_back_pair(
+            lane,
+            low,
+            None,
+            q_ref[0],
+            k_ref[0],
+            v_ref[0],
+            do_ref[0],
+            o_ref[0],
+            l_ref[0, 0],
+            columns(0),
+            columns(1),
+            columns(2),
+        )
+
+    clear_at(turn == pairs, sums_ref)
+
+    @pl.when(turn >= pairs)
+    def _():
+        here = pl.ds(pl.multiple_of((turn - pairs) * rows, rows), rows)
+        normed, inverse = normalize(x_ref[0].astype(F32))
+        in_s[here] = (normed * (1.0 + mod_ref[0, 1:2]) + mod_ref[0, 0:1]).astype(BF)
+        grad_in = None
+        for index in range(3):
+            part = slice(index * width, (index + 1) * width)
+            product = nt(grad_s[here, part], w_ref[:, part])
+            grad_in = product if grad_in is None else grad_in + product
+        out_ref[0] = (
+            dh_ref[0] + norm_back(normed, inverse, grad_in * (1.0 + mod_ref[0, 1:2]))
+        ).astype(BF)
+        sums_ref[0] += jnp.concatenate(
+            [column_sum(grad_in), column_sum(grad_in * normed)], axis=0
+        )
+
+    @pl.when(turn == period - 1)
+    def _():
+        turned = in_s[...].T
+        for index in range(3):
+            part = slice(index * width, (index + 1) * width)
+            product = nn(turned, grad_s[:, part])
+
+            @pl.when(clip == 0)
+            def _(product=product, part=part):
+                dw_ref[:, part] = product.astype(BF)
+
+            @pl.when(clip > 0)
+            def _(product=product, part=part):
+                dw_ref[:, part] = (dw_ref[:, part].astype(F32) + product).astype(BF)
 
     @pl.when(step == last)
     def _():
-        for name in (
-            "middle3", "home1", "pass1", "home2", "pass2", "inner0", "home3", "final"
-        ):
+        for name in ("home3", "final"):
             stages[name]()
         deal.start()
         finish()
@@ -2063,27 +2224,62 @@
         deal.gone()
 
 
-def back_and_scatter(queries, grad, mixed, lse, chunks, group, inner, collective, pairs=2):
+def back_and_scatter(
+    queries, grad, mixed, lse, latents, dh, mod, weight, chunks, group, inner, collective
+):
     clips, frames, wide = queries.shape
     width = wide // 3
-    count = HEADS // 2 // pairs
+    pairs = HEADS // 2
+    rows = frames // 3
+    period = pairs + frames // rows
 
     def pair_at(part):
         return pl.BlockSpec(
-            (1, frames, 2 * HD * pairs), lambda s: (s // count, 0, s % count + part * count)
-        )
-
-    lse_at = pl.BlockSpec((1, pairs, frames, 2 * HD), lambda s: (s // count, s % count, 0, 0))
+            (1, frames, 2 * HD),
+            lambda s: (s // period, 0, jnp.minimum(s % period, pairs - 1) + part * pairs),
+        )
+
+    lse_at = pl.BlockSpec(
+        (1, 1, frames, 2 * HD),
+        lambda s: (s // period, jnp.minimum(s % period, pairs - 1), 0, 0),
+    )
+    rows_at = pl.BlockSpec(
+        (1, rows, width), lambda s: (s // period, jnp.maximum(s % period - pairs, 0), 0)
+    )
+
+    def clip_at(count):
+        return pl.BlockSpec((1, count, width), lambda s: (s // period, 0, 0))
+
+    whole = pl.BlockSpec(weight.shape, lambda s: (0, 0), pipeline_mode=pl.Buffered(1))
     return remote_call(
-        functools.partial(back_kernel, group=group, inner=inner),
-        [pair_at(0), pair_at(1), pair_at(2), pair_at(0), pair_at(0), lse_at, ANYWHERE],
-        [pair_at(0)] * 3 + [ANYWHERE],
-        [struct((clips, frames, width), BF)] * 3 + [struct((group.padded, LANE), BF)],
-        scatter_scratch(group, inner) + Deal.semaphores(group, True),
+        functools.partial(back_kernel, group=group, inner=inner, pairs=pairs, period=period),
+        [
+            pair_at(0),
+            pair_at(1),
+            pair_at(2),
+            pair_at(0),
+            pair_at(0),
+            lse_at,
+            rows_at,
+            rows_at,
+            clip_at(9),
+            whole,
+            ANYWHERE,
+        ],
+        [rows_at, whole, clip_at(2), ANYWHERE],
+        [
+            struct((clips, frames, width), BF),
+            struct(weight.shape, BF),
+            struct((clips, 2, width), F32),
+            struct((group.padded, LANE), BF),
+        ],
+        [pltpu.VMEM((frames, wide), BF), pltpu.VMEM((frames, width), BF)]
+        + scatter_scratch(group, inner)
+        + Deal.semaphores(group, True),
         collective,
         "back_and_scatter",
-        (clips * count,),
-    )(queries, queries, queries, grad, mixed, lse, chunks)
+        (clips * period,),
+    )(queries, queries, queries, grad, mixed, lse, latents, dh, mod, weight, chunks)
 
 
 def exchange_kernel(in_ref, out_ref, own_sem, send_sem, recv_sem, *, group, inner):
@@ -2152,11 +2348,18 @@
     )(lin, cond)
 
 
-def own_grad_kernel(cond_ref, dmod_ref, early_ref, late_ref, g_ref, sums_ref, lin, *, group, inner):
+def own_grad_kernel(
+    cond_ref, given_ref, early_ref, late_ref, g_ref, sums_ref, lin, dmod_ref, *, group, inner
+):
     me = lax.axis_index("dp") * inner + lax.axis_index("fsdp")
     count = group.devices // 2
     border = jnp.clip(group.first - group.share * me, 0, group.share)
     middle = jnp.clip(group.last - group.share * me, 0, group.share)
+
+    @pl.when(border > 0)
+    def _():
+        dmod_ref[...] = given_ref[...].astype(F32)
+
     for half, (shift, top) in enumerate(ada_spots(me, group)):
         condition = cond_ref[pl.ds(top, TALL)].astype(BF)
 
@@ -2202,7 +2405,10 @@
             jax.ShapeDtypeStruct((group.padded, LANE), F32),
             jax.ShapeDtypeStruct((8, LANE), F32),
         ],
-        scratch_shapes=[pltpu.VMEM((2 * HALF * TALL, LANE), F32)],
+        scratch_shapes=[
+            pltpu.VMEM((2 * HALF * TALL, LANE), F32),
+            pltpu.VMEM(dmod.shape, F32),
+        ],
         compiler_params=pltpu.CompilerParams(vmem_limit_bytes=VMEM_LIMIT),
         name="own_grad",
     )(cond, dmod, early, late)
@@ -2261,12 +2467,22 @@
         )
         return triple, mixed, lse, unpack_weights(later, late, tuple(range(3, 13)))
 
-    def back(triple, grad_mixed, mixed, lse, gradients):
+    def back(triple, grad_mixed, mixed, lse, latents, dh, mod, triple_weight, gradients):
         chunks = pack_grads(gradients, late, tuple(range(3, 13)))
-        *grads, rest = back_and_scatter(
-            triple, grad_mixed, mixed, lse, chunks, late, inner, 4
-        )
-        return grads, rest
+        return back_and_scatter(
+            triple,
+            grad_mixed,
+            mixed,
+            lse,
+            latents,
+            dh,
+            mod,
+            triple_weight,
+            chunks,
+            late,
+            inner,
+            4,
+        )
 
     output, input_grad, grad_mod, grad_triple, _, late_grads = block_pass(
         latents, captions, lengths, cotangent, mod, triple_weight, front, back
@@ -2278,7 +2494,7 @@
     early_grads, dmod = scatter_chunks(chunks, grad_rows, early, inner, holders, 5)
     grads, squares = own_grad(
         columns,
-        dmod.reshape(devices * SLAB, LANE).astype(F32),
+        dmod.reshape(devices * SLAB, LANE),
         early_grads,
         late_grads,
         early,

time: 575 us -> 558 us (0.970)
  Pallas kernels: 535 us -> 519 us
    pallas_call x2 -> x1, Pallas kernels: 125 us -> 111 us  [back_and_scatter(): remote_call(functools.partial(back_kernel, group=group, inner=inner, pair...]
where the time goes in v6:
time: 558 us; the launch traced here: 554 us
  Pallas kernels  519 us (93%)
  other arithmetic  12.9 us (2%)
  local copies, waits for them, and re-layouts  9.52 us (2%)
  matrix products  8.49 us (2%)
    pallas_call x1, Pallas kernels, back_and_scatter(): remote_call(functools.partial(back_kernel, group=group, inner=inner, pair...  111 us
    pallas_call x1, Pallas kernels, front_and_gather(): remote_call(functools.partial(front_kernel, group=group, inner=inner, lea...  79.6 us
    pallas_call x1, Pallas kernels, feed(): call(functools.partial(feed_kernel, clips=clips, frames=frames, rows=rows...  75 us
    pallas_call x1, Pallas kernels, gather_chunks(): remote_call(functools.partial(gather_kernel, group=group, later=later, in...  48.5 us
    pallas_call x1, Pallas kernels, scatter_chunks(): remote_call(functools.partial(scatter_kernel, group=group, inner=inner, r...  44 us
    pallas_call x1, Pallas kernels, attend_backward(): call(functools.partial(attend_back_kernel, masked=masked), (clips, groups...  20.7 us
    pallas_call x1, Pallas kernels, before_self(): call(before_self_kernel, (clips, frames // rows), [spec, spec, spec, spec...  20.2 us
    pallas_call x2, Pallas kernels, unpack_weights(): pl.pallas_call(functools.partial(unpack_kernel, plan=plan, indices=indice...  18.5 us

profile of v6, /device:TPU:0, one launch (start us, length us, event | category | flops | bytes accessed | tf_op | source)
XLA Modules:
  0.0 553.5 jit_solution(1164265514677784985)
XLA Ops:
  0.6 1.2 copy-done
  3.3 1.6 pad.13.lin_ref
  5.0 1.1 slice.37.slot_ref
  6.1 17.3 %start_chunks.1 = (f32[32,8,128]{2,1,0:T(8,128)}, bf16[448,128]{1,0:T(8,128)(2,1)}) custom-call(f32[8,128]{1,0:T(8,128)} %broadcast_in_dim.6.step_ref, bf16[3712,128]{1,0:T(8,128)(2,1)} %slice.37.slot_ref), custom_call_target="tpu_custom_call" | custom-call | tf_op jit(solution)/shard_map/start_chunks/pallas_call | solution.py:1353
  23.4 0.9 slice.22
  24.7 0.8 multiply_cosine_fusion
  25.6 1.1 maximum_maximum_fusion.cond_ref
  26.6 3.6 ada_partial.1
  30.3 48.5 %gather_chunks.1 = (bf16[32,448,128]{2,1,0:T(8,128)(2,1)}, f32[6,112,128]{2,1,0:T(8,128)}, bf16[1984,128]{1,0:T(8,128)(2,1)}) custom-call(bf16[448,128]{1,0:T(8,128)(2,1)} %get-tuple-element.60.chunk_ref, f32[2,16,112,128]{3,2,1,0:T(8,128)} %bitcast.36, bf16[3712,128]{1,0:T(8,128)(2,1)} %slice.37.slot_ref), custom_call_target="tpu_custom_call" | custom-call | tf_op jit(solution)/shard_map/gather_chunks/pallas_call | solution.py:1678
  78.8 1.0 reduce_sum.18
  80.4 4.8 unpack.2.w_ref
  85.3 79.6 %front_and_gather.1 = (bf16[2,864,2304]{2,1,0:T(8,128)(2,1)}, bf16[2,864,768]{2,1,0:T(8,128)(2,1)}, f32[2,6,864,128]{3,2,1,0:T(8,128)}, bf16[32,1984,128]{2,1,0:T(8,128)(2,1)}) custom-call(bf16[2,864,768]{2,1,0:T(8,128)(2,1)} %x_ref.5, f32[2,9,768]{2,1,0:T(8,128)} %reshape.46.mod_ref, bf16[768,2304]{1,0:T(8,128)(2,1)} %unpack.2.w_ref, ...), custom_call_target="tpu_custom_call" | custom-call | tf_op jit(solution)/shard_map/front_and_gather/pallas_call | solution.py:2092
  164.9 13.7 %unpack.3 = (bf16[768,768]{1,0:T(8,128)(2,1)}, f32[1,768]{1,0:T(1,128)}, bf16[768,768]{1,0:T(8,128)(2,1)}, bf16[1024,1536]{1,0:T(8,128)(2,1)}, bf16[768,768]{1,0...) custom-call(bf16[32,1984,128]{2,1,0:T(8,128)(2,1)} %get-tuple-elemen, ...), custom_call_target="tpu_custom_call" | custom-call | tf_op jit(solution)/shard_map/unpack/pallas_call | solution.py:1026
  178.6 4.8 convolution_convert_fusion
  183.4 10.8 %after_self.1 = (bf16[2,864,768]{2,1,0:T(8,128)(2,1)}, f32[2,864,768]{2,1,0:T(8,128)}, bf16[2,864,768]{2,1,0:T(8,128)(2,1)}) custom-call(bf16[2,864,768]{2,1,0:T(8,128)(2,1)} %get-tuple-element.65.o_ref, bf16[2,864,768]{2,1,0:T(8,128)(2,1)} %x_ref.5, f32[2,9,768]{2,1,0:T(8,128)} %reshape.46.mod_ref, bf16[768,768]{1,0:T(8,128)(2,1)} %get-tuple-element.67.wo_ref, ...), custom_call_target="tpu_custom_call" | custom-call | tf_op jit(solution)/shard_map/after_self/pallas_call | solution.py:400
  194.2 14.3 %cross_forward.1 = (bf16[2,864,768]{2,1,0:T(8,128)(2,1)}, f32[2,6,864,128]{3,2,1,0:T(8,128)}) custom-call(s32[2]{0:T(128)} %refs_0_.3, bf16[2,864,768]{2,1,0:T(8,128)(2,1)} %get-tuple-element.70.refs_1_, bf16[2,256,1536]{2,1,0:T(8,128)(2,1)} %bitcast.31, bf16[2,256,1536]{2,1,0:T(8,128)(2,1)} %bitcast.32), custom_call_target="tpu_custom_call" | custom-call | tf_op jit(solution)/shard_map/cross_forward/pallas_call | solution.py:260
  208.5 8.6 %after_cross.1 = (bf16[2,864,768]{2,1,0:T(8,128)(2,1)}, f32[2,864,768]{2,1,0:T(8,128)}) custom-call(bf16[2,864,768]{2,1,0:T(8,128)(2,1)} %get-tuple-element.72.o_ref.refs_5_, f32[2,864,768]{2,1,0:T(8,128)} %get-tuple-element.73.h_ref, f32[2,9,768]{2,1,0:T(8,128)} %reshape.46.mod_ref, bf16[768,768]{1,0:T(8,128)(2,1)} %get-tuple-element.74.wo_ref.w_ref, ...), custom_call_target="tpu_custom_call" | custom-call | tf_op jit(solution)/shard_map/after_cross/pallas_call | solution.py:424
  217.1 75.0 %feed.1 = (bf16[2,864,768]{2,1,0:T(8,128)(2,1)}, f32[2,864,768]{2,1,0:T(8,128)}, bf16[768,3072]{1,0:T(8,128)(2,1)}, bf16[3072,768]{1,0:T(8,128)(2,1)}, f32[1,307...) custom-call(f32[2,864,768]{2,1,0:T(8,128)} %get-tuple-element.76.h_ref, bf16[2,864,768]{2,1,0:T(8,128)(2,1)} %dy_ref.1, ...), custom_call_target="tpu_custom_call" | custom-call | tf_op jit(solution)/shard_map/feed/pallas_call | solution.py:569
  292.2 10.7 %before_cross.1 = (bf16[2,864,768]{2,1,0:T(8,128)(2,1)}, bf16[768,768]{1,0:T(8,128)(2,1)}, f32[1,768]{1,0:T(1,128)}, f32[2,1,768]{2,1,0:T(1,128)}) custom-call(f32[2,864,768]{2,1,0:T(8,128)} %get-tuple-element.83.dh_ref, bf16[2,864,768]{2,1,0:T(8,128)(2,1)} %get-tuple-element.84.z_ref, bf16[2,864,768]{2,1,0:T(8,128)(2,1)} %get-tuple-element.72.o_ref.refs_5_, ...), custom_call_target="tpu_custom_call" | custom-call | tf_op jit(solution)/shard_map/before_cross/pallas_call | solution.py:644
  302.8 20.7 %cross_back.1 = (bf16[2,864,768]{2,1,0:T(8,128)(2,1)}, bf16[2,256,768]{2,1,0:T(8,128)(2,1)}, bf16[2,256,768]{2,1,0:T(8,128)(2,1)}) custom-call(s32[2]{0:T(128)} %refs_0_.3, bf16[2,864,768]{2,1,0:T(8,128)(2,1)} %get-tuple-element.70.refs_1_, bf16[2,256,1536]{2,1,0:T(8,128)(2,1)} %bitcast.33, bf16[2,256,1536]{2,1,0:T(8,128)(2,1)} %bitcast.34, ...), custom_call_target="tpu_custom_call" | custom-call | tf_op jit(solution)/shard_map/cross_back/pallas_call | solution.py:371
  323.5 20.2 %before_self.1 = (f32[2,864,768]{2,1,0:T(8,128)}, bf16[2,864,768]{2,1,0:T(8,128)(2,1)}, bf16[768,768]{1,0:T(8,128)(2,1)}, bf16[768,768]{1,0:T(8,128)(2,1)}, f32[1,768]{1,0:T(1,128)}, /*index=5*/f32[2,3,768]{2,1,0:T(4,128)}) custom-call(bf16[2,864,768]{2,1,0:T(8,128)(2,1)} %get-tuple-element.87.dq_ref, f32[2,864,768]{2,1,0:T(8,128)} %get-tuple-element.73.h_ref, ...), custom_call_target="tpu_custom_call" | custom-call | tf_op jit(solution)/shard_map/before_self/pallas_call | solution.py:716
  343.8 0.7 convert.21
  344.6 3.7 fusion.refs_3_
  348.3 13.4 %pack.2.g_ref = bf16[32,1984,128]{2,1,0:T(8,128)(2,1)} custom-call(bf16[768,768]{1,0:T(8,128)(2,1)} %get-tuple-element.92.refs_0_, f32[1,768]{1,0:T(1,128)} %get-tuple-element.93.refs_1_, bf16[768,768]{1,0:T(8,128)(2,1)} %get-tuple-element.94.refs_2_, bf16[1024,1536]{1,0:T(8,128)(2,1)} %fusion.refs_3_, bf16[768,768]{1,0:T(8,128)(2,1)} %get-tuple-element.97.refs_4_, ...), custom_call_target="tpu_custom_call" | custom-call | tf_op jit(solution)/shard_map/pack/pallas_call | solution.py:1134
  361.7 111.2 %back_and_scatter.1 = (bf16[2,864,768]{2,1,0:T(8,128)(2,1)}, bf16[768,2304]{1,0:T(8,128)(2,1)}, f32[2,2,768]{2,1,0:T(2,128)}, bf16[3712,128]{1,0:T(8,128)(2,1)}) custom-call(bf16[2,864,2304]{2,1,0:T(8,128)(2,1)} %get-tuple-element.82.q_ref.k_ref.v_ref, bf16[2,864,2304]{2,1,0:T(8,128)(2,1)} %get-tuple-element.82.q_ref.k_ref.v_ref, ...), custom_call_target="tpu_custom_call" | custom-call | tf_op jit(solution)/shard_map/back_and_scatter/pallas_call | solution.py:2254
  474.5 4.6 pack.3.g_ref
  479.1 44.0 %scatter_chunks.1 = (bf16[3712,128]{1,0:T(8,128)(2,1)}, bf16[32,112,128]{2,1,0:T(8,128)(2,1)}) custom-call(bf16[32,448,128]{2,1,0:T(8,128)(2,1)} %pack.3.g_ref, bf16[112,128]{1,0:T(8,128)(2,1)} %pad.14.rows_ref), custom_call_target="tpu_custom_call" | custom-call | tf_op jit(solution)/shard_map/scatter_chunks/pallas_call | solution.py:2002
  523.1 6.1 %own_grad.1 = (f32[3712,128]{1,0:T(8,128)}, f32[8,128]{1,0:T(8,128)}) custom-call(f32[832,64]{1,0:T(8,128)} %maximum_maximum_fusion.cond_ref, bf16[3584,128]{1,0:T(8,128)(2,1)} %bitcast.37, bf16[3712,128]{1,0:T(8,128)(2,1)} %get-tuple-element.110.early_ref, bf16[3712,128]{1,0:T(8,128)(2,1)} %get-tuple-element.111.late_ref), custom_call_target="tpu_custom_call" | custom-call | tf_op jit(solution)/shard_map/own_grad/pallas_call | solution.py:2402
  529.2 12.3 %squares.1 = f32[32,8,128]{2,1,0:T(8,128)} custom-call(f32[8,128]{1,0:T(8,128)} %get-tuple-element.112.in_ref), custom_call_target="tpu_custom_call" | custom-call | tf_op jit(solution)/shard_map/squares/pallas_call | solution.py:2297
  541.5 1.5 reduce_sum.19
  543.8 6.2 %multiply_subtract_fusion = (f32[473472]{0:T(1024)}, f32[473472]{0:T(1024)}, f32[473472]{0:T(1024)}) fusion(f32[473472]{0:T(1024)S(1)} %copy-done.3, f32[]{:T(128)S(6)} %div.31, f32[3712,128]{1,0:T(8,128)} %get-tuple-element.113, f32[473472]{0:T(1024)} %param.14, f32[473472]{0:T(1024)} %param.15), kind=kLoop, calls=%fused_computation.8 | loop fusion | flops 7575552 | bytes 13257220 | tf_op jit(solution)/shard_map/sub | solution.py:2570
  550.0 1.5 copy.32
  (41 shorter events, 4.6 us)
Async XLA Ops:
  0.6 1.2 copy-start
  4.9 20.6 %copy-start.2 = (f32[3888,128]{1,0:T(8,128)}, f32[3888,128]{1,0:T(8,128)S(1)}, u32[]{:S(2)}) copy-start(f32[3888,128]{1,0:T(8,128)S(1)} %pad.13.lin_ref) | copy-start | bytes 5971972
  323.5 20.3 %copy-start.7 = (f32[2,1,768]{2,1,0:T(1,128)S(1)}, f32[2,1,768]{2,1,0:T(1,128)}, u32[]{:S(2)}) copy-start(f32[2,1,768]{2,1,0:T(1,128)} %get-tuple-element.107) | copy-start | bytes 18436
  323.5 21.0 %copy-start.6 = (f32[2,3,768]{2,1,0:T(4,128)S(1)}, f32[2,3,768]{2,1,0:T(4,128)}, u32[]{:S(2)}) copy-start(f32[2,3,768]{2,1,0:T(4,128)} %get-tuple-element.108) | copy-start | bytes 55300
  323.5 21.1 %copy-start.8 = (bf16[2,256,768]{2,1,0:T(8,128)(2,1)S(1)}, bf16[2,256,768]{2,1,0:T(8,128)(2,1)}, u32[]{:S(2)}) copy-start(bf16[2,256,768]{2,1,0:T(8,128)(2,1)} %get-tuple-element.95) | copy-start | bytes 2359300
  323.5 21.1 %copy-start.9 = (bf16[2,256,768]{2,1,0:T(8,128)(2,1)S(1)}, bf16[2,256,768]{2,1,0:T(8,128)(2,1)}, u32[]{:S(2)}) copy-start(bf16[2,256,768]{2,1,0:T(8,128)(2,1)} %get-tuple-element.96) | copy-start | bytes 2359300
  344.5 3.7 copy-start.5
  361.7 112.0 %slice-start = ((bf16[2,3,768]{2,1,0:T(4,128)(2,1)}), bf16[2,2,768]{2,1,0:T(2,128)(2,1)S(1)}, s32[]{:S(2)}) async-start(bf16[2,3,768]{2,1,0:T(4,128)(2,1)} %copy-done.5), calls=%async_computation | async-start | bytes 12288 | tf_op jit(solution)/shard_map/slice | solution.py:854
  523.1 20.7 %copy-start.3 = (f32[473472]{0:T(1024)S(1)}, f32[473472]{0:T(1024)}, u32[]{:S(2)}) copy-start(f32[473472]{0:T(1024)} %param.13) | copy-start | bytes 5681668
  543.7 6.2 %copy-start.4 = (bf16[2,864,768]{2,1,0:T(8,128)(2,1)S(1)}, bf16[2,864,768]{2,1,0:T(8,128)(2,1)}, u32[]{:S(2)}) copy-start(bf16[2,864,768]{2,1,0:T(8,128)(2,1)} %get-tuple-element.126) | copy-start | bytes 7962628
  550.0 2.0 copy-start.1

commit v7 on v6

--- a/solution.py
+++ b/solution.py
@@ -382,7 +382,13 @@
     )(*args)
 
 
-def after_self_kernel(o_ref, x_ref, mod_ref, wo_ref, bo_ref, wq_ref, z_ref, h_ref, q_ref):
+def after_self_kernel(
+    o_ref, x_ref, mod_ref, wo_ref, bo_ref, wq_ref, cap_ref, wkv_ref, z_ref, h_ref, q_ref, kv_ref
+):
+    @pl.when(pl.program_id(1) == 0)
+    def _():
+        kv_ref[0] = nn(cap_ref[0], wkv_ref[...]).astype(BF)
+
     branch = nn(o_ref[0], wo_ref[...]) + bo_ref[...]
     hidden = x_ref[0].astype(F32) + mod_ref[0, 2:3] * branch
     normed, _ = normalize(hidden)
@@ -392,23 +398,35 @@
     q_ref[0] = nn(second_in, wq_ref[...]).astype(BF)
 
 
-def after_self(mixed, latents, mod, weight, bias, query_weight):
+def after_self(mixed, latents, mod, weight, bias, query_weight, captions, keyval_weight):
     clips, frames, width = latents.shape
+    slots, context = captions.shape[1:]
+    wide = keyval_weight.shape[1]
     rows = row_block(frames)
     spec = rows_spec(rows, width)
     square = whole_spec((width, width))
     return call(
         after_self_kernel,
         (clips, frames // rows),
-        [spec, spec, clip_spec(9, width), square, whole_spec((1, width)), square],
-        [spec, spec, spec],
+        [
+            spec,
+            spec,
+            clip_spec(9, width),
+            square,
+            whole_spec((1, width)),
+            square,
+            clip_spec(slots, context),
+            whole_spec(keyval_weight.shape),
+        ],
+        [spec, spec, spec, clip_spec(slots, wide)],
         [
             struct(latents.shape, BF),
             struct(latents.shape, F32),
             struct(latents.shape, BF),
+            struct((clips, slots, wide), BF),
         ],
         "after_self",
-    )(mixed, latents, mod, weight, bias, query_weight)
+    )(mixed, latents, mod, weight, bias, query_weight, captions, keyval_weight)
 
 
 def after_cross_kernel(o_ref, h_ref, mod_ref, wo_ref, bo_ref, z_ref, out_ref):
@@ -666,12 +684,16 @@
     mod_ref,
     wq_ref,
     wo_ref,
+    cap_ref,
+    dk_ref,
+    dv_ref,
     out_ref,
     do_ref,
     dwq_ref,
     dwo_ref,
     db_ref,
     sums_ref,
+    dkv_ref,
     in_s,
     dq_s,
     o_s,
@@ -706,18 +728,35 @@
     def _():
         dwq_ref[...] = tn(in_s[...], dq_s[...]).astype(BF)
         dwo_ref[...] = tn(o_s[...], dz_s[...]).astype(BF)
-
-
-def before_self(grad_query, hidden, dh, branch, mixed, mod, query_weight, weight):
+        turned = cap_ref[...].T
+        half = dk_ref.shape[1]
+        dkv_ref[:, :half] = nn(turned, dk_ref[...]).astype(BF)
+        dkv_ref[:, half:] = nn(turned, dv_ref[...]).astype(BF)
+
+
+def before_self(
+    grad_query, hidden, dh, branch, mixed, mod, query_weight, weight, captions, grad_k, grad_v
+):
     clips, frames, width = dh.shape
+    captions, grad_k, grad_v = [t.reshape(-1, t.shape[2]) for t in (captions, grad_k, grad_v)]
+    keyval_shape = (captions.shape[1], 2 * width)
     rows = row_block(frames)
     spec = rows_spec(rows, width)
     square = whole_spec((width, width))
     return call(
         before_self_kernel,
         (clips, frames // rows),
-        [spec, spec, spec, spec, spec, clip_spec(9, width), square, square],
-        [spec, spec, square, square, whole_spec((1, width)), clip_spec(3, width)],
+        [spec, spec, spec, spec, spec, clip_spec(9, width), square, square]
+        + [whole_spec(t.shape) for t in (captions, grad_k, grad_v)],
+        [
+            spec,
+            spec,
+            square,
+            square,
+            whole_spec((1, width)),
+            clip_spec(3, width),
+            whole_spec(keyval_shape),
+        ],
         [
             struct(dh.shape, F32),
             struct(dh.shape, BF),
@@ -725,10 +764,23 @@
             struct((width, width), BF),
             struct((1, width), F32),
             struct((clips, 3, width), F32),
+            struct(keyval_shape, BF),
         ],
         "before_self",
         [pltpu.VMEM((clips * frames, width), BF)] * 4,
-    )(grad_query, hidden, dh, branch, mixed, mod, query_weight, weight)
+    )(
+        grad_query,
+        hidden,
+        dh,
+        branch,
+        mixed,
+        mod,
+        query_weight,
+        weight,
+        captions,
+        grad_k,
+        grad_v,
+    )
 
 
 def input_kernel(
@@ -798,17 +850,9 @@
         down_weight,
         down_bias,
     ) = weights
-    clips, frames, width = latents.shape
-    slots = captions.shape[1]
     groups = HEADS // 2
-    caption_flat = captions.reshape(clips * slots, captions.shape[2])
-    branch_one, hidden_one, cross_queries = after_self(
-        mixed_one, latents, mod, output_weight, output_bias, cross_query
-    )
-    pairs = (
-        jnp.dot(caption_flat, cross_keyval, preferred_element_type=F32)
-        .astype(BF)
-        .reshape(clips, slots, 2 * width)
+    branch_one, hidden_one, cross_queries, pairs = after_self(
+        mixed_one, latents, mod, output_weight, output_bias, cross_query, captions, cross_keyval
     )
     mixed_two, lse_two = attend_forward(cross_queries, 0, pairs, groups, lengths, "cross_forward")
     branch_two, hidden_two = after_cross(mixed_two, hidden_one, mod, cross_output, cross_bias)
@@ -830,10 +874,26 @@
         "cross_back",
         2,
     )
-    grad_pairs = jnp.concatenate([grad_ck, grad_cv], axis=-1).reshape(clips * slots, 2 * width)
-    grad_keyval = jnp.dot(caption_flat.T, grad_pairs, preferred_element_type=F32).astype(BF)
-    dh_one, grad_mixed_one, grad_cross_query, grad_output, grad_output_bias, sums_two = before_self(
-        grad_cq, hidden_one, dh_two, branch_one, mixed_one, mod, cross_query, output_weight
+    (
+        dh_one,
+        grad_mixed_one,
+        grad_cross_query,
+        grad_output,
+        grad_output_bias,
+        sums_two,
+        grad_keyval,
+    ) = before_self(
+        grad_cq,
+        hidden_one,
+        dh_two,
+        branch_one,
+        mixed_one,
+        mod,
+        cross_query,
+        output_weight,
+        captions,
+        grad_ck,
+        grad_cv,
     )
     gradients = [
         grad_output,
@@ -898,6 +958,14 @@
         self.tiles = 2 * -(-total // (2 * devices))
         self.chunk = self.tiles * TILE
         self.half = self.chunk // 2
+        small = self.tiles // 9 * TILE
+        large = self.half - small
+        self.parts = (
+            (0, large),
+            (large, large),
+            (2 * large, small),
+            (2 * large + small, small),
+        )
         self.folds = next(
             n
             for n in range(1, 99)
@@ -1385,13 +1453,13 @@
     @staticmethod
     def semaphores(group):
         dma = pltpu.SemaphoreType.DMA
-        return [dma, dma((5, group.devices // 2, 2)), dma((group.devices, 2))]
+        return [dma, dma((5, group.devices // 2, 4)), dma((group.devices, 4))]
 
     def copy(self, kind, yy, xx, zz, part, cc=None, mine=False):
         core = self.c if cc is None else cc
         column = yy * 2 + xx
         index = column * self.inner + zz * 2 + core
-        rows = pl.ds(part * self.group.half, self.group.half)
+        rows = pl.ds(*self.group.parts[part])
         return pltpu.make_async_remote_copy(
             src_ref=self.chunk_ref.at[rows] if mine else self.out_ref.at[index, rows],
             dst_ref=self.out_ref.at[index, rows],
@@ -1422,6 +1490,30 @@
                 [zz < self.levels if sign > 0 else None, zz >= 0 if sign < 0 else None]
             )
             yield zz, sign, inside
+
+    def relay(self, distance, sign, inside, yy, xx, zz):
+        own = yy is self.y and xx is self.x
+        for part in (2, 3):
+            mine = own and distance == 0
+            if not mine:
+                self.arrive(inside, yy, xx, zz, part)
+            if distance == 0:
+                if own:
+                    kinds = ("x", "y") if part == 2 else ("y", "x")
+                elif part == 2 and yy is self.y:
+                    kinds = ("y",)
+                elif part == 3 and xx is self.x:
+                    kinds = ("x",)
+                else:
+                    kinds = ()
+                for kind in kinds:
+                    self.send(inside, kind, yy, xx, zz, part, mine)
+            if sign <= 0:
+                on = when_all([inside, self.z < self.levels - 1])
+                self.send(on, "up", yy, xx, zz, part, mine)
+            if sign >= 0:
+                self.send(when_all([inside, self.z > 0]), "down", yy, xx, zz, part, mine)
+            self.send(inside, "twin", yy, xx, zz, part, mine)
 
     def turn(self, turn):
         y, x, z, levels = self.y, self.x, self.z, self.levels
@@ -1440,6 +1532,7 @@
                     for kind in ("x", "y") if part else ("y", "x"):
                         self.send(inside, kind, y, x, zz, part, mine)
                     self.send(inside, "twin", y, x, zz, part, mine)
+                self.relay(turn, sign, inside, y, x, zz)
         if 1 <= turn <= levels:
             for zz, sign, inside in self.spread(turn - 1):
                 self.arrive(inside, y, 1 - x, zz, 0)
@@ -1452,16 +1545,19 @@
                 self.send(inside, "twin", 1 - y, x, zz, 0)
                 self.arrive(inside, y, 1 - x, zz, 1)
                 self.send(inside, "twin", y, 1 - x, zz, 1)
+                self.relay(turn - 1, sign, inside, y, 1 - x, zz)
+                self.relay(turn - 1, sign, inside, 1 - y, x, zz)
         if turn >= 2:
             for zz, sign, inside in self.spread(turn - 2):
                 for part in range(2):
                     self.arrive(inside, 1 - y, 1 - x, zz, part)
                     self.send(inside, "twin", 1 - y, 1 - x, zz, part)
+                self.relay(turn - 2, sign, inside, 1 - y, 1 - x, zz)
 
     def finish(self):
         def twin_arrivals(i, _):
             column, zz = i // self.levels, i % self.levels
-            for part in range(2):
+            for part in range(4):
                 self.copy("twin", column // 2, column % 2, zz, part, 1 - self.c).wait_recv()
             return 0
 
@@ -2031,7 +2127,7 @@
         meet_all(me, group.devices, inner)
         gather.turn(0)
 
-    for turn, at in ((1, leads), (2, leads + 2), (3, leads + 4)):
+    for turn, at in ((1, leads + 1), (2, leads + 3), (3, leads + 5)):
 
         @pl.when(step == at)
         def _(turn=turn):

time: 558 us -> 550 us (0.986)
  matrix products: 8.49 us -> 0 us
    dot_general x2 -> x0, matrix products: 8.49 us -> none  [the longest x1 4.83 us: block_pass(): jnp.dot(caption_flat, cross_keyval, preferred_element_type=F32).astype(BF)]
where the time goes in v7:
time: 550 us; the launch traced here: 545 us
  Pallas kernels  522 us (95%)
  other arithmetic  12.9 us (2%)
  local copies, waits for them, and re-layouts  7.81 us (1%)
    pallas_call x1, Pallas kernels, back_and_scatter(): remote_call(functools.partial(back_kernel, group=group, inner=inner, pair...  107 us
    pallas_call x1, Pallas kernels, front_and_gather(): remote_call(functools.partial(front_kernel, group=group, inner=inner, lea...  78.2 us
    pallas_call x1, Pallas kernels, feed(): call(functools.partial(feed_kernel, clips=clips, frames=frames, rows=rows...  75.1 us
    pallas_call x1, Pallas kernels, gather_chunks(): remote_call(functools.partial(gather_kernel, group=group, later=later, in...  48.5 us
    pallas_call x1, Pallas kernels, scatter_chunks(): remote_call(functools.partial(scatter_kernel, group=group, inner=inner, r...  44 us
    pallas_call x1, Pallas kernels, before_self(): call(before_self_kernel, (clips, frames // rows), [spec, spec, spec, spec...  23.4 us
    pallas_call x1, Pallas kernels, attend_backward(): call(functools.partial(attend_back_kernel, masked=masked), (clips, groups...  20.7 us
    pallas_call x2, Pallas kernels, unpack_weights(): pl.pallas_call(functools.partial(unpack_kernel, plan=plan, indices=indice...  19.3 us

profile of v7, /device:TPU:0, one launch (start us, length us, event | category | flops | bytes accessed | tf_op | source)
XLA Modules:
  0.0 545.4 jit_solution(11477755791919630975)
XLA Ops:
  0.6 0.7 convert_element_type.19
  1.4 0.7 broadcast_in_dim.6.step_ref
  2.1 1.6 pad.13.lin_ref
  3.7 1.1 slice.37.slot_ref
  4.8 17.3 %start_chunks.1 = (f32[32,8,128]{2,1,0:T(8,128)}, bf16[448,128]{1,0:T(8,128)(2,1)}) custom-call(f32[8,128]{1,0:T(8,128)} %broadcast_in_dim.6.step_ref, bf16[3712,128]{1,0:T(8,128)(2,1)} %slice.37.slot_ref), custom_call_target="tpu_custom_call" | custom-call | tf_op jit(solution)/shard_map/start_chunks/pallas_call | solution.py:1421
  22.2 0.9 slice.22
  23.4 0.8 multiply_cosine_fusion
  24.3 1.1 maximum_maximum_fusion.cond_ref
  25.4 3.6 ada_partial.1
  29.0 48.5 %gather_chunks.1 = (bf16[32,448,128]{2,1,0:T(8,128)(2,1)}, f32[6,112,128]{2,1,0:T(8,128)}, bf16[1984,128]{1,0:T(8,128)(2,1)}) custom-call(bf16[448,128]{1,0:T(8,128)(2,1)} %get-tuple-element.62.chunk_ref, f32[2,16,112,128]{3,2,1,0:T(8,128)} %bitcast.21, bf16[3712,128]{1,0:T(8,128)(2,1)} %slice.37.slot_ref), custom_call_target="tpu_custom_call" | custom-call | tf_op jit(solution)/shard_map/gather_chunks/pallas_call | solution.py:1774
  77.5 1.0 reduce_sum.18
  79.2 4.8 unpack.2.w_ref
  84.0 78.2 %front_and_gather.1 = (bf16[2,864,2304]{2,1,0:T(8,128)(2,1)}, bf16[2,864,768]{2,1,0:T(8,128)(2,1)}, f32[2,6,864,128]{3,2,1,0:T(8,128)}, bf16[32,1984,128]{2,1,0:T(8,128)(2,1)}) custom-call(bf16[2,864,768]{2,1,0:T(8,128)(2,1)} %x_ref.5, f32[2,9,768]{2,1,0:T(8,128)} %reshape.48.mod_ref, bf16[768,2304]{1,0:T(8,128)(2,1)} %unpack.2.w_ref, ...), custom_call_target="tpu_custom_call" | custom-call | tf_op jit(solution)/shard_map/front_and_gather/pallas_call | solution.py:2188
  162.1 14.5 %unpack.3 = (bf16[768,768]{1,0:T(8,128)(2,1)}, f32[1,768]{1,0:T(1,128)}, bf16[768,768]{1,0:T(8,128)(2,1)}, bf16[1024,1536]{1,0:T(8,128)(2,1)}, bf16[768,768]{1,0...) custom-call(bf16[32,1984,128]{2,1,0:T(8,128)(2,1)} %get-tuple-elemen, ...), custom_call_target="tpu_custom_call" | custom-call | tf_op jit(solution)/shard_map/unpack/pallas_call | solution.py:1094
  176.6 14.0 %after_self.1 = (bf16[2,864,768]{2,1,0:T(8,128)(2,1)}, f32[2,864,768]{2,1,0:T(8,128)}, bf16[2,864,768]{2,1,0:T(8,128)(2,1)}, bf16[2,256,1536]{2,1,0:T(8,128)(2,1)}) custom-call(bf16[2,864,768]{2,1,0:T(8,128)(2,1)} %get-tuple-element.67.o_ref, bf16[2,864,768]{2,1,0:T(8,128)(2,1)} %x_ref.5, f32[2,9,768]{2,1,0:T(8,128)} %reshape.48.mod_ref, ...), custom_call_target="tpu_custom_call" | custom-call | tf_op jit(solution)/shard_map/after_self/pallas_call | solution.py:408
  190.6 14.3 %cross_forward.1 = (bf16[2,864,768]{2,1,0:T(8,128)(2,1)}, f32[2,6,864,128]{3,2,1,0:T(8,128)}) custom-call(s32[2]{0:T(128)} %refs_0_.3, bf16[2,864,768]{2,1,0:T(8,128)(2,1)} %get-tuple-element.73.refs_1_, bf16[2,256,1536]{2,1,0:T(8,128)(2,1)} %get-tuple-element.74.refs_2_.refs_3_, bf16[2,256,1536]{2,1,0:T(8,128)(2,1)} %get-tuple-element.74.refs_2_.refs_3_), custom_call_target="tpu_custom_call" | custom-call | tf_op jit(solution)/shard_map/cross_forward/pallas_call | solution.py:260
  204.9 8.7 %after_cross.1 = (bf16[2,864,768]{2,1,0:T(8,128)(2,1)}, f32[2,864,768]{2,1,0:T(8,128)}) custom-call(bf16[2,864,768]{2,1,0:T(8,128)(2,1)} %get-tuple-element.75.o_ref.refs_5_, f32[2,864,768]{2,1,0:T(8,128)} %get-tuple-element.76.h_ref, f32[2,9,768]{2,1,0:T(8,128)} %reshape.48.mod_ref, bf16[768,768]{1,0:T(8,128)(2,1)} %get-tuple-element.77.wo_ref.w_ref, ...), custom_call_target="tpu_custom_call" | custom-call | tf_op jit(solution)/shard_map/after_cross/pallas_call | solution.py:442
  213.5 75.1 %feed.1 = (bf16[2,864,768]{2,1,0:T(8,128)(2,1)}, f32[2,864,768]{2,1,0:T(8,128)}, bf16[768,3072]{1,0:T(8,128)(2,1)}, bf16[3072,768]{1,0:T(8,128)(2,1)}, f32[1,307...) custom-call(f32[2,864,768]{2,1,0:T(8,128)} %get-tuple-element.79.h_ref, bf16[2,864,768]{2,1,0:T(8,128)(2,1)} %dy_ref.1, ...), custom_call_target="tpu_custom_call" | custom-call | tf_op jit(solution)/shard_map/feed/pallas_call | solution.py:587
  288.6 10.7 %before_cross.1 = (bf16[2,864,768]{2,1,0:T(8,128)(2,1)}, bf16[768,768]{1,0:T(8,128)(2,1)}, f32[1,768]{1,0:T(1,128)}, f32[2,1,768]{2,1,0:T(1,128)}) custom-call(f32[2,864,768]{2,1,0:T(8,128)} %get-tuple-element.86.dh_ref, bf16[2,864,768]{2,1,0:T(8,128)(2,1)} %get-tuple-element.87.z_ref, bf16[2,864,768]{2,1,0:T(8,128)(2,1)} %get-tuple-element.75.o_ref.refs_5_, ...), custom_call_target="tpu_custom_call" | custom-call | tf_op jit(solution)/shard_map/before_cross/pallas_call | solution.py:662
  299.3 20.7 %cross_back.1 = (bf16[2,864,768]{2,1,0:T(8,128)(2,1)}, bf16[2,256,768]{2,1,0:T(8,128)(2,1)}, bf16[2,256,768]{2,1,0:T(8,128)(2,1)}) custom-call(s32[2]{0:T(128)} %refs_0_.3, bf16[2,864,768]{2,1,0:T(8,128)(2,1)} %get-tuple-element.73.refs_1_, bf16[2,256,1536]{2,1,0:T(8,128)(2,1)} %get-tuple-element.74.refs_2_.refs_3_, ...), custom_call_target="tpu_custom_call" | custom-call | tf_op jit(solution)/shard_map/cross_back/pallas_call | solution.py:371
  320.1 23.4 %before_self.1 = (f32[2,864,768]{2,1,0:T(8,128)}, bf16[2,864,768]{2,1,0:T(8,128)(2,1)}, bf16[768,768]{1,0:T(8,128)(2,1)}, bf16[768,768]{1,0:T(8,128)(2,1)}, f32[...) custom-call(bf16[2,864,768]{2,1,0:T(8,128)(2,1)} %get-tuple-element.90.dq_ref, ...), custom_call_target="tpu_custom_call" | custom-call | tf_op jit(solution)/shard_map/before_self/pallas_call | solution.py:746
  343.5 0.7 convert.21
  344.2 13.4 %pack.2.g_ref = bf16[32,1984,128]{2,1,0:T(8,128)(2,1)} custom-call(bf16[768,768]{1,0:T(8,128)(2,1)} %get-tuple-element.97.refs_0_, f32[1,768]{1,0:T(1,128)} %get-tuple-element.98.refs_1_, bf16[768,768]{1,0:T(8,128)(2,1)} %get-tuple-element.99.refs_2_, bf16[1024,1536]{1,0:T(8,128)(2,1)} %get-tuple-element.100.refs_3_, ...), custom_call_target="tpu_custom_call" | custom-call | tf_op jit(solution)/shard_map/pack/pallas_call | solution.py:1202
  357.7 107.4 %back_and_scatter.1 = (bf16[2,864,768]{2,1,0:T(8,128)(2,1)}, bf16[768,2304]{1,0:T(8,128)(2,1)}, f32[2,2,768]{2,1,0:T(2,128)}, bf16[3712,128]{1,0:T(8,128)(2,1)}) custom-call(bf16[2,864,2304]{2,1,0:T(8,128)(2,1)} %get-tuple-element.85.q_ref.k_ref.v_ref, bf16[2,864,2304]{2,1,0:T(8,128)(2,1)} %get-tuple-element.85.q_ref.k_ref.v_ref, ...), custom_call_target="tpu_custom_call" | custom-call | tf_op jit(solution)/shard_map/back_and_scatter/pallas_call | solution.py:2350
  465.1 0.7 convert.20
  466.7 4.8 pack.3.g_ref
  471.4 44.0 %scatter_chunks.1 = (bf16[3712,128]{1,0:T(8,128)(2,1)}, bf16[32,112,128]{2,1,0:T(8,128)(2,1)}) custom-call(bf16[32,448,128]{2,1,0:T(8,128)(2,1)} %pack.3.g_ref, bf16[112,128]{1,0:T(8,128)(2,1)} %pad.14.rows_ref), custom_call_target="tpu_custom_call" | custom-call | tf_op jit(solution)/shard_map/scatter_chunks/pallas_call | solution.py:2098
  515.4 6.1 %own_grad.1 = (f32[3712,128]{1,0:T(8,128)}, f32[8,128]{1,0:T(8,128)}) custom-call(f32[832,64]{1,0:T(8,128)} %maximum_maximum_fusion.cond_ref, bf16[3584,128]{1,0:T(8,128)(2,1)} %bitcast.23, bf16[3712,128]{1,0:T(8,128)(2,1)} %get-tuple-element.114.early_ref, bf16[3712,128]{1,0:T(8,128)(2,1)} %get-tuple-element.115.late_ref), custom_call_target="tpu_custom_call" | custom-call | tf_op jit(solution)/shard_map/own_grad/pallas_call | solution.py:2498
  521.5 12.3 %squares.1 = f32[32,8,128]{2,1,0:T(8,128)} custom-call(f32[8,128]{1,0:T(8,128)} %get-tuple-element.116.in_ref), custom_call_target="tpu_custom_call" | custom-call | tf_op jit(solution)/shard_map/squares/pallas_call | solution.py:2393
  533.8 1.5 reduce_sum.19
  536.1 6.2 %multiply_subtract_fusion = (f32[473472]{0:T(1024)}, f32[473472]{0:T(1024)}, f32[473472]{0:T(1024)}) fusion(f32[473472]{0:T(1024)S(1)} %copy-done.1, f32[]{:T(128)S(6)} %div.31, f32[3712,128]{1,0:T(8,128)} %get-tuple-element.117, f32[473472]{0:T(1024)} %param.14, f32[473472]{0:T(1024)} %param.15), kind=kLoop, calls=%fused_computation.5 | loop fusion | flops 7575552 | bytes 13257220 | tf_op jit(solution)/shard_map/sub | solution.py:2666
  542.3 1.5 copy.23
  (28 shorter events, 2.1 us)
Async XLA Ops:
  3.7 20.6 %copy-start = (f32[3888,128]{1,0:T(8,128)}, f32[3888,128]{1,0:T(8,128)S(1)}, u32[]{:S(2)}) copy-start(f32[3888,128]{1,0:T(8,128)S(1)} %pad.13.lin_ref) | copy-start | bytes 5971972
  320.0 23.4 %copy-start.4 = (f32[2,1,768]{2,1,0:T(1,128)S(1)}, f32[2,1,768]{2,1,0:T(1,128)}, u32[]{:S(2)}) copy-start(f32[2,1,768]{2,1,0:T(1,128)} %get-tuple-element.111) | copy-start | bytes 18436
  320.0 24.2 %copy-start.3 = (f32[2,3,768]{2,1,0:T(4,128)S(1)}, f32[2,3,768]{2,1,0:T(4,128)}, u32[]{:S(2)}) copy-start(f32[2,3,768]{2,1,0:T(4,128)} %get-tuple-element.112) | copy-start | bytes 55300
  515.4 20.7 %copy-start.1 = (f32[473472]{0:T(1024)S(1)}, f32[473472]{0:T(1024)}, u32[]{:S(2)}) copy-start(f32[473472]{0:T(1024)} %param.13) | copy-start | bytes 5681668
  536.1 6.2 %copy-start.2 = (bf16[2,864,768]{2,1,0:T(8,128)(2,1)S(1)}, bf16[2,864,768]{2,1,0:T(8,128)(2,1)}, u32[]{:S(2)}) copy-start(bf16[2,864,768]{2,1,0:T(8,128)(2,1)} %get-tuple-element.130) | copy-start | bytes 7962628

commit v8 on v7

--- a/solution.py
+++ b/solution.py
@@ -402,7 +402,7 @@
     clips, frames, width = latents.shape
     slots, context = captions.shape[1:]
     wide = keyval_weight.shape[1]
-    rows = row_block(frames)
+    rows = frames
     spec = rows_spec(rows, width)
     square = whole_spec((width, width))
     return call(
@@ -437,7 +437,7 @@
 
 def after_cross(mixed, hidden, mod, weight, bias):
     clips, frames, width = hidden.shape
-    rows = row_block(frames)
+    rows = frames
     spec = rows_spec(rows, width)
     return call(
         after_cross_kernel,
@@ -656,7 +656,7 @@
 
 def before_cross(dh, branch, mixed, mod, weight):
     clips, frames, width = dh.shape
-    rows = row_block(frames)
+    rows = frames
     spec = rows_spec(rows, width)
     square = whole_spec((width, width))
     return call(
@@ -2081,10 +2081,9 @@
     trade = Trade(
         rows_ref, all_ref, own_sem, row_send, row_recv, group, inner, group.devices, receivers
     )
-    for name, stage in stages.items():
+    trade.start()
+    for stage in stages.values():
         stage()
-        if name == "once0":
-            trade.start()
     deal = Deal(group, total, out_ref, *rest[-2:], inner, True)
     deal.start()
     finish()

time: 550 us -> 547 us (level)
  no operation moved by 1% of the time
where the time goes in v8:
time: 547 us; the launch traced here: 542 us
  Pallas kernels  519 us (95%)
  other arithmetic  12.9 us (2%)
  local copies, waits for them, and re-layouts  7.81 us (1%)
    pallas_call x1, Pallas kernels, back_and_scatter(): remote_call(functools.partial(back_kernel, group=group, inner=inner, pair...  107 us
    pallas_call x1, Pallas kernels, front_and_gather(): remote_call(functools.partial(front_kernel, group=group, inner=inner, lea...  78.2 us
    pallas_call x1, Pallas kernels, feed(): call(functools.partial(feed_kernel, clips=clips, frames=frames, rows=rows...  74.9 us
    pallas_call x1, Pallas kernels, gather_chunks(): remote_call(functools.partial(gather_kernel, group=group, later=later, in...  48.5 us
    pallas_call x1, Pallas kernels, scatter_chunks(): remote_call(functools.partial(scatter_kernel, group=group, inner=inner, r...  42.5 us
    pallas_call x1, Pallas kernels, before_self(): call(before_self_kernel, (clips, frames // rows), [spec, spec, spec, spec...  23.4 us
    pallas_call x1, Pallas kernels, attend_backward(): call(functools.partial(attend_back_kernel, masked=masked), (clips, groups...  20.7 us
    pallas_call x2, Pallas kernels, unpack_weights(): pl.pallas_call(functools.partial(unpack_kernel, plan=plan, indices=indice...  19.5 us

profile of v8, /device:TPU:0, one launch (start us, length us, event | category | flops | bytes accessed | tf_op | source)
XLA Modules:
  0.0 542.2 jit_solution(2857474153198275651)
XLA Ops:
  0.6 0.7 convert_element_type.19
  1.4 0.7 broadcast_in_dim.6.step_ref
  2.1 1.6 pad.13.lin_ref
  3.7 1.1 slice.37.slot_ref
  4.8 17.3 %start_chunks.1 = (f32[32,8,128]{2,1,0:T(8,128)}, bf16[448,128]{1,0:T(8,128)(2,1)}) custom-call(f32[8,128]{1,0:T(8,128)} %broadcast_in_dim.6.step_ref, bf16[3712,128]{1,0:T(8,128)(2,1)} %slice.37.slot_ref), custom_call_target="tpu_custom_call" | custom-call | tf_op jit(solution)/shard_map/start_chunks/pallas_call | solution.py:1421
  22.2 0.9 slice.22
  23.4 0.8 multiply_cosine_fusion
  24.3 1.1 maximum_maximum_fusion.cond_ref
  25.4 3.6 ada_partial.1
  29.0 48.5 %gather_chunks.1 = (bf16[32,448,128]{2,1,0:T(8,128)(2,1)}, f32[6,112,128]{2,1,0:T(8,128)}, bf16[1984,128]{1,0:T(8,128)(2,1)}) custom-call(bf16[448,128]{1,0:T(8,128)(2,1)} %get-tuple-element.62.chunk_ref, f32[2,16,112,128]{3,2,1,0:T(8,128)} %bitcast.21, bf16[3712,128]{1,0:T(8,128)(2,1)} %slice.37.slot_ref), custom_call_target="tpu_custom_call" | custom-call | tf_op jit(solution)/shard_map/gather_chunks/pallas_call | solution.py:1774
  77.5 1.0 reduce_sum.18
  79.2 5.0 unpack.2.w_ref
  84.2 78.2 %front_and_gather.1 = (bf16[2,864,2304]{2,1,0:T(8,128)(2,1)}, bf16[2,864,768]{2,1,0:T(8,128)(2,1)}, f32[2,6,864,128]{3,2,1,0:T(8,128)}, bf16[32,1984,128]{2,1,0:T(8,128)(2,1)}) custom-call(bf16[2,864,768]{2,1,0:T(8,128)(2,1)} %x_ref.5, f32[2,9,768]{2,1,0:T(8,128)} %reshape.48.mod_ref, bf16[768,2304]{1,0:T(8,128)(2,1)} %unpack.2.w_ref, ...), custom_call_target="tpu_custom_call" | custom-call | tf_op jit(solution)/shard_map/front_and_gather/pallas_call | solution.py:2187
  162.4 14.5 %unpack.3 = (bf16[768,768]{1,0:T(8,128)(2,1)}, f32[1,768]{1,0:T(1,128)}, bf16[768,768]{1,0:T(8,128)(2,1)}, bf16[1024,1536]{1,0:T(8,128)(2,1)}, bf16[768,768]{1,0...) custom-call(bf16[32,1984,128]{2,1,0:T(8,128)(2,1)} %get-tuple-elemen, ...), custom_call_target="tpu_custom_call" | custom-call | tf_op jit(solution)/shard_map/unpack/pallas_call | solution.py:1094
  176.9 13.7 %after_self.1 = (bf16[2,864,768]{2,1,0:T(8,128)(2,1)}, f32[2,864,768]{2,1,0:T(8,128)}, bf16[2,864,768]{2,1,0:T(8,128)(2,1)}, bf16[2,256,1536]{2,1,0:T(8,128)(2,1)}) custom-call(bf16[2,864,768]{2,1,0:T(8,128)(2,1)} %get-tuple-element.67.o_ref, bf16[2,864,768]{2,1,0:T(8,128)(2,1)} %x_ref.5, f32[2,9,768]{2,1,0:T(8,128)} %reshape.48.mod_ref, ...), custom_call_target="tpu_custom_call" | custom-call | tf_op jit(solution)/shard_map/after_self/pallas_call | solution.py:408
  190.6 14.2 %cross_forward.1 = (bf16[2,864,768]{2,1,0:T(8,128)(2,1)}, f32[2,6,864,128]{3,2,1,0:T(8,128)}) custom-call(s32[2]{0:T(128)} %refs_0_.3, bf16[2,864,768]{2,1,0:T(8,128)(2,1)} %get-tuple-element.73.refs_1_, bf16[2,256,1536]{2,1,0:T(8,128)(2,1)} %get-tuple-element.74.refs_2_.refs_3_, bf16[2,256,1536]{2,1,0:T(8,128)(2,1)} %get-tuple-element.74.refs_2_.refs_3_), custom_call_target="tpu_custom_call" | custom-call | tf_op jit(solution)/shard_map/cross_forward/pallas_call | solution.py:260
  204.8 7.7 %after_cross.1 = (bf16[2,864,768]{2,1,0:T(8,128)(2,1)}, f32[2,864,768]{2,1,0:T(8,128)}) custom-call(bf16[2,864,768]{2,1,0:T(8,128)(2,1)} %get-tuple-element.75.o_ref.refs_5_, f32[2,864,768]{2,1,0:T(8,128)} %get-tuple-element.76.h_ref, f32[2,9,768]{2,1,0:T(8,128)} %reshape.48.mod_ref, bf16[768,768]{1,0:T(8,128)(2,1)} %get-tuple-element.77.wo_ref.w_ref, ...), custom_call_target="tpu_custom_call" | custom-call | tf_op jit(solution)/shard_map/after_cross/pallas_call | solution.py:442
  212.5 74.9 %feed.1 = (bf16[2,864,768]{2,1,0:T(8,128)(2,1)}, f32[2,864,768]{2,1,0:T(8,128)}, bf16[768,3072]{1,0:T(8,128)(2,1)}, bf16[3072,768]{1,0:T(8,128)(2,1)}, f32[1,307...) custom-call(f32[2,864,768]{2,1,0:T(8,128)} %get-tuple-element.79.h_ref, bf16[2,864,768]{2,1,0:T(8,128)(2,1)} %dy_ref.1, ...), custom_call_target="tpu_custom_call" | custom-call | tf_op jit(solution)/shard_map/feed/pallas_call | solution.py:587
  287.4 10.2 %before_cross.1 = (bf16[2,864,768]{2,1,0:T(8,128)(2,1)}, bf16[768,768]{1,0:T(8,128)(2,1)}, f32[1,768]{1,0:T(1,128)}, f32[2,1,768]{2,1,0:T(1,128)}) custom-call(f32[2,864,768]{2,1,0:T(8,128)} %get-tuple-element.86.dh_ref, bf16[2,864,768]{2,1,0:T(8,128)(2,1)} %get-tuple-element.87.z_ref, bf16[2,864,768]{2,1,0:T(8,128)(2,1)} %get-tuple-element.75.o_ref.refs_5_, ...), custom_call_target="tpu_custom_call" | custom-call | tf_op jit(solution)/shard_map/before_cross/pallas_call | solution.py:662
  297.6 20.7 %cross_back.1 = (bf16[2,864,768]{2,1,0:T(8,128)(2,1)}, bf16[2,256,768]{2,1,0:T(8,128)(2,1)}, bf16[2,256,768]{2,1,0:T(8,128)(2,1)}) custom-call(s32[2]{0:T(128)} %refs_0_.3, bf16[2,864,768]{2,1,0:T(8,128)(2,1)} %get-tuple-element.73.refs_1_, bf16[2,256,1536]{2,1,0:T(8,128)(2,1)} %get-tuple-element.74.refs_2_.refs_3_, ...), custom_call_target="tpu_custom_call" | custom-call | tf_op jit(solution)/shard_map/cross_back/pallas_call | solution.py:371
  318.3 23.4 %before_self.1 = (f32[2,864,768]{2,1,0:T(8,128)}, bf16[2,864,768]{2,1,0:T(8,128)(2,1)}, bf16[768,768]{1,0:T(8,128)(2,1)}, bf16[768,768]{1,0:T(8,128)(2,1)}, f32[...) custom-call(bf16[2,864,768]{2,1,0:T(8,128)(2,1)} %get-tuple-element.90.dq_ref, ...), custom_call_target="tpu_custom_call" | custom-call | tf_op jit(solution)/shard_map/before_self/pallas_call | solution.py:746
  341.7 0.7 convert.21
  342.5 13.4 %pack.2.g_ref = bf16[32,1984,128]{2,1,0:T(8,128)(2,1)} custom-call(bf16[768,768]{1,0:T(8,128)(2,1)} %get-tuple-element.97.refs_0_, f32[1,768]{1,0:T(1,128)} %get-tuple-element.98.refs_1_, bf16[768,768]{1,0:T(8,128)(2,1)} %get-tuple-element.99.refs_2_, bf16[1024,1536]{1,0:T(8,128)(2,1)} %get-tuple-element.100.refs_3_, ...), custom_call_target="tpu_custom_call" | custom-call | tf_op jit(solution)/shard_map/pack/pallas_call | solution.py:1202
  355.9 107.3 %back_and_scatter.1 = (bf16[2,864,768]{2,1,0:T(8,128)(2,1)}, bf16[768,2304]{1,0:T(8,128)(2,1)}, f32[2,2,768]{2,1,0:T(2,128)}, bf16[3712,128]{1,0:T(8,128)(2,1)}) custom-call(bf16[2,864,2304]{2,1,0:T(8,128)(2,1)} %get-tuple-element.85.q_ref.k_ref.v_ref, bf16[2,864,2304]{2,1,0:T(8,128)(2,1)} %get-tuple-element.85.q_ref.k_ref.v_ref, ...), custom_call_target="tpu_custom_call" | custom-call | tf_op jit(solution)/shard_map/back_and_scatter/pallas_call | solution.py:2349
  463.3 0.7 convert.20
  464.8 4.8 pack.3.g_ref
  469.6 42.5 %scatter_chunks.1 = (bf16[3712,128]{1,0:T(8,128)(2,1)}, bf16[32,112,128]{2,1,0:T(8,128)(2,1)}) custom-call(bf16[32,448,128]{2,1,0:T(8,128)(2,1)} %pack.3.g_ref, bf16[112,128]{1,0:T(8,128)(2,1)} %pad.14.rows_ref), custom_call_target="tpu_custom_call" | custom-call | tf_op jit(solution)/shard_map/scatter_chunks/pallas_call | solution.py:2097
  512.1 6.1 %own_grad.1 = (f32[3712,128]{1,0:T(8,128)}, f32[8,128]{1,0:T(8,128)}) custom-call(f32[832,64]{1,0:T(8,128)} %maximum_maximum_fusion.cond_ref, bf16[3584,128]{1,0:T(8,128)(2,1)} %bitcast.23, bf16[3712,128]{1,0:T(8,128)(2,1)} %get-tuple-element.114.early_ref, bf16[3712,128]{1,0:T(8,128)(2,1)} %get-tuple-element.115.late_ref), custom_call_target="tpu_custom_call" | custom-call | tf_op jit(solution)/shard_map/own_grad/pallas_call | solution.py:2497
  518.2 12.6 %squares.1 = f32[32,8,128]{2,1,0:T(8,128)} custom-call(f32[8,128]{1,0:T(8,128)} %get-tuple-element.116.in_ref), custom_call_target="tpu_custom_call" | custom-call | tf_op jit(solution)/shard_map/squares/pallas_call | solution.py:2392
  530.8 1.5 reduce_sum.19
  533.1 6.2 %multiply_subtract_fusion = (f32[473472]{0:T(1024)}, f32[473472]{0:T(1024)}, f32[473472]{0:T(1024)}) fusion(f32[473472]{0:T(1024)S(1)} %copy-done.1, f32[]{:T(128)S(6)} %div.31, f32[3712,128]{1,0:T(8,128)} %get-tuple-element.117, f32[473472]{0:T(1024)} %param.14, f32[473472]{0:T(1024)} %param.15), kind=kLoop, calls=%fused_computation.5 | loop fusion | flops 7575552 | bytes 13257220 | tf_op jit(solution)/shard_map/sub | solution.py:2665
  539.3 1.5 copy.23
  (28 shorter events, 2.1 us)
Async XLA Ops:
  3.7 20.6 %copy-start = (f32[3888,128]{1,0:T(8,128)}, f32[3888,128]{1,0:T(8,128)S(1)}, u32[]{:S(2)}) copy-start(f32[3888,128]{1,0:T(8,128)S(1)} %pad.13.lin_ref) | copy-start | bytes 5971972
  318.3 23.4 %copy-start.4 = (f32[2,1,768]{2,1,0:T(1,128)S(1)}, f32[2,1,768]{2,1,0:T(1,128)}, u32[]{:S(2)}) copy-start(f32[2,1,768]{2,1,0:T(1,128)} %get-tuple-element.111) | copy-start | bytes 18436
  318.3 24.2 %copy-start.3 = (f32[2,3,768]{2,1,0:T(4,128)S(1)}, f32[2,3,768]{2,1,0:T(4,128)}, u32[]{:S(2)}) copy-start(f32[2,3,768]{2,1,0:T(4,128)} %get-tuple-element.112) | copy-start | bytes 55300
  512.1 21.0 %copy-start.1 = (f32[473472]{0:T(1024)S(1)}, f32[473472]{0:T(1024)}, u32[]{:S(2)}) copy-start(f32[473472]{0:T(1024)} %param.13) | copy-start | bytes 5681668
  533.1 6.2 %copy-start.2 = (bf16[2,864,768]{2,1,0:T(8,128)(2,1)S(1)}, bf16[2,864,768]{2,1,0:T(8,128)(2,1)}, u32[]{:S(2)}) copy-start(bf16[2,864,768]{2,1,0:T(8,128)(2,1)} %get-tuple-element.130) | copy-start | bytes 7962628
